TPU v7x, 32 devices: a whole 2x2x4 slice. The times are simulated.
32 devices in a mesh: hi: 8 (over y, x, core), lo: 4 (over z).
Axes of the slice: x: 2, y: 2, z: 4, core: 2. Of those that a mesh axis runs over, the one named last changes fastest.
Arguments:
- previous: float32 [32, 524288], P(None, ('hi', 'lo')), may hold values from -6 to 6
- current: float32 [32, 524288], P(None, ('hi', 'lo')), may hold values from -6 to 6
- field_levels: int32 [19], replicated, may hold values from -4 to 4
- bond_levels: int32 [18], replicated, may hold values from 1 to 3
Outputs:
- ortho_block: float32 [32, 524288], P(None, ('hi', 'lo'))
- upper_factor: float32 [32, 32], replicated
All inputs are finite; a program needn't handle non-finite values.
Results may differ from a plain program's by a relative error of at most 0.00005.
Values sent between devices are 32-bit elements; how exact they have to be, the bound alone decides.
No kernel may reach another device: no remote copies, remote signals or barrier semaphores. Data moves between devices by JAX's collectives and lax.ppermute only.
A program may use at most 64 MiB of HBM per device.

v0:
```python
import jax
import jax.numpy as jnp
from jax import lax
from jax.sharding import PartitionSpec as P

FIELD_STEP = 0.75
COUPLING_STEP = 0.5


def chain_matrix(couplings, bit_count, bond_list):
    width = 2**bit_count
    rows = lax.iota(jnp.int32, width)[:, None]
    cols = lax.iota(jnp.int32, width)[None, :]
    matrix = jnp.zeros((width, width), jnp.float32)
    for site_number, spot in bond_list:
        differ = cols >> spot & 1 != cols >> spot + 1 & 1
        target = rows == cols ^ 3 << spot
        matrix = matrix + jnp.where(differ & target, 0.5 * couplings[site_number], 0.0)
    return matrix


def cross_flip(values, coupling, low_spot):
    width = values.shape[-1]
    index = lax.iota(jnp.int32, width)
    permute = (index[:, None] == index[None, :] ^ 1 << low_spot).astype(jnp.float32)
    moved = jnp.einsum("vatbl,lj->vatbj", values, permute, precision=lax.Precision.HIGHEST)
    flipped = jnp.flip(moved, axis=2)
    upper = lax.iota(jnp.int32, 2)[:, None]
    keep = (index[None, :] >> low_spot & 1 != upper).astype(jnp.float32)
    return 0.5 * coupling * flipped * keep[None, None, :, None, :]


def local(previous, current, field_levels, bond_levels):
    vectors, amp_count = current.shape
    site_count = field_levels.shape[0]
    devices = lax.axis_size("hi") * lax.axis_size("lo")
    local_bits = amp_count.bit_length() - 1
    global_bits = devices.bit_length() - 1
    rest_bits = local_bits - global_bits
    device = lax.axis_index("hi") * lax.axis_size("lo") + lax.axis_index("lo")
    local_index = lax.iota(jnp.int32, amp_count)
    top_width = 2**global_bits
    low_width = 2**rest_bits

    def position(site_number):
        if site_number < global_bits:
            return rest_bits + site_number
        return site_number - global_bits

    def spin_value(site_number):
        if site_number < local_bits:
            return 0.5 - (local_index >> position(site_number) & 1).astype(jnp.float32)
        return 0.5 - (device >> site_number - local_bits & 1).astype(jnp.float32)

    fields = FIELD_STEP * field_levels.astype(jnp.float32)
    couplings = COUPLING_STEP * bond_levels.astype(jnp.float32)
    diagonal = jnp.zeros((amp_count,), jnp.float32)
    for site_number in range(site_count):
        diagonal = diagonal + fields[site_number] * spin_value(site_number)
        if site_number < site_count - 1:
            diagonal = diagonal + couplings[site_number] * spin_value(site_number) * spin_value(
                site_number + 1
            )
    top_matrix = chain_matrix(
        couplings,
        global_bits,
        [(site_number, site_number) for site_number in range(global_bits - 1)],
    )
    low_matrix = chain_matrix(
        couplings,
        rest_bits,
        [
            (site_number, site_number - global_bits)
            for site_number in range(global_bits, local_bits - 1)
        ],
    )
    blocks = current.reshape(vectors, top_width, low_width)
    applied = diagonal[None, :] * current
    applied = applied + jnp.einsum(
        "vtl,tu->vul", blocks, top_matrix, precision=lax.Precision.HIGHEST
    ).reshape(vectors, amp_count)
    applied = applied + jnp.einsum(
        "vtl,lu->vtu", blocks, low_matrix, precision=lax.Precision.HIGHEST
    ).reshape(vectors, amp_count)
    joined = cross_flip(
        current.reshape(vectors, 1, 2, top_width // 2, low_width), couplings[global_bits - 1], 0
    )
    applied = applied + joined.reshape(vectors, amp_count)
    far_matrix = chain_matrix(
        couplings,
        global_bits,
        [
            (site_number, site_number - local_bits)
            for site_number in range(local_bits, site_count - 1)
        ],
    )
    shaped = current.reshape(vectors, devices, amp_count // devices)
    arrived = lax.all_to_all(shaped, ("hi", "lo"), split_axis=1, concat_axis=1, tiled=True)
    count = arrived.shape[0]
    bond_terms = jnp.einsum(
        "vtl,tu->vul", arrived, far_matrix, precision=lax.Precision.HIGHEST
    ).reshape(count, amp_count)
    seam = cross_flip(
        arrived.reshape(count, top_width // 2, 2, 1, low_width),
        couplings[local_bits - 1],
        rest_bits - 1,
    )
    bond_terms = bond_terms + seam.reshape(count, amp_count)
    remote_part = lax.all_to_all(
        bond_terms.reshape(arrived.shape), ("hi", "lo"), split_axis=1, concat_axis=1, tiled=True
    ).reshape(vectors, amp_count)
    filtered = 4.0 / site_count * (applied + remote_part) - previous
    local_gram = jnp.dot(filtered, filtered.T, precision=lax.Precision.HIGHEST) / (
        amp_count * devices
    )
    gram_matrix = lax.psum(local_gram, ("hi", "lo"))
    lower_factor = jnp.linalg.cholesky(gram_matrix)
    inverse = jax.scipy.linalg.solve_triangular(
        lower_factor, jnp.eye(vectors, dtype=jnp.float32), lower=True
    )
    ortho_block = jnp.dot(inverse, filtered, precision=lax.Precision.HIGHEST)
    return (ortho_block, lower_factor.T)


def solution(mesh):
    in_specs = (P(None, ("hi", "lo")), P(None, ("hi", "lo")), P(), P())
    out_specs = (P(None, ("hi", "lo")), P())
    return jax.shard_map(local, mesh=mesh, in_specs=in_specs, out_specs=out_specs, check_vma=False)
```

profile of v0, /device:TPU:0, one launch (start us, length us, event | category | flops | bytes accessed | tf_op | source)
XLA Modules:
  0.0 185.2 jit_solution(9063930395883796828)
XLA Ops:
  0.6 3.2 %copy.74 = f32[4,32,8,512]{3,2,0,1:T(8,128)} copy(f32[4,32,8,512]{3,2,1,0:T(8,128)} %bitcast.103) | data formatting | bytes 4194304 | tf_op jit(solution)/shard_map/reshape | solution.py:77
  3.8 7.3 %all-to-all-start = ((f32[32,32,512]{2,0,1:T(8,128)}), f32[32,32,512]{2,0,1:T(8,128)S(1)}, u32[]{:S(2)}, u32[]{:S(2)}) async-start(f32[32,32,512]{2,0,1:T(8,128)} %bitcast.115), calls=%async_computation | async-start | bytes 4194304 | tf_op jit(solution)/shard_map/all_to_all | solution.py:98
  11.1 0.7 fusion.151
  15.0 43.6 %all-to-all-done = f32[32,32,512]{2,0,1:T(8,128)S(1)} async-done(((f32[32,32,512]{2,0,1:T(8,128)}), f32[32,32,512]{2,0,1:T(8,128)S(1)}, u32[]{:S(2)}, u32[]{:S(2)}) %all-to-all-start) | async-done | bytes 2097184 | tf_op jit(solution)/shard_map/all_to_all | solution.py:98
  58.6 1.9 %convolution_bitcast_fusion = f32[32,16,2,512]{3,0,2,1:T(8,128)S(1)} fusion(f32[32,16,2,512]{3,0,2,1:T(8,128)S(1)} %bitcast.109, s32[512]{0:T(512)S(1)} %iota_xor_fusion), kind=kOutput, calls=%fused_computation.10 | convolution fusion | flops 3221487616 | bytes 4196352 | tf_op jit(solution)/shard_map/vatbl,lj->vatbj/dot_general | solution.py:26
  60.5 0.4 multiply_multiply_fusion
  60.9 4.1 %copy_add_fusion = f32[32,32,512]{2,1,0:T(8,128)S(1)} fusion(f32[32,32,512]{2,0,1:T(8,128)S(1)} %bitcast.105, f32[32,32,512]{2,0,1:T(8,128)S(1)} %all-to-all-done, f32[]{:T(128)S(6)} %mul.638, f32[]{:T(128)S(6)} %mul.637, f32[]{:T(128)S(6)} %mul.636, f32[]{:T(128)S(6)} %mul.635, s32[32]{0:T(128)S(1)} %get-tuple-element.51, s32[32]{0:T(128)S(1)} %get-tuple-element.52, ...), kind=kOutput, calls=%fused_computation.1 | convolution fusion | flops 201866240 | bytes 6292112 | tf_op jit(solution)/shard_map/vtl,tu->vul/dot_general | solution.py:100
  65.0 2.5 %copy.43 = f32[32,32,512]{2,0,1:T(8,128)} copy(f32[32,32,512]{2,1,0:T(8,128)S(1)} %copy_add_fusion) | data formatting | bytes 4194304 | tf_op jit(solution)/shard_map/add | solution.py:108
  67.5 4.5 %all-to-all-start.1 = ((f32[32,32,512]{2,0,1:T(8,128)}), f32[32,32,512]{2,0,1:T(8,128)}, u32[]{:S(2)}, u32[]{:S(2)}) async-start(f32[32,32,512]{2,0,1:T(8,128)} %copy.43), calls=%async_computation.1 | async-start | bytes 4194304 | tf_op jit(solution)/shard_map/all_to_all | solution.py:109
  72.0 2.6 %copy.58 = f32[4,8,32,512]{3,2,1,0:T(8,128)} copy(f32[4,8,32,512]{3,1,2,0:T(8,128)S(1)} %bitcast.104) | data formatting | bytes 4194304
  75.2 4.5 %fusion.6 = f32[32,2,16,512]{3,0,2,1:T(8,128)S(1)} fusion(f32[32,2,16,512]{3,2,1,0:T(8,128)} %bitcast.112, s32[512]{0:T(512)S(1)} %iota_xor_fusion.1), kind=kOutput, calls=%fused_computation.9 | convolution fusion | flops 3221487616 | bytes 4196352 | tf_op jit(solution)/shard_map/vatbl,lj->vatbj/dot_general | solution.py:26
  79.7 0.4 multiply_multiply_fusion.1
  80.1 1.5 copy.62
  86.6 5.4 %fusion.9 = f32[512,32,32]{0,2,1:T(8,128)S(1)} fusion(f32[32,32,512]{2,1,0:T(8,128)S(1)} %bitcast.113, f32[]{:T(128)S(6)} %mul.629, s32[512]{0:T(512)S(1)} %get-tuple-element.59, f32[]{:T(128)S(6)} %mul.628, s32[512]{0:T(512)S(1)} %get-tuple-element.60, f32[]{:T(128)S(6)} %mul.627, s32[512]{0:T(512)S(1)} %get-tuple-element.63, f32[]{:T(128)S(6)} %mul.626, ...), kind=kOutput, calls=%fused_computation.12 | convolution fusion | flops 3229351936 | bytes 4214816 | tf_op jit(solution)/shard_map/vtl,lu->vtu/dot_general | solution.py:82
  92.0 2.6 %copy.60 = f32[4,8,32,512]{3,1,2,0:T(8,128)} copy(f32[4,8,32,512]{3,2,1,0:T(8,128)S(1)} %bitcast.117) | data formatting | bytes 4194304
  97.2 2.2 %fusion.77 = f32[32,32,512]{2,0,1:T(8,128)S(1)} fusion(f32[32,32,512]{2,1,0:T(8,128)S(1)} %bitcast.114, f32[]{:T(128)S(6)} %mul.621, s32[32]{0:T(128)S(1)} %get-tuple-element.51, f32[]{:T(128)S(6)} %mul.620, s32[32]{0:T(128)S(1)} %get-tuple-element.52, f32[]{:T(128)S(6)} %mul.619, s32[32]{0:T(128)S(1)} %get-tuple-element.53, f32[]{:T(128)S(6)} %mul.618, ...), kind=kOutput, calls=%fused_computation.82 | convolution fusion | flops 201341952 | bytes 4194960 | tf_op jit(solution)/shard_map/vtl,tu->vul/dot_general | solution.py:79
  99.4 2.6 %copy.59 = f32[4,8,32,512]{3,1,2,0:T(8,128)} copy(f32[4,8,32,512]{3,2,1,0:T(8,128)S(1)} %bitcast.116) | data formatting | bytes 4194304
  102.6 0.7 fusion.150
  108.3 17.4 %add_add_fusion = f32[16384]{0:T(1024)S(1)} fusion(f32[]{:T(128)S(6)} %mul.615, f32[]{:T(128)S(6)} %mul.614, f32[]{:T(128)S(6)} %mul.612, f32[]{:T(128)S(6)} %mul.611, f32[]{:T(128)S(6)} %mul.609, f32[]{:T(128)S(6)} %mul.608, f32[]{:T(128)S(6)} %mul.606, f32[]{:T(128)S(6)} %mul.605, f32[]{:T(128)S(6)} %mul.603, f32[]{:T(128)S(6)} %sub.220, f32[]{:T(128)} %bitcast.27, ...), kind=kLoop, calls=%fused_computation.76 | loop fusion | flops 2195456 | bytes 65688 | tf_op jit(solution)/shard_map/add | solution.py:59
  125.7 2.0 %copy.57 = f32[32,4,8,512]{3,2,0,1:T(8,128)S(1)} copy(f32[32,4,8,512]{3,2,1,0:T(8,128)} %bitcast.59) | data formatting | bytes 4194304 | tf_op jit(solution)/shard_map/reshape | solution.py:111
  127.7 0.2 copy-done.1
  127.9 0.6 copy-done.2
  128.5 3.5 %multiply_subtract_fusion = f32[32,16384]{1,0:T(8,128)S(1)} fusion(f32[32,16384]{1,0:T(8,128)} %param.4, f32[32,16384]{1,0:T(8,128)S(1)} %bitcast.110, f32[32,16384]{1,0:T(8,128)S(1)} %bitcast.106, f32[32,16384]{1,0:T(8,128)} %bitcast.107, f32[32,16384]{1,0:T(8,128)} %bitcast.108, f32[32,16384]{1,0:T(8,128)S(1)} %copy-done.1, f32[16384]{0:T(1024)S(1)} %add_add_fusion), kind=kLoop, calls=%fused_computation.6 | loop fusion | flops 3670016 | bytes 14745600 | tf_op jit(solution)/shard_map/sub | solution.py:112
  132.0 1.8 convolution_multiply_fusion
  133.8 40.5 %psum.7 = f32[32,32]{0,1:T(8,128)S(1)} all-reduce(f32[32,32]{0,1:T(8,128)S(1)} %convolution_multiply_fusion), channel_id=1, replica_groups=mesh['hi'=8,'lo'=4] {'hi','lo'}, use_global_device_ids=true, to_apply=%region_0.1 | all-reduce | flops 1024 | bytes 8192 | tf_op jit(solution)/shard_map/psum | solution.py:116
  174.4 2.9 %cholesky.16 = f32[32,32]{1,0:T(8,128)S(1)} custom-call(f32[32,32]{1,0:T(8,128)S(1)} %fusion.75), custom_call_target="Cholesky" | custom-call | tf_op jit(solution)/shard_map/jit(cholesky)/cholesky | solution.py:117
  177.3 0.6 compare_reduce_fusion
  178.0 0.7 fusion.105
  178.6 2.4 %custom-call.7 = f32[1,32,32]{1,2,0:T(8,128)S(1)} custom-call(f32[1,32,32]{2,1,0:T(8,128)S(1)} %get-tuple-element.11), custom_call_target="InvertDiagBlocksLowerTriangular" | custom-call | tf_op jit(solution)/shard_map/jit(_solve_triangular)/triangular_solve | solution.py:118
  181.1 0.2 fusion.73
  181.3 3.2 %fusion.152 = f32[32,16384]{1,0:T(8,128)} fusion(f32[32,32]{1,0:T(8,128)S(1)} %fusion.73, f32[32,16384]{1,0:T(8,128)S(1)} %multiply_subtract_fusion), kind=kOutput, calls=%fused_computation.191 | convolution fusion | flops 201326592 | bytes 4198400 | tf_op jit(solution)/shard_map/dot_general | solution.py:121
  184.5 0.7 copy.47
  (34 shorter events, 0.2 us)
Async XLA Ops:
  3.8 7.3 %copy-start.4 = (s32[18]{0:T(128)S(1)}, s32[18]{0:T(128)}, u32[]{:S(2)}) copy-start(s32[18]{0:T(128)} %param.7) | copy-start | bytes 220
  3.8 54.8 %all-to-all-start = ((f32[32,32,512]{2,0,1:T(8,128)}), f32[32,32,512]{2,0,1:T(8,128)S(1)}, u32[]{:S(2)}, u32[]{:S(2)}) async-start(f32[32,32,512]{2,0,1:T(8,128)} %bitcast.115), calls=%async_computation | async-start | bytes 4194304 | tf_op jit(solution)/shard_map/all_to_all | solution.py:98
  67.5 4.5 %copy-start = (f32[32,16384]{1,0:T(8,128)S(1)}, f32[32,16384]{1,0:T(8,128)}, u32[]{:S(2)}) copy-start(f32[32,16384]{1,0:T(8,128)} %param.5) | copy-start | bytes 6291460
  67.5 58.2 %all-to-all-start.1 = ((f32[32,32,512]{2,0,1:T(8,128)}), f32[32,32,512]{2,0,1:T(8,128)}, u32[]{:S(2)}, u32[]{:S(2)}) async-start(f32[32,32,512]{2,0,1:T(8,128)} %copy.43), calls=%async_computation.1 | async-start | bytes 4194304 | tf_op jit(solution)/shard_map/all_to_all | solution.py:109
  80.1 6.5 %copy-start.3 = (f32[4,8,32,512]{3,2,1,0:T(8,128)S(1)}, f32[4,8,32,512]{3,2,1,0:T(8,128)}, u32[]{:S(2)}) copy-start(f32[4,8,32,512]{3,2,1,0:T(8,128)} %copy.58) | copy-start | bytes 6291460
  99.4 3.2 %copy-start.5 = (s32[19]{0:T(128)S(1)}, s32[19]{0:T(128)}, u32[]{:S(2)}) copy-start(s32[19]{0:T(128)} %param.6) | copy-start | bytes 232
  125.7 2.2 %copy-start.1 = (f32[32,16384]{1,0:T(8,128)S(1)}, f32[32,16384]{1,0:T(8,128)}, u32[]{:S(2)}) copy-start(f32[32,16384]{1,0:T(8,128)} %param.5) | copy-start | bytes 6291460
  125.7 2.8 %copy-start.2 = (f32[4,8,32,512]{3,1,2,0:T(8,128)S(1)}, f32[4,8,32,512]{3,1,2,0:T(8,128)}, u32[]{:S(2)}) copy-start(f32[4,8,32,512]{3,1,2,0:T(8,128)} %copy.62) | copy-start | bytes 6291460
where the time goes:
time: 186 us; the launch traced here: 185 us
  waiting for transfers between devices  43.6 us (23%)
  blocking collectives  40.5 us (22%)
  other arithmetic  28.4 us (15%)
  matrix products  23.2 us (12%)
  local copies, waits for them, and re-layouts  20 us (11%)
  between operations  17.7 us (10%)
  starting transfers between devices  11.7 us (6%)
    all_to_all x1, waiting for transfers between devices, local(): lax.all_to_all(shaped, ('hi', 'lo'), split_axis=1, concat_axis=1, tiled=T...  43.6 us
    psum x1, blocking collectives, local(): gram_matrix = lax.psum(local_gram, ('hi', 'lo'))  40.5 us
    add x1, other arithmetic, local(): diagonal = diagonal + fields[site_number] * spin_value(site_number)  17.4 us
    unnamed x17, local copies, waits for them, and re-layouts  10.8 us
    all_to_all x1, starting transfers between devices, local(): lax.all_to_all(shaped, ('hi', 'lo'), split_axis=1, concat_axis=1, tiled=T...  7.3 us
    dot_general x2, matrix products, cross_flip(): jnp.einsum('vatbl,lj->vatbj', values, permute, precision=lax.Precision.HI...  6.38 us
    dot_general x1, matrix products, local(): jnp.einsum('vtl,lu->vtu', blocks, low_matrix, precision=lax.Precision.HIG...  5.41 us
    all_to_all x1, starting transfers between devices, local(): lax.all_to_all(bond_terms.reshape(arrived.shape), ('hi', 'lo'), split_axi...  4.45 us
  transfers between devices with their start and end apart: 2, of which 1 were waited for; matrix products, arithmetic and copies ran while one was open for 22% of the time, Pallas kernels for 0%

commit v1 on v0

v1 whole, which is shorter than its diff:
```python
import functools

import jax
import jax.numpy as jnp
from jax import lax
from jax.experimental import pallas as pl
from jax.experimental.pallas import tpu as pltpu
from jax.sharding import PartitionSpec as P

FIELD_STEP = 0.75
COUPLING_STEP = 0.5
AXES = ("hi", "lo")
LANES = 128
LANE_BITS = 7
GROUP = 256
GROUP_BITS = 8
VMEM_LIMIT = 48 * 1024 * 1024


def pieces(values, count):
    parts = []
    for _ in range(count):
        part = values.astype(jnp.bfloat16)
        parts.append(part)
        values = values - part.astype(jnp.float32)
    return parts


def smem():
    return pl.BlockSpec(memory_space=pltpu.SMEM)


def params():
    return pltpu.CompilerParams(vmem_limit_bytes=VMEM_LIMIT)


def triple_pairs(devices, p, m, q, sum_low):
    def routes(moves):
        table = {}
        for source, target in moves:
            for one, two in ((source, target), (tuple(1 - b for b in source), tuple(1 - b for b in target))):
                table[one] = two
        pairs = []
        for device in range(devices):
            state = (device >> p & 1, device >> m & 1, device >> q & 1)
            if state in table:
                goal = table[state]
                other = device & ~(1 << p | 1 << m | 1 << q)
                pairs.append((device, other | goal[0] << p | goal[1] << m | goal[2] << q))
        return pairs

    site = (0, 1, 0) if sum_low else (1, 1, 1)
    first = routes([((0, 1, 0), (1, 0, 0)), ((1, 1, 0), site)])
    second = routes([(site, (1, 0, 1)), ((1, 0, 0), (0, 0, 1))])
    return first, second, site


def half_kernel(select_ref, x_ref, out_ref, *, span):
    upper = select_ref[0] == 1
    for k in range(out_ref.shape[1] // span):
        lower_part = x_ref[:, 2 * k * span : (2 * k + 1) * span]
        upper_part = x_ref[:, (2 * k + 1) * span : (2 * k + 2) * span]
        out_ref[:, k * span : (k + 1) * span] = jnp.where(upper, upper_part, lower_part)


def take_half(current, select, span):
    vectors, amp_count = current.shape
    steps = 4 if amp_count // (2 * span) % 4 == 0 else 1
    return pl.pallas_call(
        functools.partial(half_kernel, span=span),
        grid=(steps,),
        out_shape=jax.ShapeDtypeStruct((vectors, amp_count // 2), jnp.float32),
        in_specs=[smem(), pl.BlockSpec((vectors, amp_count // steps), lambda i: (0, i))],
        out_specs=pl.BlockSpec((vectors, amp_count // 2 // steps), lambda i: (0, i)),
        compiler_params=params(),
        name="take_half",
    )(select, current)


def local_kernel(weight_ref, x_ref, prev_ref, diag_ref, matrix_ref, out_ref, *, tile_bonds, wraps):
    vectors, amp_count = x_ref.shape
    groups = amp_count // GROUP
    stacked = jnp.concatenate([x_ref[:, k * GROUP : (k + 1) * GROUP] for k in range(groups)], axis=0)
    matrix = matrix_ref[...]
    product = None
    for part in pieces(stacked, 3):
        term = jnp.dot(part, matrix, preferred_element_type=jnp.float32)
        product = term if product is None else product + term
    scale = weight_ref[len(tile_bonds) + len(wraps)]
    lane = lax.broadcasted_iota(jnp.int32, (vectors, LANES), 1)

    def tile(t):
        return x_ref[:, t * LANES : (t + 1) * LANES]

    for t in range(amp_count // LANES):
        row = t // 2 * vectors
        side = (t & 1) * LANES
        total = diag_ref[:, t * LANES : (t + 1) * LANES] * tile(t) - prev_ref[:, t * LANES : (t + 1) * LANES]
        total = total + scale * product[row : row + vectors, side : side + LANES]
        for number, (one, two) in enumerate(tile_bonds):
            if (t >> one & 1) != (t >> two & 1):
                total = total + weight_ref[number] * tile(t ^ (1 << one) ^ (1 << two))
        for number, (high, low) in enumerate(wraps):
            up = t >> high & 1
            shift = 1 << low if up == 0 else LANES - (1 << low)
            moved = pltpu.roll(tile(t ^ (1 << high)), shift, 1)
            total = total + jnp.where((lane >> low & 1) != up, weight_ref[len(tile_bonds) + number] * moved, 0.0)
        out_ref[:, t * LANES : (t + 1) * LANES] = total


def gather_kernel(weight_ref, local_ref, one_ref, two_ref, half_ref, out_ref, *, span):
    first, second = weight_ref[0], weight_ref[1]
    lower, upper = weight_ref[2], weight_ref[3]
    for k in range(half_ref.shape[1] // span):
        part = half_ref[:, k * span : (k + 1) * span]
        for side, weight in ((0, lower), (1, upper)):
            cols = slice((2 * k + side) * span, (2 * k + side + 1) * span)
            out_ref[:, cols] = local_ref[:, cols] + first * one_ref[:, cols] + second * two_ref[:, cols] + weight * part


def filter_kernel(weight_ref, acc_ref, one_ref, two_ref, half_ref, out_ref, gram_ref, total_ref, *, span, scale):
    lower, upper = weight_ref[2], weight_ref[3]
    step = pl.program_id(0)
    vectors = acc_ref.shape[0]

    @pl.when(step == 0)
    def _():
        total_ref[...] = jnp.zeros_like(total_ref)

    for k in range(half_ref.shape[1] // span):
        part = half_ref[:, k * span : (k + 1) * span]
        for side, weight in ((0, lower), (1, upper)):
            cols = slice((2 * k + side) * span, (2 * k + side + 1) * span)
            out_ref[:, cols] = acc_ref[:, cols] + one_ref[:, cols] + two_ref[:, cols] + weight * part
    stacked = jnp.concatenate(pieces(out_ref[...], 3), axis=0)
    total_ref[...] += lax.dot_general(
        stacked, stacked, (((1,), (1,)), ((), ())), preferred_element_type=jnp.float32
    )

    @pl.when(step == pl.num_programs(0) - 1)
    def _():
        table = total_ref[...]

        def block(a, b):
            return table[a * vectors : (a + 1) * vectors, b * vectors : (b + 1) * vectors]

        gram = block(0, 0) + (block(0, 1) + block(1, 0)) + (block(1, 1) + (block(0, 2) + block(2, 0)))
        gram_ref[...] = gram * scale


def finish_kernel(gram_ref, filtered_ref, out_ref, upper_ref, inverse_ref):
    vectors = gram_ref.shape[0]

    @pl.when(pl.program_id(0) == 0)
    def _():
        rows = lax.broadcasted_iota(jnp.int32, (vectors, vectors), 0)
        cols = lax.broadcasted_iota(jnp.int32, (vectors, vectors), 1)
        rest = gram_ref[...]
        inverse = (rows == cols).astype(jnp.float32)
        factor = jnp.zeros_like(rest)
        for k in range(vectors):
            root = lax.rsqrt(rest[k : k + 1, k : k + 1])
            top = rest[k : k + 1, :] * root
            column = rest[:, k : k + 1] * root
            below = jnp.where(rows[:, :1] > k, column, 0.0)
            inverse_row = inverse[k : k + 1, :] * root
            factor = jnp.where(rows == k, jnp.where(cols >= k, top, 0.0), factor)
            inverse = jnp.where(rows == k, inverse_row, inverse - below * inverse_row)
            rest = rest - below * top
        upper_ref[...] = factor
        inverse_ref[...] = inverse

    left = pieces(inverse_ref[...], 3)
    right = pieces(filtered_ref[...], 3)
    order = ((0, 0), (0, 1), (1, 0), (1, 1), (0, 2), (2, 0))
    out_ref[...] = jnp.dot(
        jnp.concatenate([left[a] for a, _ in order], axis=1),
        jnp.concatenate([right[b] for _, b in order], axis=0),
        preferred_element_type=jnp.float32,
    )


def local(previous, current, field_levels, bond_levels, lo_bits):
    vectors, amp_count = current.shape
    site_count = field_levels.shape[0]
    devices = lax.axis_size("hi") * lax.axis_size("lo")
    local_bits = amp_count.bit_length() - 1
    global_bits = devices.bit_length() - 1
    rest_bits = local_bits - global_bits
    device = lax.axis_index("hi") * lax.axis_size("lo") + lax.axis_index("lo")
    local_index = lax.iota(jnp.int32, amp_count)
    scale = 4.0 / site_count

    def position(site_number):
        if site_number < global_bits:
            return rest_bits + site_number
        return site_number - global_bits

    def device_bit(k):
        return device >> k & 1

    def spin_value(site_number):
        if site_number < local_bits:
            return 0.5 - (local_index >> position(site_number) & 1).astype(jnp.float32)
        return 0.5 - device_bit(site_number - local_bits).astype(jnp.float32)

    def permute(values, pairs):
        return lax.ppermute(values, AXES, pairs)

    def flips(mask, keep=lambda i: True):
        return [(i, i ^ mask) for i in range(devices) if keep(i)]

    fields = FIELD_STEP * field_levels.astype(jnp.float32)
    couplings = COUPLING_STEP * bond_levels.astype(jnp.float32)
    strength = scale * (0.5 * couplings)

    triples = []
    swaps = {}
    for m in range(1, global_bits - 1, 2):
        sum_low = m == 1
        first, second, site = triple_pairs(devices, m - 1, m, m + 1, sum_low)
        triples.append((m, first, second, site, m + 1 if sum_low else m - 1))
    firsts = [permute(current, first) for _, first, _, _, _ in triples]
    for _, _, _, _, bit in triples:
        if bit not in swaps:
            swaps[bit] = permute(current, flips(1 << bit))
    extra = []
    if global_bits % 2 == 0:
        top = global_bits - 1
        moved = permute(current, [(i, i ^ (3 << top - 1)) for i in range(devices) if (i >> top & 1) != (i >> top - 1 & 1)])
        extra.append(strength[site_count - 2] * moved)

    span = 2 ** (rest_bits - 1)
    tiled = span >= LANES
    side = 1 - device_bit(0)
    if tiled:
        half = take_half(current, side.reshape(1), span)
    else:
        half = lax.dynamic_index_in_dim(current.reshape(vectors, -1, 2, span), side, 2, False).reshape(vectors, -1)
    middle = (1, 2) if global_bits > 1 else (0, 1)
    mask = 3 if global_bits > 1 else 1
    half_early = permute(half, flips(1, lambda i: (i & mask) in middle))

    diagonal = jnp.zeros((amp_count,), jnp.float32)
    for site_number in range(site_count):
        diagonal = diagonal + fields[site_number] * spin_value(site_number)
        if site_number < site_count - 1:
            diagonal = diagonal + couplings[site_number] * spin_value(site_number) * spin_value(site_number + 1)
    rows = lax.iota(jnp.int32, GROUP)[:, None]
    cols = lax.iota(jnp.int32, GROUP)[None, :]
    matrix = jnp.zeros((GROUP, GROUP), jnp.float32)
    tile_bonds, tile_weights, wraps, wrap_weights = [], [], [], []
    for site_number in range(local_bits - 1):
        one, two = position(site_number), position(site_number + 1)
        low, high = min(one, two), max(one, two)
        if high < GROUP_BITS:
            differ = (cols >> low & 1) != (cols >> high & 1)
            target = rows == cols ^ (1 << low | 1 << high)
            matrix = matrix + jnp.where(differ & target, 0.5 * couplings[site_number], 0.0)
        elif low >= LANE_BITS:
            tile_bonds.append((low - LANE_BITS, high - LANE_BITS))
            tile_weights.append(strength[site_number])
        else:
            wraps.append((high - LANE_BITS, low))
            wrap_weights.append(strength[site_number])
    weights = jnp.stack(tile_weights + wrap_weights + [jnp.float32(scale)])
    here = pl.pallas_call(
        functools.partial(local_kernel, tile_bonds=tuple(tile_bonds), wraps=tuple(wraps)),
        out_shape=jax.ShapeDtypeStruct((vectors, amp_count), jnp.float32),
        in_specs=[smem()] + [pl.BlockSpec(memory_space=pltpu.VMEM)] * 4,
        out_specs=pl.BlockSpec(memory_space=pltpu.VMEM),
        compiler_params=params(),
        name="local_bonds",
    )(weights, current, previous, (scale * diagonal)[None, :], matrix.astype(jnp.bfloat16))

    seconds = []
    own = []
    for (m, _, second, site, bit), arrived in zip(triples, firsts):
        low_strength = strength[local_bits + m - 1]
        high_strength = strength[local_bits + m]
        at_site = functools.reduce(
            jnp.logical_and, [device_bit(m - 1 + j) == (site[j] ^ device_bit(m) ^ site[1]) for j in range(3)]
        )
        sent = jnp.where(at_site, low_strength, 0.0) * swaps[bit] + high_strength * arrived
        seconds.append(permute(sent, second))
        uses = (device_bit(m - 1) != device_bit(m)) & (device_bit(m + 1) == device_bit(m))
        own.append(jnp.where(uses, low_strength, 0.0))
    late = half
    if firsts:
        late, _ = lax.optimization_barrier((half, firsts[0]))
    half_late = permute(late, flips(1, lambda i: (i & mask) not in middle))
    half_strength = strength[local_bits - 1]
    half_weights = [jnp.where(side == 0, half_strength, 0.0), jnp.where(side == 1, half_strength, 0.0)]

    while len(own) < 2:
        own.append(jnp.float32(0.0))
        firsts.append(current)
        seconds.append(jnp.zeros_like(current))
    for arrived, weight, more in zip(firsts[2:], own[2:], seconds[2:]):
        extra.append(weight * arrived + more)
    if not tiled:
        both = half_strength * (half_early + half_late)
        placed = jnp.where(lax.iota(jnp.int32, 2)[None, None, :, None] == side, both.reshape(vectors, -1, 1, span), 0.0)
        extra.append(placed.reshape(vectors, amp_count))
        half_early = half_late = jnp.zeros_like(half)
        span = LANES
    for term in extra:
        here = here + term
    steps = 4
    block = pl.BlockSpec((vectors, amp_count // steps), lambda i: (0, i))
    half_block = pl.BlockSpec((vectors, amp_count // 2 // steps), lambda i: (0, i))
    weights = jnp.stack(own[:2] + half_weights)
    acc = pl.pallas_call(
        functools.partial(gather_kernel, span=span),
        grid=(steps,),
        out_shape=jax.ShapeDtypeStruct((vectors, amp_count), jnp.float32),
        in_specs=[smem(), block, block, block, half_block],
        out_specs=block,
        compiler_params=params(),
        name="gather_first",
    )(weights, here, firsts[0], firsts[1], half_early)
    filtered, gram = pl.pallas_call(
        functools.partial(filter_kernel, span=span, scale=1.0 / (amp_count * devices)),
        grid=(steps,),
        out_shape=(
            jax.ShapeDtypeStruct((vectors, amp_count), jnp.float32),
            jax.ShapeDtypeStruct((vectors, vectors), jnp.float32),
        ),
        in_specs=[smem(), block, block, block, half_block],
        out_specs=(block, pl.BlockSpec((vectors, vectors), lambda i: (0, 0))),
        scratch_shapes=[pltpu.VMEM((3 * vectors, 3 * vectors), jnp.float32)],
        compiler_params=params(),
        name="filter_gram",
    )(weights, acc, seconds[0], seconds[1], half_late)

    hub = lo_bits
    gram = gram + permute(gram, flips(1 << hub, lambda i: not i >> hub & 1))
    for k in range(global_bits):
        if k != hub:
            gram = gram + permute(gram, flips(1 << k, lambda i: i >> hub & 1))
    gram = jnp.where(device_bit(hub) == 1, gram, permute(gram, flips(1 << hub, lambda i: i >> hub & 1)))

    return pl.pallas_call(
        finish_kernel,
        grid=(steps,),
        out_shape=(
            jax.ShapeDtypeStruct((vectors, amp_count), jnp.float32),
            jax.ShapeDtypeStruct((vectors, vectors), jnp.float32),
        ),
        in_specs=[pl.BlockSpec((vectors, vectors), lambda i: (0, 0)), block],
        out_specs=(block, pl.BlockSpec((vectors, vectors), lambda i: (0, 0))),
        scratch_shapes=[pltpu.VMEM((vectors, vectors), jnp.float32)],
        compiler_params=params(),
        name="factor_apply",
    )(gram, filtered)


def solution(mesh):
    in_specs = (P(None, AXES), P(None, AXES), P(), P())
    out_specs = (P(None, AXES), P())
    lo_bits = mesh.shape["lo"].bit_length() - 1
    return jax.shard_map(
        functools.partial(local, lo_bits=lo_bits), mesh=mesh, in_specs=in_specs, out_specs=out_specs, check_vma=False
    )
```

time: 186 us -> 131 us (0.70)
  blocking collectives: 40.5 us -> 0 us
  matrix products: 23.2 us -> 0 us
  starting transfers between devices: 11.7 us -> 30.7 us
  Pallas kernels: 0 us -> 18.2 us
  local copies, waits for them, and re-layouts: 20 us -> 3.75 us
  waiting for transfers between devices: 43.6 us -> 33.9 us
  between operations: 17.7 us -> 14.7 us
    all_to_all x2 -> x0, waiting for transfers between devices: 43.6 us -> none  [the longest x1 43.6 us: local(): lax.all_to_all(shaped, ('hi', 'lo'), split_axis=1, concat_axis=1, tiled=T...]
    psum x1 -> x0, blocking collectives: 40.5 us -> none  [local(): gram_matrix = lax.psum(local_gram, ('hi', 'lo'))]
    ppermute x0 -> x13, waiting for transfers between devices: none -> 33.9 us  [permute(): return lax.ppermute(values, AXES, pairs)]
    ppermute x0 -> x13, starting transfers between devices: none -> 30.7 us  [permute(): return lax.ppermute(values, AXES, pairs)]
    dot_general x7 -> x0, matrix products: 23 us -> none  [the longest x2 6.38 us: cross_flip(): jnp.einsum('vatbl,lj->vatbj', values, permute, precision=lax.Precision.HI...]
    mul x2 -> x1, other arithmetic: 0.77 us -> 19.9 us  [local(): scale * diagonal]
    pallas_call x0 -> x5, Pallas kernels: none -> 18.2 us  [the longest x1 5.69 us: local(): pl.pallas_call(finish_kernel, grid=(steps,), out_shape=(jax.ShapeDtypeStr...]
    all_to_all x2 -> x0, starting transfers between devices: 11.7 us -> none  [the longest x1 7.3 us: local(): lax.all_to_all(shaped, ('hi', 'lo'), split_axis=1, concat_axis=1, tiled=T...]
  transfers between devices with their start and end apart: 2 -> 13, of which waited for: 1 -> 4; matrix products, arithmetic and copies ran while one was open for 22% -> 24% of each run, Pallas kernels for 0% -> 6%
where the time goes in v1:
time: 131 us; the launch traced here: 130 us
  waiting for transfers between devices  33.9 us (26%)
  starting transfers between devices  30.7 us (23%)
  other arithmetic  28.6 us (22%)
  Pallas kernels  18.2 us (14%)
  between operations  14.7 us (11%)
  local copies, waits for them, and re-layouts  3.75 us (3%)
    ppermute x13, waiting for transfers between devices, permute(): return lax.ppermute(values, AXES, pairs)  33.9 us
    ppermute x13, starting transfers between devices, permute(): return lax.ppermute(values, AXES, pairs)  30.7 us
    mul x1, other arithmetic, local(): scale * diagonal  19.9 us
    add x1, other arithmetic, local(): jnp.where(at_site, low_strength, 0.0) * swaps[bit] + high_strength * arrived  6.74 us
    pallas_call x1, Pallas kernels, local(): pl.pallas_call(finish_kernel, grid=(steps,), out_shape=(jax.ShapeDtypeStr...  5.69 us
    pallas_call x1, Pallas kernels, local(): pl.pallas_call(functools.partial(filter_kernel, span=span, scale=1.0 / (a...  4.37 us
    pallas_call x1, Pallas kernels, local(): pl.pallas_call(functools.partial(local_kernel, tile_bonds=tuple(tile_bond...  3.25 us
    pallas_call x1, Pallas kernels, local(): pl.pallas_call(functools.partial(gather_kernel, span=span), grid=(steps,)...  3.22 us
  transfers between devices with their start and end apart: 13, of which 4 were waited for; matrix products, arithmetic and copies ran while one was open for 24% of the time, Pallas kernels for 6%

profile of v1, /device:TPU:0, one launch (start us, length us, event | category | flops | bytes accessed | tf_op | source)
XLA Modules:
  0.0 129.9 jit_solution(1149153290024473594)
XLA Ops:
  0.6 1.4 %collective-permute-start.1 = (f32[32,16384]{1,0:T(8,128)}, f32[32,16384]{1,0:T(8,128)}, u32[]{:S(2)}, u32[]{:S(2)}) collective-permute-start(f32[32,16384]{1,0:T(8,128)} %x_ref.3), channel_id=1, source_target_pairs={{8,4},{9,5},{10,6},{11,7},{12,28},{13,29},{14,30},{15,31},{16,0},{... | collective-permute-start | bytes 6291464 | tf_op jit(solution)/shard_map/ppermute | solution.py:208
  2.1 2.0 %collective-permute-start = (f32[32,16384]{1,0:T(8,128)}, f32[32,16384]{1,0:T(8,128)}, u32[]{:S(2)}, u32[]{:S(2)}) collective-permute-start(f32[32,16384]{1,0:T(8,128)} %x_ref.3), channel_id=1, source_target_pairs={{2,1},{3,2},{4,5},{5,6},{10,9},{11,10},{12,13},{13,14},{18,17},{19... | collective-permute-start | bytes 6291464 | tf_op jit(solution)/shard_map/ppermute | solution.py:208
  4.1 3.8 %collective-permute-start.3 = (f32[32,16384]{1,0:T(8,128)}, f32[32,16384]{1,0:T(8,128)}, u32[]{:S(2)}, u32[]{:S(2)}) collective-permute-start(f32[32,16384]{1,0:T(8,128)} %x_ref.3), channel_id=1, source_target_pairs={{0,4},{1,5},{2,6},{3,7},{4,0},{5,1},{6,2},{7,3},{8,12},{9,13},{10,... | collective-permute-start | bytes 6291464 | tf_op jit(solution)/shard_map/ppermute | solution.py:208
  7.9 1.6 %copy-done = f32[32,16384]{1,0:T(8,128)S(1)} copy-done((f32[32,16384]{1,0:T(8,128)S(1)}, f32[32,16384]{1,0:T(8,128)}, u32[]{:S(2)}) %copy-start) | copy-done | bytes 2097176
  9.5 1.7 %take_half.1 = f32[32,8192]{1,0:T(8,128)} custom-call(s32[1]{0:T(128)} %bitcast.44.select_ref, f32[32,16384]{1,0:T(8,128)S(1)} %copy-done), custom_call_target="tpu_custom_call" | custom-call | tf_op jit(solution)/shard_map/take_half/pallas_call | solution.py:69
  11.2 1.3 collective-permute-start.2
  12.6 0.7 fusion.17
  15.9 0.7 fusion.16
  19.7 0.7 fusion.15
  21.6 7.7 %collective-permute-done.1.two_ref = f32[32,16384]{1,0:T(8,128)} collective-permute-done((f32[32,16384]{1,0:T(8,128)}, f32[32,16384]{1,0:T(8,128)}, u32[]{:S(2)}, u32[]{:S(2)}) %collective-permute-start.1) | collective-permute-done | bytes 2097184 | tf_op jit(solution)/shard_map/ppermute | solution.py:208
  29.4 6.7 %multiply_add_fusion = (f32[32,16384]{1,0:T(8,128)}, f32[32,16384]{1,0:T(8,128)}) fusion(f32[32,16384]{1,0:T(8,128)} %collective-permute-done.1.two_ref, f32[32,16384]{1,0:T(8,128)} %collective-permute-done.3, f32[]{:T(128)} %bitcast.46, f32[]{:T(128)S(6)} %select_n.62, f32[32,16384]{1,0:T(8,128)} %collective-permute-done.one_ref, f32[]{:T(128)} %bitcast.45, ...), kind=kLoop, calls=%fused_computation | loop fusion | flops 3145728 | bytes 10485776 | tf_op jit(solution)/shard_map/add | solution.py:284
  36.1 2.8 %collective-permute-start.5 = (f32[32,16384]{1,0:T(8,128)}, f32[32,16384]{1,0:T(8,128)}, u32[]{:S(2)}, u32[]{:S(2)}) collective-permute-start(f32[32,16384]{1,0:T(8,128)} %get-tuple-element.8), channel_id=1, source_target_pairs={{0,8},{1,9},{2,10},{3,11},{4,16},{5,17},{6,18},{7,19},{24,12},{25,... | collective-permute-start | bytes 6291464 | tf_op jit(solution)/shard_map/ppermute | solution.py:208
  38.9 2.0 %collective-permute-start.4 = (f32[32,16384]{1,0:T(8,128)}, f32[32,16384]{1,0:T(8,128)}, u32[]{:S(2)}, u32[]{:S(2)}) collective-permute-start(f32[32,16384]{1,0:T(8,128)} %get-tuple-element.9), channel_id=1, source_target_pairs={{1,4},{2,5},{5,2},{6,3},{9,12},{10,13},{13,10},{14,11},{17,20},{18... | collective-permute-start | bytes 6291464 | tf_op jit(solution)/shard_map/ppermute | solution.py:208
  40.9 19.9 %add_multiply_fusion.diag_ref = f32[1,16384]{1,0:T(1,128)S(1)} fusion(f32[]{:T(128)S(6)} %mul.707, f32[]{:T(128)S(6)} %mul.706, f32[]{:T(128)S(6)} %mul.704, f32[]{:T(128)S(6)} %mul.703, f32[]{:T(128)S(6)} %mul.701, f32[]{:T(128)S(6)} %mul.700, f32[]{:T(128)S(6)} %mul.698, f32[]{:T(128)S(6)} %mul.697, f32[]{:T(128)S(6)} %mul.695, f32[]{:T(128)S(6)} %sub.263, ...), kind=kLoop, calls=%fused_computation.17 | loop fusion | flops 2211840 | bytes 65688 | tf_op jit(solution)/shard_map/mul | solution.py:274
  60.9 11.4 %collective-permute-start.6 = (f32[32,8192]{1,0:T(8,128)}, f32[32,8192]{1,0:T(8,128)}, u32[]{:S(2)}, u32[]{:S(2)}) collective-permute-start(f32[32,8192]{1,0:T(8,128)} %take_half.1), channel_id=1, source_target_pairs={{0,1},{3,2},{4,5},{7,6},{8,9},{11,10},{12,13},{15,14},{16,17},{19,... | collective-permute-start | bytes 3145736 | tf_op jit(solution)/shard_map/ppermute | solution.py:208
  72.3 1.3 %pad_maximum_fusion.1.weight_ref = f32[7]{0:T(128)S(1)} fusion(f32[1]{0:T(128)} %constant.37.clone.1, f32[1]{0:T(128)} %get-tuple-element.12, f32[1]{0:T(128)} %get-tuple-element.13, f32[4]{0:T(128)S(1)} %bitcast.48), kind=kLoop, calls=%fused_computation.43 | loop fusion | flops 21 | bytes 56 | tf_op jit(solution)/shard_map/stack | solution.py:266
  80.5 0.4 add_convert_fusion.matrix_ref
  81.0 3.3 %local_bonds.1.local_ref = f32[32,16384]{1,0:T(8,128)S(1)} custom-call(f32[7]{0:T(128)S(1)} %pad_maximum_fusion.1.weight_ref, f32[32,16384]{1,0:T(8,128)S(1)} %copy-done.1, f32[32,16384]{1,0:T(8,128)} %prev_ref.1, f32[1,16384]{1,0:T(1,128)S(1)} %add_multiply_fusion.diag_ref, bf16[256,256]{1,0:T(8,128)(2,1)S(1)} %add_convert_fusion.matrix_ref), custom_call_target="tpu_custom_call" | custom-call | tf_op jit(solution)/shard_map/local_bonds/pallas_call | solution.py:267
  84.2 0.1 pad_maximum_fusion.weight_ref
  84.3 3.2 %gather_first.1.acc_ref = f32[32,16384]{1,0:T(8,128)S(1)} custom-call(f32[4]{0:T(128)S(1)} %pad_maximum_fusion.weight_ref, f32[32,16384]{1,0:T(8,128)S(1)} %local_bonds.1.local_ref, f32[32,16384]{1,0:T(8,128)} %collective-permute-done.one_ref, f32[32,16384]{1,0:T(8,128)} %collective-permute-done.1.two_ref, f32[32,8192]{1,0:T(8,128)S(1)} %collective-permute-done.2.half_ref), custom_call_target="tpu_custom_call" | custom-call | tf_op jit(solution)/shard_map/gather_first/pallas_call | solution.py:313
  87.5 7.6 %collective-permute-done.6.half_ref = f32[32,8192]{1,0:T(8,128)} collective-permute-done((f32[32,8192]{1,0:T(8,128)}, f32[32,8192]{1,0:T(8,128)}, u32[]{:S(2)}, u32[]{:S(2)}) %collective-permute-start.6) | collective-permute-done | bytes 1048608 | tf_op jit(solution)/shard_map/ppermute | solution.py:208
  95.1 0.0 collective-permute-done.5.two_ref
  95.1 4.4 %filter_gram.1 = (f32[32,16384]{1,0:T(8,128)S(1)}, f32[32,32]{1,0:T(8,128)S(1)}) custom-call(f32[4]{0:T(128)S(1)} %pad_maximum_fusion.weight_ref, f32[32,16384]{1,0:T(8,128)S(1)} %gather_first.1.acc_ref, f32[32,16384]{1,0:T(8,128)} %collective-permute-done.4.one_ref, f32[32,16384]{1,0:T(8,128)} %collective-permute-done.5.two_ref, ...), custom_call_target="tpu_custom_call" | custom-call | tf_op jit(solution)/shard_map/filter_gram/pallas_call | solution.py:322
  99.5 2.0 %collective-permute-start.7 = (f32[32,32]{1,0:T(8,128)S(1)}, f32[32,32]{1,0:T(8,128)S(1)}, u32[]{:S(2)}, u32[]{:S(2)}) collective-permute-start(f32[32,32]{1,0:T(8,128)S(1)} %get-tuple-element.6), channel_id=1, source_target_pairs={{0,4},{1,5},{2,6},{3,7},{8,12},{9,13},{10,14},{11,15},{16,20},{17,... | collective-permute-start | bytes 12296 | tf_op jit(solution)/shard_map/ppermute | solution.py:208
  101.5 0.8 collective-permute-done.7
  102.3 0.7 collective-permute-start.8
  103.0 0.7 collective-permute-start.9
  103.7 0.7 collective-permute-start.10
  104.4 0.7 collective-permute-start.11
  105.1 1.3 collective-permute-start.12
  106.4 17.8 %collective-permute-done.12 = f32[32,32]{1,0:T(8,128)S(1)} collective-permute-done((f32[32,32]{1,0:T(8,128)S(1)}, f32[32,32]{1,0:T(8,128)S(1)}, u32[]{:S(2)}, u32[]{:S(2)}) %collective-permute-start.12) | collective-permute-done | bytes 4128 | tf_op jit(solution)/shard_map/ppermute | solution.py:208
  124.2 5.7 %factor_apply.1 = (f32[32,16384]{1,0:T(8,128)}, f32[32,32]{1,0:T(8,128)}) custom-call(f32[32,32]{1,0:T(8,128)S(1)} %broadcast_select_fusion.gram_ref, f32[32,16384]{1,0:T(8,128)S(1)} %get-tuple-element.7.filtered_ref), custom_call_target="tpu_custom_call" | custom-call | tf_op jit(solution)/shard_map/factor_apply/pallas_call | solution.py:343
  (31 shorter events, 0.1 us)
Async XLA Ops:
  0.6 11.9 %copy-start.2 = (s32[18]{0:T(128)S(1)}, s32[18]{0:T(128)}, u32[]{:S(2)}) copy-start(s32[18]{0:T(128)} %param.7) | copy-start | bytes 220
  0.6 15.2 %copy-start.3 = (s32[19]{0:T(128)S(1)}, s32[19]{0:T(128)}, u32[]{:S(2)}) copy-start(s32[19]{0:T(128)} %param.6) | copy-start | bytes 232
  0.6 28.7 %collective-permute-start.1 = (f32[32,16384]{1,0:T(8,128)}, f32[32,16384]{1,0:T(8,128)}, u32[]{:S(2)}, u32[]{:S(2)}) collective-permute-start(f32[32,16384]{1,0:T(8,128)} %x_ref.3), channel_id=1, source_target_pairs={{8,4},{9,5},{10,6},{11,7},{12,28},{13,29},{14,30},{15,31},{16,0},{... | collective-permute-start | bytes 6291464 | tf_op jit(solution)/shard_map/ppermute | solution.py:208
  2.1 27.3 %collective-permute-start = (f32[32,16384]{1,0:T(8,128)}, f32[32,16384]{1,0:T(8,128)}, u32[]{:S(2)}, u32[]{:S(2)}) collective-permute-start(f32[32,16384]{1,0:T(8,128)} %x_ref.3), channel_id=1, source_target_pairs={{2,1},{3,2},{4,5},{5,6},{10,9},{11,10},{12,13},{13,14},{18,17},{19... | collective-permute-start | bytes 6291464 | tf_op jit(solution)/shard_map/ppermute | solution.py:208
  4.1 25.3 %collective-permute-start.3 = (f32[32,16384]{1,0:T(8,128)}, f32[32,16384]{1,0:T(8,128)}, u32[]{:S(2)}, u32[]{:S(2)}) collective-permute-start(f32[32,16384]{1,0:T(8,128)} %x_ref.3), channel_id=1, source_target_pairs={{0,4},{1,5},{2,6},{3,7},{4,0},{5,1},{6,2},{7,3},{8,12},{9,13},{10,... | collective-permute-start | bytes 6291464 | tf_op jit(solution)/shard_map/ppermute | solution.py:208
  7.9 1.6 %copy-start = (f32[32,16384]{1,0:T(8,128)S(1)}, f32[32,16384]{1,0:T(8,128)}, u32[]{:S(2)}) copy-start(f32[32,16384]{1,0:T(8,128)} %x_ref.3) | copy-start | bytes 6291460
  11.2 73.1 %collective-permute-start.2 = (f32[32,8192]{1,0:T(8,128)}, f32[32,8192]{1,0:T(8,128)S(1)}, u32[]{:S(2)}, u32[]{:S(2)}) collective-permute-start(f32[32,8192]{1,0:T(8,128)} %take_half.1), channel_id=1, source_target_pairs={{1,0},{2,3},{5,4},{6,7},{9,8},{10,11},{13,12},{14,15},{17,16},{18,... | collective-permute-start | bytes 3145736 | tf_op jit(solution)/shard_map/ppermute | solution.py:208
  29.4 51.6 %copy-start.1 = (f32[32,16384]{1,0:T(8,128)S(1)}, f32[32,16384]{1,0:T(8,128)}, u32[]{:S(2)}) copy-start(f32[32,16384]{1,0:T(8,128)} %x_ref.3) | copy-start | bytes 6291460
  36.1 59.0 %collective-permute-start.5 = (f32[32,16384]{1,0:T(8,128)}, f32[32,16384]{1,0:T(8,128)}, u32[]{:S(2)}, u32[]{:S(2)}) collective-permute-start(f32[32,16384]{1,0:T(8,128)} %get-tuple-element.8), channel_id=1, source_target_pairs={{0,8},{1,9},{2,10},{3,11},{4,16},{5,17},{6,18},{7,19},{24,12},{25,... | collective-permute-start | bytes 6291464 | tf_op jit(solution)/shard_map/ppermute | solution.py:208
  38.9 56.2 %collective-permute-start.4 = (f32[32,16384]{1,0:T(8,128)}, f32[32,16384]{1,0:T(8,128)}, u32[]{:S(2)}, u32[]{:S(2)}) collective-permute-start(f32[32,16384]{1,0:T(8,128)} %get-tuple-element.9), channel_id=1, source_target_pairs={{1,4},{2,5},{5,2},{6,3},{9,12},{10,13},{13,10},{14,11},{17,20},{18... | collective-permute-start | bytes 6291464 | tf_op jit(solution)/shard_map/ppermute | solution.py:208
  60.9 34.2 %collective-permute-start.6 = (f32[32,8192]{1,0:T(8,128)}, f32[32,8192]{1,0:T(8,128)}, u32[]{:S(2)}, u32[]{:S(2)}) collective-permute-start(f32[32,8192]{1,0:T(8,128)} %take_half.1), channel_id=1, source_target_pairs={{0,1},{3,2},{4,5},{7,6},{8,9},{11,10},{12,13},{15,14},{16,17},{19,... | collective-permute-start | bytes 3145736 | tf_op jit(solution)/shard_map/ppermute | solution.py:208
  99.5 2.8 %collective-permute-start.7 = (f32[32,32]{1,0:T(8,128)S(1)}, f32[32,32]{1,0:T(8,128)S(1)}, u32[]{:S(2)}, u32[]{:S(2)}) collective-permute-start(f32[32,32]{1,0:T(8,128)S(1)} %get-tuple-element.6), channel_id=1, source_target_pairs={{0,4},{1,5},{2,6},{3,7},{8,12},{9,13},{10,14},{11,15},{16,20},{17,... | collective-permute-start | bytes 12296 | tf_op jit(solution)/shard_map/ppermute | solution.py:208
  102.3 0.7 collective-permute-start.8
  103.0 0.7 collective-permute-start.9
  103.7 0.7 collective-permute-start.10
  104.4 0.7 collective-permute-start.11
  105.1 19.1 %collective-permute-start.12 = (f32[32,32]{1,0:T(8,128)S(1)}, f32[32,32]{1,0:T(8,128)S(1)}, u32[]{:S(2)}, u32[]{:S(2)}) collective-permute-start(f32[32,32]{1,0:T(8,128)S(1)} %add.487), channel_id=1, source_target_pairs={{4,0},{5,1},{6,2},{7,3},{12,8},{13,9},{14,10},{15,11},{20,16},{21,... | collective-permute-start | bytes 12296 | tf_op jit(solution)/shard_map/ppermute | solution.py:208

commit v2 on v1

v2 whole, which is shorter than its diff:
```python
import functools

import jax
import jax.numpy as jnp
from jax import lax
from jax.experimental import pallas as pl
from jax.experimental.pallas import tpu as pltpu
from jax.sharding import PartitionSpec as P

FIELD_STEP = 0.75
COUPLING_STEP = 0.5
AXES = ("hi", "lo")
LANES = 128
LANE_BITS = 7
GROUP = 256
GROUP_BITS = 8
VMEM_LIMIT = 48 * 1024 * 1024


def pieces(values, count):
    parts = []
    for _ in range(count):
        part = values.astype(jnp.bfloat16)
        parts.append(part)
        values = values - part.astype(jnp.float32)
    return parts


def smem():
    return pl.BlockSpec(memory_space=pltpu.SMEM)


def params():
    return pltpu.CompilerParams(vmem_limit_bytes=VMEM_LIMIT)


FIRST = {(0, 1, 0): (1, 0, 0), (1, 1, 0): (0, 1, 0), (1, 0, 0): (0, 0, 0), (0, 0, 0): (0, 0, 1)}
SECOND = {(0, 1, 0): (1, 0, 1), (1, 0, 0): (0, 0, 1), (0, 0, 0): (1, 0, 0), (1, 1, 0): (1, 1, 1)}
BOTH = {(0, 1, 0): (1, 0, 0), (1, 0, 0): (0, 1, 0), (1, 1, 0): (1, 1, 1), (0, 0, 0): (0, 0, 1)}
ON = {(1, 0, 1): (1, 1, 1), (0, 0, 0): (0, 1, 0), (1, 0, 0): (0, 0, 1), (0, 0, 1): (1, 0, 0)}


def route(devices, m, table):
    full = {}
    for one, two in table.items():
        full[one] = two
        full[tuple(1 - b for b in one)] = tuple(1 - b for b in two)
    pairs = []
    for device in range(devices):
        goal = full[tuple(device >> m + j & 1 for j in (-1, 0, 1))]
        pairs.append((device, device & ~(7 << m - 1) | goal[0] << m - 1 | goal[1] << m | goal[2] << m + 1))
    return pairs


def bit_of(device_ref, k):
    return device_ref[0] >> k & 1


def cost(flops, moved):
    return pl.CostEstimate(flops=flops, bytes_accessed=moved, transcendentals=0)


def strength_of(bond_ref, bond, scale):
    return bond_ref[bond].astype(jnp.float32) * (0.5 * COUPLING_STEP * scale)


def tile_of(ref, t):
    return ref[:, t * LANES : (t + 1) * LANES]


def across(ref, t, bit):
    if bit >= LANE_BITS:
        return tile_of(ref, t ^ (1 << bit - LANE_BITS))
    values = tile_of(ref, t)
    lane = lax.broadcasted_iota(jnp.int32, values.shape, 1)
    return jnp.where(lane >> bit & 1 == 1, pltpu.roll(values, 1 << bit, 1), pltpu.roll(values, LANES - (1 << bit), 1))


def sided(pair, t, bit):
    if bit >= LANE_BITS:
        return pair[t >> bit - LANE_BITS & 1]
    lane = lax.broadcasted_iota(jnp.int32, (1, LANES), 1)
    return jnp.where(lane >> bit & 1 == 1, pair[1], pair[0])


def local_kernel(device_ref, field_ref, bond_ref, x_ref, prev_ref, out_ref, *, global_bits, scale):
    vectors, amp_count = x_ref.shape
    local_bits = amp_count.bit_length() - 1
    rest_bits = local_bits - global_bits
    site_count = field_ref.shape[0]
    tile_bits = local_bits - LANE_BITS

    def position(site):
        if site >= local_bits:
            return site
        return rest_bits + site if site < global_bits else site - global_bits

    fields = [field_ref[s].astype(jnp.float32) * (FIELD_STEP * scale) for s in range(site_count)]
    couplings = [bond_ref[s].astype(jnp.float32) * COUPLING_STEP for s in range(site_count - 1)]
    scaled = [value * scale for value in couplings]
    lane = lax.broadcasted_iota(jnp.int32, (1, LANES), 1)
    lane_spin = [0.5 - (lane >> k & 1).astype(jnp.float32) for k in range(LANE_BITS)]
    far_spin = [0.5 - bit_of(device_ref, k).astype(jnp.float32) for k in range(site_count - local_bits)]

    lane_row = jnp.zeros((1, LANES), jnp.float32)
    rest = jnp.float32(0.0)
    fields_of = [jnp.float32(0.0)] * tile_bits
    bonds_of = [[] for _ in range(tile_bits)]
    mixed = []
    for s in range(site_count):
        spot = position(s)
        if spot < LANE_BITS:
            lane_row = lane_row + fields[s] * lane_spin[spot]
        elif spot < local_bits:
            fields_of[spot - LANE_BITS] = fields_of[spot - LANE_BITS] + fields[s]
        else:
            rest = rest + fields[s] * far_spin[spot - local_bits]
        if s == site_count - 1:
            continue
        low, high = sorted((spot, position(s + 1)))
        if high < LANE_BITS:
            lane_row = lane_row + scaled[s] * (lane_spin[low] * lane_spin[high])
        elif high < local_bits and low >= LANE_BITS:
            bonds_of[high - LANE_BITS].append((low - LANE_BITS, scaled[s]))
        elif high < local_bits:
            mixed.append((high - LANE_BITS, scaled[s] * lane_spin[low]))
        elif low >= local_bits:
            rest = rest + scaled[s] * (far_spin[low - local_bits] * far_spin[high - local_bits])
        elif low >= LANE_BITS:
            fields_of[low - LANE_BITS] = fields_of[low - LANE_BITS] + scaled[s] * far_spin[high - local_bits]
        else:
            lane_row = lane_row + scaled[s] * far_spin[high - local_bits] * lane_spin[low]
    number = [rest]
    for k in range(tile_bits):
        longer = []
        for up in (0, 1):
            for t, value in enumerate(number):
                term = (0.5 - up) * fields_of[k]
                for other, coupling in bonds_of[k]:
                    term = term + (0.5 - up) * (0.5 - (t >> other & 1)) * coupling
                longer.append(value + term)
        number = longer
    mixed_bits = sorted({bit for bit, _ in mixed})
    lane_rows = {}
    for pattern in range(1 << len(mixed_bits)):
        row = lane_row
        for bit, vector in mixed:
            row = row + (0.5 - (pattern >> mixed_bits.index(bit) & 1)) * vector
        lane_rows[pattern] = row

    rows = lax.broadcasted_iota(jnp.int32, (GROUP, GROUP), 0)
    cols = lax.broadcasted_iota(jnp.int32, (GROUP, GROUP), 1)
    change = rows ^ cols
    matrix = jnp.zeros((GROUP, GROUP), jnp.float32)
    tile_bonds, wraps = [], []
    for s in range(local_bits - 1):
        low, high = sorted((position(s), position(s + 1)))
        if high < GROUP_BITS:
            chosen = (change == (1 << low | 1 << high)) & ((cols >> low & 1) != (cols >> high & 1))
            matrix = jnp.where(chosen, 0.5 * couplings[s], matrix)
        elif low >= LANE_BITS:
            tile_bonds.append((low - LANE_BITS, high - LANE_BITS, 0.5 * scaled[s]))
        else:
            shown = [jnp.where((lane >> low & 1) != up, 0.5 * scaled[s], 0.0) for up in (0, 1)]
            wraps.append((high - LANE_BITS, low, shown))
    matrix = matrix.astype(jnp.bfloat16)
    stacked = jnp.concatenate([x_ref[:, k * GROUP : (k + 1) * GROUP] for k in range(amp_count // GROUP)], axis=0)
    product = None
    for part in pieces(stacked, 3):
        term = jnp.dot(part, matrix, preferred_element_type=jnp.float32)
        product = term if product is None else product + term

    def tile(t):
        return x_ref[:, t * LANES : (t + 1) * LANES]

    for t in range(amp_count // LANES):
        row = t // 2 * vectors
        side = (t & 1) * LANES
        pattern = sum((t >> bit & 1) << j for j, bit in enumerate(mixed_bits))
        total = (lane_rows[pattern] + number[t]) * tile(t) - prev_ref[:, t * LANES : (t + 1) * LANES]
        total = total + scale * product[row : row + vectors, side : side + LANES]
        for one, two, weight in tile_bonds:
            if (t >> one & 1) != (t >> two & 1):
                total = total + weight * tile(t ^ (1 << one) ^ (1 << two))
        for high, low, shown in wraps:
            up = t >> high & 1
            shift = 1 << low if up == 0 else LANES - (1 << low)
            total = total + shown[up] * pltpu.roll(tile(t ^ (1 << high)), shift, 1)
        out_ref[:, t * LANES : (t + 1) * LANES] = total


def sent_kernel(device_ref, bond_ref, own_ref, swap_ref, arrived_ref, out_ref, *, bit, bond, scale):
    p, m, q = (bit_of(device_ref, k) for k in range(3))
    joint, low, high = (strength_of(bond_ref, bond + k, scale) for k in range(3))
    at_sum = (p != m) & (q != m)
    passing = (p != m) & (q == m)
    corner = (p == m) & (q == m)
    low = jnp.where(at_sum, low, 0.0)
    high = jnp.where(p != m, high, 0.0)
    swap_pair = [jnp.where(passing & (p == side), joint, 0.0) for side in (0, 1)]
    own_pair = [jnp.where(corner & (p == side), joint, 0.0) for side in (0, 1)]
    for t in range(out_ref.shape[1] // LANES):
        total = low * tile_of(swap_ref, t) + high * tile_of(arrived_ref, t)
        total = total + sided(swap_pair, t, bit) * across(swap_ref, t, bit)
        total = total + sided(own_pair, t, bit) * across(own_ref, t, bit)
        out_ref[:, t * LANES : (t + 1) * LANES] = total


def gather_kernel(device_ref, bond_ref, local_ref, first_ref, *refs, bit, local_bits, scale):
    out_ref = refs[-1]
    p, m, q = (bit_of(device_ref, k) for k in range(3))
    joint, low = (strength_of(bond_ref, local_bits - 1 + k, scale) for k in range(2))
    low = jnp.where((p != m) & (q == m), low, 0.0)
    halves = ((p == m) & (q == m)) | ((p != m) & (q != m))
    pair = [jnp.where(halves & (p != side), joint, 0.0) for side in (0, 1)]
    weights = []
    for k in range(len(refs) - 1):
        differ = bit_of(device_ref, 2 * k + 2) != bit_of(device_ref, 2 * k + 3)
        weights.append(jnp.where(differ, strength_of(bond_ref, local_bits + 2 * k + 2, scale), 0.0))
    for t in range(out_ref.shape[1] // LANES):
        total = tile_of(local_ref, t) + low * tile_of(first_ref, t)
        total = total + sided(pair, t, bit) * across(first_ref, t, bit)
        for weight, ref in zip(weights, refs):
            total = total + weight * tile_of(ref, t)
        out_ref[:, t * LANES : (t + 1) * LANES] = total


def packed(gram, vectors):
    fold = max(1, LANES // vectors)
    rows = vectors // fold
    return jnp.concatenate([gram[k * rows : (k + 1) * rows, :] for k in range(fold)], axis=1)


def unpacked(table, vectors):
    fold = max(1, LANES // vectors)
    return jnp.concatenate([table[:, k * vectors : (k + 1) * vectors] for k in range(fold)], axis=0)


def filter_kernel(device_ref, bond_ref, acc_ref, second_ref, *refs, local_bits, scale, share):
    out_ref, gram_ref, total_ref = refs[-3:]
    step = pl.program_id(0)
    vectors = acc_ref.shape[0]
    weights = []
    for k in range(len(refs) - 3):
        differ = bit_of(device_ref, 2 * k + 3) != bit_of(device_ref, 2 * k + 4)
        weights.append(jnp.where(differ, strength_of(bond_ref, local_bits + 2 * k + 3, scale), 0.0))

    @pl.when(step == 0)
    def _():
        total_ref[...] = jnp.zeros_like(total_ref)

    total = acc_ref[...] + second_ref[...]
    for weight, ref in zip(weights, refs):
        total = total + weight * ref[...]
    out_ref[...] = total
    stacked = jnp.concatenate(pieces(out_ref[...], 3), axis=0)
    total_ref[...] += lax.dot_general(
        stacked, stacked, (((1,), (1,)), ((), ())), preferred_element_type=jnp.float32
    )

    @pl.when(step == pl.num_programs(0) - 1)
    def _():
        table = total_ref[...]

        def block(a, b):
            return table[a * vectors : (a + 1) * vectors, b * vectors : (b + 1) * vectors]

        gram = block(0, 0) + (block(0, 1) + block(1, 0)) + (block(1, 1) + (block(0, 2) + block(2, 0)))
        gram_ref[...] = packed(gram * share, vectors)


def finish_kernel(gram_ref, filtered_ref, out_ref, upper_ref, inverse_ref):
    vectors = filtered_ref.shape[0]

    @pl.when(pl.program_id(0) == 0)
    def _():
        rows = lax.broadcasted_iota(jnp.int32, (vectors, vectors), 0)
        cols = lax.broadcasted_iota(jnp.int32, (vectors, vectors), 1)
        rest = unpacked(gram_ref[...], vectors)
        inverse = (rows == cols).astype(jnp.float32)
        factor = jnp.zeros_like(rest)
        for k in range(vectors):
            root = lax.rsqrt(rest[k : k + 1, k : k + 1])
            top = rest[k : k + 1, :] * root
            column = rest[:, k : k + 1] * root
            below = jnp.where(rows[:, :1] > k, column, 0.0)
            inverse_row = inverse[k : k + 1, :] * root
            factor = jnp.where(rows == k, jnp.where(cols >= k, top, 0.0), factor)
            inverse = jnp.where(rows == k, inverse_row, inverse - below * inverse_row)
            rest = rest - below * top
        upper_ref[...] = factor
        inverse_ref[...] = inverse

    left = pieces(inverse_ref[...], 3)
    right = pieces(filtered_ref[...], 3)
    order = ((0, 0), (0, 1), (1, 0), (1, 1), (0, 2), (2, 0))
    out_ref[...] = jnp.dot(
        jnp.concatenate([left[a] for a, _ in order], axis=1),
        jnp.concatenate([right[b] for _, b in order], axis=0),
        preferred_element_type=jnp.float32,
    )


def local(previous, current, field_levels, bond_levels, lo_bits):
    vectors, amp_count = current.shape
    site_count = field_levels.shape[0]
    devices = lax.axis_size("hi") * lax.axis_size("lo")
    local_bits = amp_count.bit_length() - 1
    global_bits = devices.bit_length() - 1
    rest_bits = local_bits - global_bits
    device = lax.axis_index("hi") * lax.axis_size("lo") + lax.axis_index("lo")
    place = device.astype(jnp.int32).reshape(1)
    scale = 4.0 / site_count
    whole = jax.ShapeDtypeStruct((vectors, amp_count), jnp.float32)
    size = vectors * amp_count
    steps = 4
    block = pl.BlockSpec((vectors, amp_count // steps), lambda i: (0, i))
    vmem = pl.BlockSpec(memory_space=pltpu.VMEM)

    def permute(values, pairs):
        return lax.ppermute(values, AXES, pairs)

    def flips(mask, keep=lambda i: True):
        return [(i, i ^ mask) for i in range(devices) if keep(i)]

    def strength(bond):
        return (scale * 0.5 * COUPLING_STEP) * bond_levels[bond].astype(jnp.float32)

    middles = tuple(range(3, global_bits - 1, 2))
    first = permute(current, route(devices, 1, FIRST))
    swap = permute(current, flips(4))
    boths = [permute(current, route(devices, m, BOTH)) for m in middles]
    extra = []
    if global_bits % 2 == 0:
        top = global_bits - 1
        moved = permute(current, flips(3 << top - 1, lambda i: (i >> top & 1) != (i >> top - 1 & 1)))
        extra.append(strength(site_count - 2) * moved)

    here = pl.pallas_call(
        functools.partial(local_kernel, global_bits=global_bits, scale=scale),
        out_shape=whole,
        in_specs=[smem()] * 3 + [vmem] * 2,
        out_specs=vmem,
        compiler_params=params(),
        cost_estimate=cost(6 * size * GROUP, 12 * size),
        name="local_bonds",
    )(place, field_levels, bond_levels, current, previous)
    first, here = lax.optimization_barrier((first, here))

    sent = pl.pallas_call(
        functools.partial(sent_kernel, bit=rest_bits - 1, bond=local_bits - 1, scale=scale),
        grid=(steps,),
        out_shape=whole,
        in_specs=[smem()] * 2 + [block] * 3,
        out_specs=block,
        compiler_params=params(),
        cost_estimate=cost(6 * size, 16 * size),
        name="sent_on",
    )(place, bond_levels, current, swap, first)
    second = permute(sent, route(devices, 1, SECOND))
    ons = [permute(both, route(devices, m, ON)) for m, both in zip(middles, boths)]

    for term in extra:
        here = here + term
    acc = pl.pallas_call(
        functools.partial(gather_kernel, bit=rest_bits - 1, local_bits=local_bits, scale=scale),
        grid=(steps,),
        out_shape=whole,
        in_specs=[smem()] * 2 + [block] * (2 + len(boths)),
        out_specs=block,
        compiler_params=params(),
        cost_estimate=cost(6 * size, 16 * size),
        name="gather_first",
    )(place, bond_levels, here, first, *boths)
    fold = max(1, LANES // vectors)
    table = (vectors // fold, vectors * fold)
    table_block = pl.BlockSpec(table, lambda i: (0, 0))
    filtered, gram = pl.pallas_call(
        functools.partial(filter_kernel, local_bits=local_bits, scale=scale, share=1.0 / (amp_count * devices)),
        grid=(steps,),
        out_shape=(whole, jax.ShapeDtypeStruct(table, jnp.float32)),
        in_specs=[smem()] * 2 + [block] * (2 + len(ons)),
        out_specs=(block, table_block),
        scratch_shapes=[pltpu.VMEM((3 * vectors, 3 * vectors), jnp.float32)],
        compiler_params=params(),
        cost_estimate=cost(6 * size * vectors, 16 * size),
        name="filter_gram",
    )(place, bond_levels, acc, second, *ons)

    for k in [lo_bits] + [k for k in range(global_bits) if k != lo_bits]:
        gram = gram + permute(gram, flips(1 << k))

    return pl.pallas_call(
        finish_kernel,
        grid=(steps,),
        out_shape=(whole, jax.ShapeDtypeStruct((vectors, vectors), jnp.float32)),
        in_specs=[table_block, block],
        out_specs=(block, pl.BlockSpec((vectors, vectors), lambda i: (0, 0))),
        scratch_shapes=[pltpu.VMEM((vectors, vectors), jnp.float32)],
        compiler_params=params(),
        cost_estimate=cost(12 * size * vectors, 8 * size),
        name="factor_apply",
    )(gram, filtered)


def solution(mesh):
    in_specs = (P(None, AXES), P(None, AXES), P(), P())
    out_specs = (P(None, AXES), P())
    lo_bits = mesh.shape["lo"].bit_length() - 1
    return jax.shard_map(
        functools.partial(local, lo_bits=lo_bits), mesh=mesh, in_specs=in_specs, out_specs=out_specs, check_vma=False
    )
```

time: 131 us -> 87 us (0.66)
  other arithmetic: 28.6 us -> 0.02 us
  starting transfers between devices: 30.7 us -> 14.5 us
  between operations: 14.7 us -> 0.69 us
  waiting for transfers between devices: 33.9 us -> 47 us
  Pallas kernels: 18.2 us -> 20.2 us
    mul x3 -> x0, other arithmetic: 20 us -> none  [the longest x1 19.9 us: local(): scale * diagonal]
    ppermute x13 -> x10, starting transfers between devices: 30.7 us -> 14.5 us  [permute(): return lax.ppermute(values, AXES, pairs)]
    ppermute x13 -> x10, waiting for transfers between devices: 33.9 us -> 47 us  [permute(): return lax.ppermute(values, AXES, pairs)]
    add x6 -> x5, other arithmetic: 6.77 us -> 0.02 us  [local(): gram = gram + permute(gram, flips(1 << k))]
    unnamed x8 -> x16, local copies, waits for them, and re-layouts: 1.6 us -> 4.24 us
    slice x3 -> x0, local copies, waits for them, and re-layouts: 2.15 us -> none  [the longest x1 0.73 us: local(): couplings[site_number] * spin_value(site_number)]
    pallas_call x5, Pallas kernels: 18.2 us -> 20.2 us  [the longest x1 5.72 us: local(): pl.pallas_call(finish_kernel, grid=(steps,), out_shape=(whole, jax.ShapeD...]
    another operation x2 -> x0, other arithmetic: 1.39 us -> none  [the longest x1 1.31 us: local(): weights = jnp.stack(tile_weights + wrap_weights + [jnp.float32(scale)])]
  transfers between devices with their start and end apart: 13 -> 10, of which waited for: 4 -> 9; matrix products, arithmetic and copies ran while one was open for 24% -> 0% of each run, Pallas kernels for 6% -> 12%
where the time goes in v2:
time: 87 us; the launch traced here: 86.6 us
  waiting for transfers between devices  47 us (54%)
  Pallas kernels  20.2 us (23%)
  starting transfers between devices  14.5 us (17%)
  local copies, waits for them, and re-layouts  4.24 us (5%)
    ppermute x10, waiting for transfers between devices, permute(): return lax.ppermute(values, AXES, pairs)  47 us
    ppermute x10, starting transfers between devices, permute(): return lax.ppermute(values, AXES, pairs)  14.5 us
    pallas_call x1, Pallas kernels, local(): pl.pallas_call(finish_kernel, grid=(steps,), out_shape=(whole, jax.ShapeD...  5.72 us
    pallas_call x1, Pallas kernels, local(): pl.pallas_call(functools.partial(filter_kernel, local_bits=local_bits, sc...  4.24 us
    unnamed x16, local copies, waits for them, and re-layouts  4.24 us
    pallas_call x1, Pallas kernels, local(): pl.pallas_call(functools.partial(local_kernel, global_bits=global_bits, s...  3.71 us
    pallas_call x1, Pallas kernels, local(): pl.pallas_call(functools.partial(sent_kernel, bit=rest_bits - 1, bond=loc...  3.27 us
    pallas_call x1, Pallas kernels, local(): pl.pallas_call(functools.partial(gather_kernel, bit=rest_bits - 1, local_...  3.22 us
  transfers between devices with their start and end apart: 10, of which 9 were waited for; matrix products, arithmetic and copies ran while one was open for 0% of the time, Pallas kernels for 12%

profile of v2, /device:TPU:0, one launch (start us, length us, event | category | flops | bytes accessed | tf_op | source)
XLA Modules:
  0.0 86.6 jit_solution(12182245739978187194)
XLA Ops:
  0.6 0.5 collective-permute-start
  1.1 2.6 %collective-permute-start.1 = (f32[32,16384]{1,0:T(8,128)}, f32[32,16384]{1,0:T(8,128)}, u32[]{:S(2)}, u32[]{:S(2)}) collective-permute-start(f32[32,16384]{1,0:T(8,128)} %own_ref.1), channel_id=1, source_target_pairs={{0,16},{1,17},{2,18},{3,19},{4,8},{5,9},{6,10},{7,11},{8,4},{9,5},... | collective-permute-start | bytes 6291464 | tf_op jit(solution)/shard_map/ppermute | solution.py:321
  3.7 0.1 collective-permute-start.2
  3.8 1.6 %copy-done = f32[32,16384]{1,0:T(8,128)S(1)} copy-done((f32[32,16384]{1,0:T(8,128)S(1)}, f32[32,16384]{1,0:T(8,128)}, u32[]{:S(2)}) %copy-start) | copy-done | bytes 2097176
  5.4 0.7 copy-done.2
  6.0 0.7 copy-done.4
  6.7 3.7 %local_bonds.1.local_ref = f32[32,16384]{1,0:T(8,128)S(1)} custom-call(s32[1]{0:T(128)} %bitcast.device_ref, s32[19]{0:T(128)S(1)} %copy-done.4, s32[18]{0:T(128)S(1)} %copy-done.2, f32[32,16384]{1,0:T(8,128)S(1)} %copy-done, f32[32,16384]{1,0:T(8,128)} %prev_ref.1), custom_call_target="tpu_custom_call" | custom-call | flops 805306368 | bytes 6291456 | tf_op jit(solution)/shard_map/local_bonds/pallas_call | solution.py:339
  10.4 0.0 copy-start.3
  10.4 17.5 %collective-permute-done.first_ref.arrived_ref = f32[32,16384]{1,0:T(8,128)S(1)} collective-permute-done((f32[32,16384]{1,0:T(8,128)}, f32[32,16384]{1,0:T(8,128)S(1)}, u32[]{:S(2)}, u32[]{:S(2)}) %collective-permute-start) | collective-permute-done | bytes 2097184 | tf_op jit(solution)/shard_map/ppermute | solution.py:321
  27.9 0.1 collective-permute-done.1.refs_0_
  28.0 1.8 %collective-permute-start.4 = (f32[32,16384]{1,0:T(8,128)}, f32[32,16384]{1,0:T(8,128)S(1)}, u32[]{:S(2)}, u32[]{:S(2)}) collective-permute-start(f32[32,16384]{1,0:T(8,128)} %collective-permute-done.1.refs_0_), channel_id=1, source_target_pairs={{0,8},{1,9},{2,10},{3,11},{4,16},{5,17},{6,18},{7,19},{8,0},{9,1},... | collective-permute-start | bytes 6291464 | tf_op jit(solution)/shard_map/ppermute | solution.py:321
  29.8 0.0 collective-permute-done.2.swap_ref
  29.8 0.0 copy-done.5
  29.8 0.0 copy-done.1
  29.8 3.3 %sent_on.1 = f32[32,16384]{1,0:T(8,128)S(1)} custom-call(s32[1]{0:T(128)} %bitcast.device_ref, s32[18]{0:T(128)S(1)} %copy-done.2, f32[32,16384]{1,0:T(8,128)S(1)} %copy-done.1, f32[32,16384]{1,0:T(8,128)} %collective-permute-done.2.swap_ref, f32[32,16384]{1,0:T(8,128)} %copy-done.5), custom_call_target="tpu_custom_call" | custom-call | flops 3145728 | bytes 8388608 | tf_op jit(solution)/shard_map/sent_on/pallas_call | solution.py:350
  33.1 1.6 %collective-permute-start.3 = (f32[32,16384]{1,0:T(8,128)S(1)}, f32[32,16384]{1,0:T(8,128)S(1)}, u32[]{:S(2)}, u32[]{:S(2)}) collective-permute-start(f32[32,16384]{1,0:T(8,128)S(1)} %sent_on.1), channel_id=1, source_target_pairs={{0,1},{1,4},{2,5},{3,7},{4,0},{5,2},{6,3},{7,6},{8,9},{9,12},{10,1... | collective-permute-start | bytes 6291464 | tf_op jit(solution)/shard_map/ppermute | solution.py:321
  34.8 3.2 %gather_first.1.acc_ref = f32[32,16384]{1,0:T(8,128)S(1)} custom-call(s32[1]{0:T(128)} %bitcast.device_ref, s32[18]{0:T(128)S(1)} %copy-done.3, f32[32,16384]{1,0:T(8,128)S(1)} %local_bonds.1.local_ref, f32[32,16384]{1,0:T(8,128)} %copy-done.5, f32[32,16384]{1,0:T(8,128)} %collective-permute-done.1.refs_0_), custom_call_target="tpu_custom_call" | custom-call | flops 3145728 | bytes 8388608 | tf_op jit(solution)/shard_map/gather_first/pallas_call | solution.py:365
  38.0 16.3 %collective-permute-done.4.refs_0_ = f32[32,16384]{1,0:T(8,128)S(1)} collective-permute-done((f32[32,16384]{1,0:T(8,128)}, f32[32,16384]{1,0:T(8,128)S(1)}, u32[]{:S(2)}, u32[]{:S(2)}) %collective-permute-start.4) | collective-permute-done | bytes 2097184 | tf_op jit(solution)/shard_map/ppermute | solution.py:321
  54.3 4.0 %collective-permute-done.3.second_ref = f32[32,16384]{1,0:T(8,128)S(1)} collective-permute-done((f32[32,16384]{1,0:T(8,128)S(1)}, f32[32,16384]{1,0:T(8,128)S(1)}, u32[]{:S(2)}, u32[]{:S(2)}) %collective-permute-start.3) | collective-permute-done | bytes 2097184 | tf_op jit(solution)/shard_map/ppermute | solution.py:321
  58.3 1.3 %copy-done.7 = f32[32,16384]{1,0:T(8,128)} copy-done((f32[32,16384]{1,0:T(8,128)}, f32[32,16384]{1,0:T(8,128)S(1)}, u32[]{:S(2)}) %copy-start.7) | copy-done | bytes 2097176
  59.6 4.2 %filter_gram.1 = (f32[32,16384]{1,0:T(8,128)S(1)}, f32[8,128]{1,0:T(8,128)S(1)}) custom-call(s32[1]{0:T(128)} %bitcast.device_ref, s32[18]{0:T(128)S(1)} %copy-done.3, f32[32,16384]{1,0:T(8,128)S(1)} %gather_first.1.acc_ref, f32[32,16384]{1,0:T(8,128)} %copy-done.7, f32[32,16384]{1,0:T(8,128)} %copy-done.6), custom_call_target="tpu_custom_call" | custom-call | flops 100663296 | bytes 8388608 | tf_op jit(solution)/shard_map/filter_gram/pallas_call | solution.py:378
  63.9 0.7 collective-permute-start.5
  64.6 0.8 collective-permute-done.5
  65.4 2.2 %collective-permute-start.6 = (f32[8,128]{1,0:T(8,128)S(1)}, f32[8,128]{1,0:T(8,128)S(1)}, u32[]{:S(2)}, u32[]{:S(2)}) collective-permute-start(f32[8,128]{1,0:T(8,128)S(1)} %add.19), channel_id=1, source_target_pairs={{0,1},{1,0},{2,3},{3,2},{4,5},{5,4},{6,7},{7,6},{8,9},{9,8},{10,11... | collective-permute-start | bytes 12296 | tf_op jit(solution)/shard_map/ppermute | solution.py:321
  67.6 1.6 %collective-permute-done.6 = f32[8,128]{1,0:T(8,128)S(1)} collective-permute-done((f32[8,128]{1,0:T(8,128)S(1)}, f32[8,128]{1,0:T(8,128)S(1)}, u32[]{:S(2)}, u32[]{:S(2)}) %collective-permute-start.6) | collective-permute-done | bytes 4128 | tf_op jit(solution)/shard_map/ppermute | solution.py:321
  69.2 2.5 %collective-permute-start.7 = (f32[8,128]{1,0:T(8,128)S(1)}, f32[8,128]{1,0:T(8,128)S(1)}, u32[]{:S(2)}, u32[]{:S(2)}) collective-permute-start(f32[8,128]{1,0:T(8,128)S(1)} %add.20), channel_id=1, source_target_pairs={{0,2},{1,3},{2,0},{3,1},{4,6},{5,7},{6,4},{7,5},{8,10},{9,11},{10,... | collective-permute-start | bytes 12296 | tf_op jit(solution)/shard_map/ppermute | solution.py:321
  71.6 2.0 %collective-permute-done.7 = f32[8,128]{1,0:T(8,128)S(1)} collective-permute-done((f32[8,128]{1,0:T(8,128)S(1)}, f32[8,128]{1,0:T(8,128)S(1)}, u32[]{:S(2)}, u32[]{:S(2)}) %collective-permute-start.7) | collective-permute-done | bytes 4128 | tf_op jit(solution)/shard_map/ppermute | solution.py:321
  73.7 1.3 %collective-permute-start.8 = (f32[8,128]{1,0:T(8,128)S(1)}, f32[8,128]{1,0:T(8,128)S(1)}, u32[]{:S(2)}, u32[]{:S(2)}) collective-permute-start(f32[8,128]{1,0:T(8,128)S(1)} %add.21), channel_id=1, source_target_pairs={{0,8},{1,9},{2,10},{3,11},{4,12},{5,13},{6,14},{7,15},{8,0},{9,1},... | collective-permute-start | bytes 12296 | tf_op jit(solution)/shard_map/ppermute | solution.py:321
  75.0 2.3 %collective-permute-done.8 = f32[8,128]{1,0:T(8,128)S(1)} collective-permute-done((f32[8,128]{1,0:T(8,128)S(1)}, f32[8,128]{1,0:T(8,128)S(1)}, u32[]{:S(2)}, u32[]{:S(2)}) %collective-permute-start.8) | collective-permute-done | bytes 4128 | tf_op jit(solution)/shard_map/ppermute | solution.py:321
  77.3 1.3 %collective-permute-start.9 = (f32[8,128]{1,0:T(8,128)S(1)}, f32[8,128]{1,0:T(8,128)S(1)}, u32[]{:S(2)}, u32[]{:S(2)}) collective-permute-start(f32[8,128]{1,0:T(8,128)S(1)} %add.22), channel_id=1, source_target_pairs={{0,16},{1,17},{2,18},{3,19},{4,20},{5,21},{6,22},{7,23},{8,24},{9,... | collective-permute-start | bytes 12296 | tf_op jit(solution)/shard_map/ppermute | solution.py:321
  78.6 2.3 %collective-permute-done.9 = f32[8,128]{1,0:T(8,128)S(1)} collective-permute-done((f32[8,128]{1,0:T(8,128)S(1)}, f32[8,128]{1,0:T(8,128)S(1)}, u32[]{:S(2)}, u32[]{:S(2)}) %collective-permute-start.9) | collective-permute-done | bytes 4128 | tf_op jit(solution)/shard_map/ppermute | solution.py:321
  80.9 5.7 %factor_apply.1 = (f32[32,16384]{1,0:T(8,128)}, f32[32,32]{1,0:T(8,128)}) custom-call(f32[8,128]{1,0:T(8,128)S(1)} %add.23.gram_ref, f32[32,16384]{1,0:T(8,128)S(1)} %get-tuple-element.9.filtered_ref), custom_call_target="tpu_custom_call" | custom-call | flops 201326592 | bytes 4194304 | tf_op jit(solution)/shard_map/factor_apply/pallas_call | solution.py:393
  (14 shorter events, 0.0 us)
Async XLA Ops:
  0.6 27.3 %collective-permute-start = (f32[32,16384]{1,0:T(8,128)}, f32[32,16384]{1,0:T(8,128)S(1)}, u32[]{:S(2)}, u32[]{:S(2)}) collective-permute-start(f32[32,16384]{1,0:T(8,128)} %own_ref.1), channel_id=1, source_target_pairs={{0,4},{1,0},{2,1},{3,2},{4,5},{5,6},{6,7},{7,3},{8,12},{9,8},{10,9... | collective-permute-start | bytes 6291464 | tf_op jit(solution)/shard_map/ppermute | solution.py:321
  1.1 26.9 %collective-permute-start.1 = (f32[32,16384]{1,0:T(8,128)}, f32[32,16384]{1,0:T(8,128)}, u32[]{:S(2)}, u32[]{:S(2)}) collective-permute-start(f32[32,16384]{1,0:T(8,128)} %own_ref.1), channel_id=1, source_target_pairs={{0,16},{1,17},{2,18},{3,19},{4,8},{5,9},{6,10},{7,11},{8,4},{9,5},... | collective-permute-start | bytes 6291464 | tf_op jit(solution)/shard_map/ppermute | solution.py:321
  3.7 26.1 %collective-permute-start.2 = (f32[32,16384]{1,0:T(8,128)}, f32[32,16384]{1,0:T(8,128)}, u32[]{:S(2)}, u32[]{:S(2)}) collective-permute-start(f32[32,16384]{1,0:T(8,128)} %own_ref.1), channel_id=1, source_target_pairs={{0,4},{1,5},{2,6},{3,7},{4,0},{5,1},{6,2},{7,3},{8,12},{9,13},{10,... | collective-permute-start | bytes 6291464 | tf_op jit(solution)/shard_map/ppermute | solution.py:321
  3.8 1.6 %copy-start = (f32[32,16384]{1,0:T(8,128)S(1)}, f32[32,16384]{1,0:T(8,128)}, u32[]{:S(2)}) copy-start(f32[32,16384]{1,0:T(8,128)} %own_ref.1) | copy-start | bytes 6291460
  5.4 0.7 copy-start.2
  6.0 0.7 copy-start.4
  6.7 23.2 %copy-start.1 = (f32[32,16384]{1,0:T(8,128)S(1)}, f32[32,16384]{1,0:T(8,128)}, u32[]{:S(2)}) copy-start(f32[32,16384]{1,0:T(8,128)} %own_ref.1) | copy-start | bytes 6291460
  10.4 24.4 %copy-start.3 = (s32[18]{0:T(128)S(1)}, s32[18]{0:T(128)}, u32[]{:S(2)}) copy-start(s32[18]{0:T(128)} %bond_ref.7) | copy-start | bytes 220
  27.9 1.9 %copy-start.5 = (f32[32,16384]{1,0:T(8,128)}, f32[32,16384]{1,0:T(8,128)S(1)}, u32[]{:S(2)}) copy-start(f32[32,16384]{1,0:T(8,128)S(1)} %collective-permute-done.first_ref.arrived_ref) | copy-start | bytes 6291460
  28.0 26.2 %collective-permute-start.4 = (f32[32,16384]{1,0:T(8,128)}, f32[32,16384]{1,0:T(8,128)S(1)}, u32[]{:S(2)}, u32[]{:S(2)}) collective-permute-start(f32[32,16384]{1,0:T(8,128)} %collective-permute-done.1.refs_0_), channel_id=1, source_target_pairs={{0,8},{1,9},{2,10},{3,11},{4,16},{5,17},{6,18},{7,19},{8,0},{9,1},... | collective-permute-start | bytes 6291464 | tf_op jit(solution)/shard_map/ppermute | solution.py:321
  33.1 25.2 %collective-permute-start.3 = (f32[32,16384]{1,0:T(8,128)S(1)}, f32[32,16384]{1,0:T(8,128)S(1)}, u32[]{:S(2)}, u32[]{:S(2)}) collective-permute-start(f32[32,16384]{1,0:T(8,128)S(1)} %sent_on.1), channel_id=1, source_target_pairs={{0,1},{1,4},{2,5},{3,7},{4,0},{5,2},{6,3},{7,6},{8,9},{9,12},{10,1... | collective-permute-start | bytes 6291464 | tf_op jit(solution)/shard_map/ppermute | solution.py:321
  54.3 4.0 %copy-start.6 = (f32[32,16384]{1,0:T(8,128)}, f32[32,16384]{1,0:T(8,128)S(1)}, u32[]{:S(2)}) copy-start(f32[32,16384]{1,0:T(8,128)S(1)} %collective-permute-done.4.refs_0_) | copy-start | bytes 6291460
  58.3 1.3 %copy-start.7 = (f32[32,16384]{1,0:T(8,128)}, f32[32,16384]{1,0:T(8,128)S(1)}, u32[]{:S(2)}) copy-start(f32[32,16384]{1,0:T(8,128)S(1)} %collective-permute-done.3.second_ref) | copy-start | bytes 6291460
  63.9 1.5 %collective-permute-start.5 = (f32[8,128]{1,0:T(8,128)S(1)}, f32[8,128]{1,0:T(8,128)S(1)}, u32[]{:S(2)}, u32[]{:S(2)}) collective-permute-start(f32[8,128]{1,0:T(8,128)S(1)} %get-tuple-element.8), channel_id=1, source_target_pairs={{0,4},{1,5},{2,6},{3,7},{4,0},{5,1},{6,2},{7,3},{8,12},{9,13},{10,... | collective-permute-start | bytes 12296 | tf_op jit(solution)/shard_map/ppermute | solution.py:321
  65.4 3.8 %collective-permute-start.6 = (f32[8,128]{1,0:T(8,128)S(1)}, f32[8,128]{1,0:T(8,128)S(1)}, u32[]{:S(2)}, u32[]{:S(2)}) collective-permute-start(f32[8,128]{1,0:T(8,128)S(1)} %add.19), channel_id=1, source_target_pairs={{0,1},{1,0},{2,3},{3,2},{4,5},{5,4},{6,7},{7,6},{8,9},{9,8},{10,11... | collective-permute-start | bytes 12296 | tf_op jit(solution)/shard_map/ppermute | solution.py:321
  69.2 4.5 %collective-permute-start.7 = (f32[8,128]{1,0:T(8,128)S(1)}, f32[8,128]{1,0:T(8,128)S(1)}, u32[]{:S(2)}, u32[]{:S(2)}) collective-permute-start(f32[8,128]{1,0:T(8,128)S(1)} %add.20), channel_id=1, source_target_pairs={{0,2},{1,3},{2,0},{3,1},{4,6},{5,7},{6,4},{7,5},{8,10},{9,11},{10,... | collective-permute-start | bytes 12296 | tf_op jit(solution)/shard_map/ppermute | solution.py:321
  73.7 3.6 %collective-permute-start.8 = (f32[8,128]{1,0:T(8,128)S(1)}, f32[8,128]{1,0:T(8,128)S(1)}, u32[]{:S(2)}, u32[]{:S(2)}) collective-permute-start(f32[8,128]{1,0:T(8,128)S(1)} %add.21), channel_id=1, source_target_pairs={{0,8},{1,9},{2,10},{3,11},{4,12},{5,13},{6,14},{7,15},{8,0},{9,1},... | collective-permute-start | bytes 12296 | tf_op jit(solution)/shard_map/ppermute | solution.py:321
  77.3 3.6 %collective-permute-start.9 = (f32[8,128]{1,0:T(8,128)S(1)}, f32[8,128]{1,0:T(8,128)S(1)}, u32[]{:S(2)}, u32[]{:S(2)}) collective-permute-start(f32[8,128]{1,0:T(8,128)S(1)} %add.22), channel_id=1, source_target_pairs={{0,16},{1,17},{2,18},{3,19},{4,20},{5,21},{6,22},{7,23},{8,24},{9,... | collective-permute-start | bytes 12296 | tf_op jit(solution)/shard_map/ppermute | solution.py:321

commit v3 on v2

--- a/solution.py
+++ b/solution.py
@@ -11,8 +11,11 @@
 COUPLING_STEP = 0.5
 AXES = ("hi", "lo")
 LANES = 128
+SUBLANES = 8
 LANE_BITS = 7
 GROUP = 256
+CHUNK = 1024
+OUT_CHUNK = 2048
 GROUP_BITS = 8
 VMEM_LIMIT = 48 * 1024 * 1024
 
@@ -30,8 +33,8 @@
     return pl.BlockSpec(memory_space=pltpu.SMEM)
 
 
-def params():
-    return pltpu.CompilerParams(vmem_limit_bytes=VMEM_LIMIT)
+def params(limit=VMEM_LIMIT):
+    return pltpu.CompilerParams(vmem_limit_bytes=limit)
 
 
 FIRST = {(0, 1, 0): (1, 0, 0), (1, 1, 0): (0, 1, 0), (1, 0, 0): (0, 0, 0), (0, 0, 0): (0, 0, 1)}
@@ -189,7 +192,46 @@
         out_ref[:, t * LANES : (t + 1) * LANES] = total
 
 
-def sent_kernel(device_ref, bond_ref, own_ref, swap_ref, arrived_ref, out_ref, *, bit, bond, scale):
+def cut_kernel(x_ref, out_ref, held_ref, in_sems, out_sems, *, start):
+    rows, width = held_ref.shape
+    strips = [pl.ds(k * SUBLANES, SUBLANES) for k in range(rows // SUBLANES)]
+    loads = [
+        pltpu.make_async_copy(x_ref.at[strip, pl.ds(start, width)], held_ref.at[strip], in_sems.at[k])
+        for k, strip in enumerate(strips)
+    ]
+    stores = [
+        pltpu.make_async_copy(held_ref.at[strip], out_ref.at[strip], out_sems.at[k]) for k, strip in enumerate(strips)
+    ]
+    for load in loads:
+        load.start()
+    for load, store in zip(loads, stores):
+        load.wait()
+        store.start()
+    for store in stores:
+        store.wait()
+
+
+def cut(values, start, width):
+    rows = values.shape[0]
+    hbm = pl.BlockSpec(memory_space=pltpu.HBM)
+    strips = rows // SUBLANES
+    return pl.pallas_call(
+        functools.partial(cut_kernel, start=start),
+        out_shape=jax.ShapeDtypeStruct((rows, width), values.dtype),
+        in_specs=[hbm],
+        out_specs=hbm,
+        scratch_shapes=[
+            pltpu.VMEM((rows, width), values.dtype),
+            pltpu.SemaphoreType.DMA((strips,)),
+            pltpu.SemaphoreType.DMA((strips,)),
+        ],
+        compiler_params=params(63 * 1024 * 1024),
+        cost_estimate=cost(0, 8 * rows * width),
+        name=f"cut_{start}",
+    )(values)
+
+
+def sent_kernel(device_ref, bond_ref, own_ref, swap_ref, arrived_ref, out_ref, *, start, bit, bond, scale):
     p, m, q = (bit_of(device_ref, k) for k in range(3))
     joint, low, high = (strength_of(bond_ref, bond + k, scale) for k in range(3))
     at_sum = (p != m) & (q != m)
@@ -200,13 +242,13 @@
     swap_pair = [jnp.where(passing & (p == side), joint, 0.0) for side in (0, 1)]
     own_pair = [jnp.where(corner & (p == side), joint, 0.0) for side in (0, 1)]
     for t in range(out_ref.shape[1] // LANES):
-        total = low * tile_of(swap_ref, t) + high * tile_of(arrived_ref, t)
-        total = total + sided(swap_pair, t, bit) * across(swap_ref, t, bit)
-        total = total + sided(own_pair, t, bit) * across(own_ref, t, bit)
+        total = low * tile_of(swap_ref, start + t) + high * tile_of(arrived_ref, t)
+        total = total + sided(swap_pair, t, bit) * across(swap_ref, start + t, bit)
+        total = total + sided(own_pair, t, bit) * across(own_ref, start + t, bit)
         out_ref[:, t * LANES : (t + 1) * LANES] = total
 
 
-def gather_kernel(device_ref, bond_ref, local_ref, first_ref, *refs, bit, local_bits, scale):
+def gather_kernel(device_ref, bond_ref, local_ref, first_ref, *refs, start, bit, local_bits, scale):
     out_ref = refs[-1]
     p, m, q = (bit_of(device_ref, k) for k in range(3))
     joint, low = (strength_of(bond_ref, local_bits - 1 + k, scale) for k in range(2))
@@ -218,7 +260,7 @@
         differ = bit_of(device_ref, 2 * k + 2) != bit_of(device_ref, 2 * k + 3)
         weights.append(jnp.where(differ, strength_of(bond_ref, local_bits + 2 * k + 2, scale), 0.0))
     for t in range(out_ref.shape[1] // LANES):
-        total = tile_of(local_ref, t) + low * tile_of(first_ref, t)
+        total = tile_of(local_ref, start + t) + low * tile_of(first_ref, t)
         total = total + sided(pair, t, bit) * across(first_ref, t, bit)
         for weight, ref in zip(weights, refs):
             total = total + weight * tile_of(ref, t)
@@ -236,69 +278,100 @@
     return jnp.concatenate([table[:, k * vectors : (k + 1) * vectors] for k in range(fold)], axis=0)
 
 
-def filter_kernel(device_ref, bond_ref, acc_ref, second_ref, *refs, local_bits, scale, share):
-    out_ref, gram_ref, total_ref = refs[-3:]
-    step = pl.program_id(0)
-    vectors = acc_ref.shape[0]
+def filter_kernel(device_ref, bond_ref, before_ref, acc_ref, second_ref, *refs, local_bits, scale, share, last):
+    out_ref, gram_ref = refs[-2:]
+    vectors, amp_count = acc_ref.shape
     weights = []
-    for k in range(len(refs) - 3):
+    for k in range(len(refs) - 2):
         differ = bit_of(device_ref, 2 * k + 3) != bit_of(device_ref, 2 * k + 4)
         weights.append(jnp.where(differ, strength_of(bond_ref, local_bits + 2 * k + 3, scale), 0.0))
-
-    @pl.when(step == 0)
-    def _():
-        total_ref[...] = jnp.zeros_like(total_ref)
-
-    total = acc_ref[...] + second_ref[...]
-    for weight, ref in zip(weights, refs):
-        total = total + weight * ref[...]
-    out_ref[...] = total
-    stacked = jnp.concatenate(pieces(out_ref[...], 3), axis=0)
-    total_ref[...] += lax.dot_general(
-        stacked, stacked, (((1,), (1,)), ((), ())), preferred_element_type=jnp.float32
+    table = before_ref[...]
+    for first in range(0, amp_count, CHUNK):
+        cols = slice(first, min(first + CHUNK, amp_count))
+        total = acc_ref[:, cols] + second_ref[:, cols]
+        for weight, ref in zip(weights, refs):
+            total = total + weight * ref[:, cols]
+        out_ref[:, cols] = total
+        stacked = jnp.concatenate(pieces(total, 3), axis=0)
+        table = table + lax.dot_general(
+            stacked, stacked, (((1,), (1,)), ((), ())), preferred_element_type=jnp.float32
+        )
+    if not last:
+        gram_ref[...] = table
+        return
+
+    def block(a, b):
+        return table[a * vectors : (a + 1) * vectors, b * vectors : (b + 1) * vectors]
+
+    gram = block(0, 0) + (block(0, 1) + block(1, 0)) + (block(1, 1) + (block(0, 2) + block(2, 0)))
+    gram_ref[...] = packed(gram * share, vectors)
+
+
+def reciprocal(values):
+    guess = pl.reciprocal(values, approx=True)
+    guess = guess * (2.0 - values * guess)
+    return guess * (2.0 - values * guess)
+
+
+def factor(gram):
+    vectors = gram.shape[0]
+    lanes = max(LANES, 2 * vectors)
+    rows = lax.broadcasted_iota(jnp.int32, (vectors, lanes), 0)
+    cols = lax.broadcasted_iota(jnp.int32, (vectors, lanes), 1)
+    rest = jnp.concatenate([gram, jnp.zeros((vectors, lanes - vectors), jnp.float32)], axis=1)
+    rest = rest + (cols == rows + vectors).astype(jnp.float32)
+    for i in range(0, vectors, 2):
+        j = i + 1
+        left = jnp.broadcast_to(rest[:, i:j], rest.shape)
+        right = jnp.broadcast_to(rest[:, j : j + 1], rest.shape)
+        one, two = rest[i:j, :], rest[j : j + 1, :]
+        a, b, d = left[i:j, :], left[j : j + 1, :], right[j : j + 1, :]
+        scale = reciprocal(a * d - b * b)
+        update = left * ((d * one - b * two) * scale) + right * ((a * two - b * one) * scale)
+        rest = rest - jnp.where(rows > j, update, 0.0)
+    diagonal = jnp.sum(jnp.where(cols == rows, rest, 0.0), axis=1, keepdims=True)
+    odd = (rows & 1) == 1
+    corner = jnp.sum(jnp.where((cols == rows - 1) & odd, rest, 0.0), axis=1, keepdims=True)
+    before = pltpu.roll(rest, 1, 0)
+    lead = pltpu.roll(jnp.broadcast_to(diagonal, rest.shape), 1, 0)
+    ratio = jnp.where(odd, corner * reciprocal(lead), 0.0)
+    rest = (rest - ratio * before) * lax.rsqrt(diagonal - corner * ratio)
+    return jnp.where(cols >= rows, rest, 0.0)[:, :vectors], rest[:, vectors : 2 * vectors]
+
+
+def finish_kernel(gram_ref, *refs):
+    out_ref, upper_ref, held_ref, sems = refs[-4:]
+    vectors = out_ref.shape[0]
+    upper, inverse = factor(unpacked(gram_ref[...], vectors))
+    upper_ref[...] = upper
+    high, middle, low = pieces(inverse, 3)
+    none = jnp.zeros_like(high)
+    left = jnp.concatenate(
+        [
+            jnp.concatenate([high, high, high], axis=1),
+            jnp.concatenate([middle, middle, none], axis=1),
+            jnp.concatenate([low, none, none], axis=1),
+        ],
+        axis=0,
     )
-
-    @pl.when(step == pl.num_programs(0) - 1)
-    def _():
-        table = total_ref[...]
-
-        def block(a, b):
-            return table[a * vectors : (a + 1) * vectors, b * vectors : (b + 1) * vectors]
-
-        gram = block(0, 0) + (block(0, 1) + block(1, 0)) + (block(1, 1) + (block(0, 2) + block(2, 0)))
-        gram_ref[...] = packed(gram * share, vectors)
-
-
-def finish_kernel(gram_ref, filtered_ref, out_ref, upper_ref, inverse_ref):
-    vectors = filtered_ref.shape[0]
-
-    @pl.when(pl.program_id(0) == 0)
-    def _():
-        rows = lax.broadcasted_iota(jnp.int32, (vectors, vectors), 0)
-        cols = lax.broadcasted_iota(jnp.int32, (vectors, vectors), 1)
-        rest = unpacked(gram_ref[...], vectors)
-        inverse = (rows == cols).astype(jnp.float32)
-        factor = jnp.zeros_like(rest)
-        for k in range(vectors):
-            root = lax.rsqrt(rest[k : k + 1, k : k + 1])
-            top = rest[k : k + 1, :] * root
-            column = rest[:, k : k + 1] * root
-            below = jnp.where(rows[:, :1] > k, column, 0.0)
-            inverse_row = inverse[k : k + 1, :] * root
-            factor = jnp.where(rows == k, jnp.where(cols >= k, top, 0.0), factor)
-            inverse = jnp.where(rows == k, inverse_row, inverse - below * inverse_row)
-            rest = rest - below * top
-        upper_ref[...] = factor
-        inverse_ref[...] = inverse
-
-    left = pieces(inverse_ref[...], 3)
-    right = pieces(filtered_ref[...], 3)
-    order = ((0, 0), (0, 1), (1, 0), (1, 1), (0, 2), (2, 0))
-    out_ref[...] = jnp.dot(
-        jnp.concatenate([left[a] for a, _ in order], axis=1),
-        jnp.concatenate([right[b] for _, b in order], axis=0),
-        preferred_element_type=jnp.float32,
-    )
+    copies = []
+    place = 0
+    for ref in refs[:-4]:
+        for first in range(0, ref.shape[1], OUT_CHUNK):
+            count = min(OUT_CHUNK, ref.shape[1] - first)
+            right = jnp.concatenate(pieces(ref[:, first : first + count], 3), axis=0)
+            product = jnp.dot(left, right, preferred_element_type=jnp.float32)
+            held_ref[:, place : place + count] = product[:vectors] + (
+                product[vectors : 2 * vectors] + product[2 * vectors :]
+            )
+            cols = pl.ds(place, count)
+            copies.append(
+                pltpu.make_async_copy(held_ref.at[:, cols], out_ref.at[:, cols], sems.at[len(copies)])
+            )
+            copies[-1].start()
+            place += count
+    for copy in copies:
+        copy.wait()
 
 
 def local(previous, current, field_levels, bond_levels, lo_bits):
@@ -313,8 +386,6 @@
     scale = 4.0 / site_count
     whole = jax.ShapeDtypeStruct((vectors, amp_count), jnp.float32)
     size = vectors * amp_count
-    steps = 4
-    block = pl.BlockSpec((vectors, amp_count // steps), lambda i: (0, i))
     vmem = pl.BlockSpec(memory_space=pltpu.VMEM)
 
     def permute(values, pairs):
@@ -327,14 +398,14 @@
         return (scale * 0.5 * COUPLING_STEP) * bond_levels[bond].astype(jnp.float32)
 
     middles = tuple(range(3, global_bits - 1, 2))
-    first = permute(current, route(devices, 1, FIRST))
+    width = amp_count // 4
+    parts = [(0, 2), (2, 2)]
     swap = permute(current, flips(4))
-    boths = [permute(current, route(devices, m, BOTH)) for m in middles]
-    extra = []
-    if global_bits % 2 == 0:
-        top = global_bits - 1
-        moved = permute(current, flips(3 << top - 1, lambda i: (i >> top & 1) != (i >> top - 1 & 1)))
-        extra.append(strength(site_count - 2) * moved)
+    firsts, boths = [], []
+    for start, count in parts:
+        piece = cut(current, start * width, count * width)
+        firsts.append(permute(piece, route(devices, 1, FIRST)))
+        boths.append([permute(piece, route(devices, m, BOTH)) for m in middles])
 
     here = pl.pallas_call(
         functools.partial(local_kernel, global_bits=global_bits, scale=scale),
@@ -345,62 +416,87 @@
         cost_estimate=cost(6 * size * GROUP, 12 * size),
         name="local_bonds",
     )(place, field_levels, bond_levels, current, previous)
-    first, here = lax.optimization_barrier((first, here))
-
-    sent = pl.pallas_call(
-        functools.partial(sent_kernel, bit=rest_bits - 1, bond=local_bits - 1, scale=scale),
-        grid=(steps,),
-        out_shape=whole,
-        in_specs=[smem()] * 2 + [block] * 3,
-        out_specs=block,
-        compiler_params=params(),
-        cost_estimate=cost(6 * size, 16 * size),
-        name="sent_on",
-    )(place, bond_levels, current, swap, first)
-    second = permute(sent, route(devices, 1, SECOND))
-    ons = [permute(both, route(devices, m, ON)) for m, both in zip(middles, boths)]
-
-    for term in extra:
-        here = here + term
-    acc = pl.pallas_call(
-        functools.partial(gather_kernel, bit=rest_bits - 1, local_bits=local_bits, scale=scale),
-        grid=(steps,),
-        out_shape=whole,
-        in_specs=[smem()] * 2 + [block] * (2 + len(boths)),
-        out_specs=block,
-        compiler_params=params(),
-        cost_estimate=cost(6 * size, 16 * size),
-        name="gather_first",
-    )(place, bond_levels, here, first, *boths)
+    firsts[0], here = lax.optimization_barrier((firsts[0], here))
+    if global_bits % 2 == 0:
+        top = global_bits - 1
+        moved = permute(current, flips(3 << top - 1, lambda i: (i >> top & 1) != (i >> top - 1 & 1)))
+        here = here + strength(site_count - 2) * moved
+
+    seconds, ons, accs = [], [], []
+    for (start, count), first, both in zip(parts, firsts, boths):
+        shape = jax.ShapeDtypeStruct((vectors, count * width), jnp.float32)
+        part_size = vectors * count * width
+        if accs:
+            first, _ = lax.optimization_barrier((first, accs[-1]))
+        sent = pl.pallas_call(
+            functools.partial(
+                sent_kernel, start=start * width // LANES, bit=rest_bits - 1, bond=local_bits - 1, scale=scale
+            ),
+            out_shape=shape,
+            in_specs=[smem()] * 2 + [vmem] * 3,
+            out_specs=vmem,
+            compiler_params=params(),
+            cost_estimate=cost(0, 0),
+            name=f"sent_on_{start}",
+        )(place, bond_levels, current, swap, first)
+        seconds.append(permute(sent, route(devices, 1, SECOND)))
+        both, sent = lax.optimization_barrier((both, sent))
+        ons.append([permute(values, route(devices, m, ON)) for m, values in zip(middles, both)])
+        accs.append(
+            pl.pallas_call(
+                functools.partial(
+                    gather_kernel, start=start * width // LANES, bit=rest_bits - 1, local_bits=local_bits, scale=scale
+                ),
+                out_shape=shape,
+                in_specs=[smem()] * 2 + [vmem] * (2 + len(both)),
+                out_specs=vmem,
+                compiler_params=params(),
+                cost_estimate=cost(0, 0),
+                name=f"gather_first_{start}",
+            )(place, bond_levels, here, first, *both)
+        )
+
     fold = max(1, LANES // vectors)
     table = (vectors // fold, vectors * fold)
-    table_block = pl.BlockSpec(table, lambda i: (0, 0))
-    filtered, gram = pl.pallas_call(
-        functools.partial(filter_kernel, local_bits=local_bits, scale=scale, share=1.0 / (amp_count * devices)),
-        grid=(steps,),
-        out_shape=(whole, jax.ShapeDtypeStruct(table, jnp.float32)),
-        in_specs=[smem()] * 2 + [block] * (2 + len(ons)),
-        out_specs=(block, table_block),
-        scratch_shapes=[pltpu.VMEM((3 * vectors, 3 * vectors), jnp.float32)],
-        compiler_params=params(),
-        cost_estimate=cost(6 * size * vectors, 16 * size),
-        name="filter_gram",
-    )(place, bond_levels, acc, second, *ons)
-
-    for k in [lo_bits] + [k for k in range(global_bits) if k != lo_bits]:
-        gram = gram + permute(gram, flips(1 << k))
-
+    square = (3 * vectors, 3 * vectors)
+    filtered = []
+    products = jnp.zeros(square, jnp.float32)
+    for number, ((start, count), acc, second, on) in enumerate(zip(parts, accs, seconds, ons)):
+        last = number == len(parts) - 1
+        part_size = vectors * count * width
+        done, products = pl.pallas_call(
+            functools.partial(
+                filter_kernel, local_bits=local_bits, scale=scale, share=1.0 / (amp_count * devices), last=last
+            ),
+            out_shape=(
+                jax.ShapeDtypeStruct((vectors, count * width), jnp.float32),
+                jax.ShapeDtypeStruct(table if last else square, jnp.float32),
+            ),
+            in_specs=[smem()] * 2 + [vmem] * (3 + len(on)),
+            out_specs=(vmem, vmem),
+            compiler_params=params(),
+            cost_estimate=cost(6 * part_size * vectors, 16 * part_size),
+            name=f"filter_gram_{start}",
+        )(place, bond_levels, products, acc, second, *on)
+        filtered.append(done)
+    gram = products
+
+    hub = 1 << lo_bits
+    gram = gram + permute(gram, flips(hub))
+    for k in [k for k in range(global_bits) if k > lo_bits] + list(range(lo_bits)):
+        gram = gram + permute(gram, flips(1 << k | hub))
+
+    chunks = sum(-(-values.shape[1] // OUT_CHUNK) for values in filtered)
     return pl.pallas_call(
         finish_kernel,
-        grid=(steps,),
         out_shape=(whole, jax.ShapeDtypeStruct((vectors, vectors), jnp.float32)),
-        in_specs=[table_block, block],
-        out_specs=(block, pl.BlockSpec((vectors, vectors), lambda i: (0, 0))),
-        scratch_shapes=[pltpu.VMEM((vectors, vectors), jnp.float32)],
+        in_specs=[vmem] * (1 + len(filtered)),
+        out_specs=(pl.BlockSpec(memory_space=pltpu.HBM), vmem),
+        scratch_shapes=[pltpu.VMEM((vectors, amp_count), jnp.float32), pltpu.SemaphoreType.DMA((chunks,))],
         compiler_params=params(),
         cost_estimate=cost(12 * size * vectors, 8 * size),
         name="factor_apply",
-    )(gram, filtered)
+    )(gram, *filtered)
 
 
 def solution(mesh):

time: 87 us -> 74.4 us (0.86)
  waiting for transfers between devices: 47 us -> 33.7 us
  local copies, waits for them, and re-layouts: 4.24 us -> 1.61 us
  starting transfers between devices: 14.5 us -> 17.1 us
    ppermute x10 -> x14, waiting for transfers between devices: 47 us -> 33.7 us  [permute(): return lax.ppermute(values, AXES, pairs)]
    unnamed x16 -> x8, local copies, waits for them, and re-layouts: 4.24 us -> 1.61 us
    ppermute x10 -> x14, starting transfers between devices: 14.5 us -> 17.1 us  [permute(): return lax.ppermute(values, AXES, pairs)]
    pallas_call x3 -> x7, Pallas kernels: 12.2 us -> 14.7 us  [the longest x1 4.09 us: local(): pl.pallas_call(finish_kernel, out_shape=(whole, jax.ShapeDtypeStruct((vec...]
    pallas_call x1 -> x2, Pallas kernels: 4.24 us -> 2.61 us  [local(): pl.pallas_call(functools.partial(filter_kernel, local_bits=local_bits, sc...]
  transfers between devices with their start and end apart: 10 -> 14, of which waited for: 9 -> 12; matrix products, arithmetic and copies ran while one was open for 0% -> 0% of each run, Pallas kernels for 12% -> 21%
where the time goes in v3:
time: 74.4 us; the launch traced here: 74.2 us
  waiting for transfers between devices  33.7 us (45%)
  Pallas kernels  21 us (28%)
  starting transfers between devices  17.1 us (23%)
  local copies, waits for them, and re-layouts  1.61 us (2%)
    ppermute x14, waiting for transfers between devices, permute(): return lax.ppermute(values, AXES, pairs)  33.7 us
    ppermute x14, starting transfers between devices, permute(): return lax.ppermute(values, AXES, pairs)  17.1 us
    pallas_call x1, Pallas kernels, local(): pl.pallas_call(finish_kernel, out_shape=(whole, jax.ShapeDtypeStruct((vec...  4.09 us
    pallas_call x2, Pallas kernels, local(): pl.pallas_call(functools.partial(sent_kernel, start=start * width // LANE...  4.05 us
    pallas_call x2, Pallas kernels, cut(): pl.pallas_call(functools.partial(cut_kernel, start=start), out_shape=jax....  3.96 us
    pallas_call x1, Pallas kernels, local(): pl.pallas_call(functools.partial(local_kernel, global_bits=global_bits, s...  3.75 us
    pallas_call x2, Pallas kernels, local(): pl.pallas_call(functools.partial(filter_kernel, local_bits=local_bits, sc...  2.61 us
    pallas_call x2, Pallas kernels, local(): pl.pallas_call(functools.partial(gather_kernel, start=start * width // LA...  2.58 us
  transfers between devices with their start and end apart: 14, of which 12 were waited for; matrix products, arithmetic and copies ran while one was open for 0% of the time, Pallas kernels for 21%

profile of v3, /device:TPU:0, one launch (start us, length us, event | category | flops | bytes accessed | tf_op | source)
XLA Modules:
  0.0 74.2 jit_solution(5514786044942852917)
XLA Ops:
  1.1 2.0 %cut_0.1 = f32[32,8192]{1,0:T(8,128)} custom-call(f32[32,16384]{1,0:T(8,128)} %own_ref.3), custom_call_target="tpu_custom_call" | custom-call | bytes 2097152 | tf_op jit(solution)/shard_map/cut_0/pallas_call | solution.py:218
  3.2 3.0 %collective-permute-start.1 = (f32[32,8192]{1,0:T(8,128)}, f32[32,8192]{1,0:T(8,128)}, u32[]{:S(2)}, u32[]{:S(2)}) collective-permute-start(f32[32,8192]{1,0:T(8,128)} %cut_0.1), channel_id=1, source_target_pairs={{0,16},{1,17},{2,18},{3,19},{4,8},{5,9},{6,10},{7,11},{8,4},{9,5},... | collective-permute-start | bytes 3145736 | tf_op jit(solution)/shard_map/ppermute | solution.py:392
  6.2 2.0 %cut_8192.1 = f32[32,8192]{1,0:T(8,128)} custom-call(f32[32,16384]{1,0:T(8,128)} %own_ref.3), custom_call_target="tpu_custom_call" | custom-call | bytes 2097152 | tf_op jit(solution)/shard_map/cut_8192/pallas_call | solution.py:218
  8.3 1.5 %collective-permute-start.6 = (f32[32,8192]{1,0:T(8,128)}, f32[32,8192]{1,0:T(8,128)S(1)}, u32[]{:S(2)}, u32[]{:S(2)}) collective-permute-start(f32[32,8192]{1,0:T(8,128)} %cut_8192.1), channel_id=1, source_target_pairs={{0,16},{1,17},{2,18},{3,19},{4,8},{5,9},{6,10},{7,11},{8,4},{9,5},... | collective-permute-start | bytes 3145736 | tf_op jit(solution)/shard_map/ppermute | solution.py:392
  9.8 1.6 %copy-done = f32[32,16384]{1,0:T(8,128)S(1)} copy-done((f32[32,16384]{1,0:T(8,128)S(1)}, f32[32,16384]{1,0:T(8,128)}, u32[]{:S(2)}) %copy-start) | copy-done | bytes 2097176
  11.4 3.8 %local_bonds.1.local_ref = f32[32,16384]{1,0:T(8,128)S(1)} custom-call(s32[1]{0:T(128)} %bitcast.device_ref, s32[19]{0:T(128)S(1)} %copy-done.3, s32[18]{0:T(128)S(1)} %copy-done.2, f32[32,16384]{1,0:T(8,128)S(1)} %copy-done, f32[32,16384]{1,0:T(8,128)} %prev_ref.1), custom_call_target="tpu_custom_call" | custom-call | flops 805306368 | bytes 6291456 | tf_op jit(solution)/shard_map/local_bonds/pallas_call | solution.py:410
  15.2 3.7 %collective-permute-done.arrived_ref.first_ref = f32[32,8192]{1,0:T(8,128)} collective-permute-done((f32[32,8192]{1,0:T(8,128)}, f32[32,8192]{1,0:T(8,128)}, u32[]{:S(2)}, u32[]{:S(2)}) %collective-permute-start) | collective-permute-done | bytes 1048608 | tf_op jit(solution)/shard_map/ppermute | solution.py:392
  18.9 2.1 %sent_on_0.1 = f32[32,8192]{1,0:T(8,128)S(1)} custom-call(s32[1]{0:T(128)} %bitcast.device_ref, s32[18]{0:T(128)S(1)} %copy-done.2, f32[32,16384]{1,0:T(8,128)S(1)} %copy-done.1, f32[32,16384]{1,0:T(8,128)} %collective-permute-done.2.swap_ref, f32[32,8192]{1,0:T(8,128)} %collective-permute-done.arrived_ref.first_ref), custom_call_target="tpu_custom_call" | custom-call | tf_op jit(solution)/shard_map/sent_on_0/pallas_call | solution.py:431
  21.0 2.1 %collective-permute-start.3 = (f32[32,8192]{1,0:T(8,128)S(1)}, f32[32,8192]{1,0:T(8,128)S(1)}, u32[]{:S(2)}, u32[]{:S(2)}) collective-permute-start(f32[32,8192]{1,0:T(8,128)S(1)} %sent_on_0.1), channel_id=1, source_target_pairs={{0,1},{1,4},{2,5},{3,7},{4,0},{5,2},{6,3},{7,6},{8,9},{9,12},{10,1... | collective-permute-start | bytes 3145736 | tf_op jit(solution)/shard_map/ppermute | solution.py:392
  23.1 1.5 %collective-permute-start.4 = (f32[32,8192]{1,0:T(8,128)}, f32[32,8192]{1,0:T(8,128)S(1)}, u32[]{:S(2)}, u32[]{:S(2)}) collective-permute-start(f32[32,8192]{1,0:T(8,128)} %collective-permute-done.1.refs_0_), channel_id=1, source_target_pairs={{0,8},{1,9},{2,10},{3,11},{4,16},{5,17},{6,18},{7,19},{8,0},{9,1},... | collective-permute-start | bytes 3145736 | tf_op jit(solution)/shard_map/ppermute | solution.py:392
  24.6 1.8 %gather_first_0.1.acc_ref = f32[32,8192]{1,0:T(8,128)S(1)} custom-call(s32[1]{0:T(128)} %bitcast.device_ref, s32[18]{0:T(128)S(1)} %copy-done.2, f32[32,16384]{1,0:T(8,128)S(1)} %local_bonds.1.local_ref, f32[32,8192]{1,0:T(8,128)} %collective-permute-done.arrived_ref.first_ref, f32[32,8192]{1,0:T(8,128)} %collective-permute-done.1.refs_0_), custom_call_target="tpu_custom_call" | custom-call | tf_op jit(solution)/shard_map/gather_first_0/pallas_call | solution.py:446
  26.4 3.6 %collective-permute-done.5.arrived_ref.first_ref = f32[32,8192]{1,0:T(8,128)S(1)} collective-permute-done((f32[32,8192]{1,0:T(8,128)}, f32[32,8192]{1,0:T(8,128)S(1)}, u32[]{:S(2)}, u32[]{:S(2)}) %collective-permute-start.5) | collective-permute-done | bytes 1048608 | tf_op jit(solution)/shard_map/ppermute | solution.py:392
  30.0 1.9 %sent_on_2.1 = f32[32,8192]{1,0:T(8,128)S(1)} custom-call(s32[1]{0:T(128)} %bitcast.device_ref, s32[18]{0:T(128)S(1)} %copy-done.2, f32[32,16384]{1,0:T(8,128)S(1)} %copy-done.1, f32[32,16384]{1,0:T(8,128)} %collective-permute-done.2.swap_ref, f32[32,8192]{1,0:T(8,128)S(1)} %collective-permute-done.5.arrived_ref.first_ref), custom_call_target="tpu_custom_call" | custom-call | tf_op jit(solution)/shard_map/sent_on_2/pallas_call | solution.py:431
  31.9 2.1 %collective-permute-start.7 = (f32[32,8192]{1,0:T(8,128)S(1)}, f32[32,8192]{1,0:T(8,128)S(1)}, u32[]{:S(2)}, u32[]{:S(2)}) collective-permute-start(f32[32,8192]{1,0:T(8,128)S(1)} %sent_on_2.1), channel_id=1, source_target_pairs={{0,1},{1,4},{2,5},{3,7},{4,0},{5,2},{6,3},{7,6},{8,9},{9,12},{10,1... | collective-permute-start | bytes 3145736 | tf_op jit(solution)/shard_map/ppermute | solution.py:392
  34.0 0.7 collective-permute-done.6.refs_0_
  34.6 0.8 %collective-permute-start.8 = (f32[32,8192]{1,0:T(8,128)S(1)}, f32[32,8192]{1,0:T(8,128)S(1)}, u32[]{:S(2)}, u32[]{:S(2)}) collective-permute-start(f32[32,8192]{1,0:T(8,128)S(1)} %collective-permute-done.6.refs_0_), channel_id=1, source_target_pairs={{0,8},{1,9},{2,10},{3,11},{4,16},{5,17},{6,18},{7,19},{8,0},{9,1},... | collective-permute-start | bytes 3145736 | tf_op jit(solution)/shard_map/ppermute | solution.py:392
  35.5 0.8 %gather_first_2.1.acc_ref = f32[32,8192]{1,0:T(8,128)S(1)} custom-call(s32[1]{0:T(128)} %bitcast.device_ref, s32[18]{0:T(128)S(1)} %copy-done.2, f32[32,16384]{1,0:T(8,128)S(1)} %local_bonds.1.local_ref, f32[32,8192]{1,0:T(8,128)S(1)} %collective-permute-done.5.arrived_ref.first_ref, f32[32,8192]{1,0:T(8,128)S(1)} %collective-permute-done.6.refs_0_), custom_call_target="tpu_custom_call" | custom-call | tf_op jit(solution)/shard_map/gather_first_2/pallas_call | solution.py:446
  36.2 4.1 %collective-permute-done.3.second_ref = f32[32,8192]{1,0:T(8,128)S(1)} collective-permute-done((f32[32,8192]{1,0:T(8,128)S(1)}, f32[32,8192]{1,0:T(8,128)S(1)}, u32[]{:S(2)}, u32[]{:S(2)}) %collective-permute-start.3) | collective-permute-done | bytes 1048608 | tf_op jit(solution)/shard_map/ppermute | solution.py:392
  40.3 2.8 %collective-permute-done.4.refs_0_ = f32[32,8192]{1,0:T(8,128)S(1)} collective-permute-done((f32[32,8192]{1,0:T(8,128)}, f32[32,8192]{1,0:T(8,128)S(1)}, u32[]{:S(2)}, u32[]{:S(2)}) %collective-permute-start.4) | collective-permute-done | bytes 1048608 | tf_op jit(solution)/shard_map/ppermute | solution.py:392
  43.1 1.2 %filter_gram_0.1 = (f32[32,8192]{1,0:T(8,128)S(1)}, f32[96,96]{1,0:T(8,128)S(1)}) custom-call(s32[1]{0:T(128)} %bitcast.device_ref, s32[18]{0:T(128)S(1)} %copy-done.2, f32[96,96]{1,0:T(8,128)S(1)} %broadcast_in_dim.3.before_ref, f32[32,8192]{1,0:T(8,128)S(1)} %gather_first_0.1.acc_ref, f32[32,8192]{1,0:T(8,128)S(1)} %collective-permute-done.3.second_ref, ...), custom_call_target="tpu_custom_call" | custom-call | flops 50331648 | bytes 4194304 | tf_op jit(solution)/shard_map/filter_gram_0/pallas_call | solution.py:467
  44.2 7.3 %collective-permute-done.7.second_ref = f32[32,8192]{1,0:T(8,128)S(1)} collective-permute-done((f32[32,8192]{1,0:T(8,128)S(1)}, f32[32,8192]{1,0:T(8,128)S(1)}, u32[]{:S(2)}, u32[]{:S(2)}) %collective-permute-start.7) | collective-permute-done | bytes 1048608 | tf_op jit(solution)/shard_map/ppermute | solution.py:392
  51.5 2.8 %collective-permute-done.8.refs_0_ = f32[32,8192]{1,0:T(8,128)S(1)} collective-permute-done((f32[32,8192]{1,0:T(8,128)S(1)}, f32[32,8192]{1,0:T(8,128)S(1)}, u32[]{:S(2)}, u32[]{:S(2)}) %collective-permute-start.8) | collective-permute-done | bytes 1048608 | tf_op jit(solution)/shard_map/ppermute | solution.py:392
  54.3 1.4 %filter_gram_2.1 = (f32[32,8192]{1,0:T(8,128)S(1)}, f32[8,128]{1,0:T(8,128)S(1)}) custom-call(s32[1]{0:T(128)} %bitcast.device_ref, s32[18]{0:T(128)S(1)} %copy-done.2, f32[96,96]{1,0:T(8,128)S(1)} %get-tuple-element.14.before_ref, f32[32,8192]{1,0:T(8,128)S(1)} %gather_first_2.1.acc_ref, f32[32,8192]{1,0:T(8,128)S(1)} %collective-permute-done.7.second_ref, ...), custom_call_target="tpu_custom_call" | custom-call | flops 50331648 | bytes 4194304 | tf_op jit(solution)/shard_map/filter_gram_2/pallas_call | solution.py:467
  55.8 1.2 %collective-permute-done.9 = f32[8,128]{1,0:T(8,128)S(1)} collective-permute-done((f32[8,128]{1,0:T(8,128)S(1)}, f32[8,128]{1,0:T(8,128)S(1)}, u32[]{:S(2)}, u32[]{:S(2)}) %collective-permute-start.9) | collective-permute-done | bytes 4128 | tf_op jit(solution)/shard_map/ppermute | solution.py:392
  57.3 2.7 %collective-permute-done.10 = f32[8,128]{1,0:T(8,128)S(1)} collective-permute-done((f32[8,128]{1,0:T(8,128)S(1)}, f32[8,128]{1,0:T(8,128)S(1)}, u32[]{:S(2)}, u32[]{:S(2)}) %collective-permute-start.10) | collective-permute-done | bytes 4128 | tf_op jit(solution)/shard_map/ppermute | solution.py:392
  60.0 1.0 %collective-permute-start.11 = (f32[8,128]{1,0:T(8,128)S(1)}, f32[8,128]{1,0:T(8,128)S(1)}, u32[]{:S(2)}, u32[]{:S(2)}) collective-permute-start(f32[8,128]{1,0:T(8,128)S(1)} %add.20), channel_id=1, source_target_pairs={{0,20},{1,21},{2,22},{3,23},{4,16},{5,17},{6,18},{7,19},{8,28},{9,... | collective-permute-start | bytes 12296 | tf_op jit(solution)/shard_map/ppermute | solution.py:392
  60.9 2.1 %collective-permute-done.11 = f32[8,128]{1,0:T(8,128)S(1)} collective-permute-done((f32[8,128]{1,0:T(8,128)S(1)}, f32[8,128]{1,0:T(8,128)S(1)}, u32[]{:S(2)}, u32[]{:S(2)}) %collective-permute-start.11) | collective-permute-done | bytes 4128 | tf_op jit(solution)/shard_map/ppermute | solution.py:392
  63.0 1.8 %collective-permute-start.12 = (f32[8,128]{1,0:T(8,128)S(1)}, f32[8,128]{1,0:T(8,128)S(1)}, u32[]{:S(2)}, u32[]{:S(2)}) collective-permute-start(f32[8,128]{1,0:T(8,128)S(1)} %add.21), channel_id=1, source_target_pairs={{0,5},{1,4},{2,7},{3,6},{4,1},{5,0},{6,3},{7,2},{8,13},{9,12},{10,... | collective-permute-start | bytes 12296 | tf_op jit(solution)/shard_map/ppermute | solution.py:392
  64.8 1.3 %collective-permute-done.12 = f32[8,128]{1,0:T(8,128)S(1)} collective-permute-done((f32[8,128]{1,0:T(8,128)S(1)}, f32[8,128]{1,0:T(8,128)S(1)}, u32[]{:S(2)}, u32[]{:S(2)}) %collective-permute-start.12) | collective-permute-done | bytes 4128 | tf_op jit(solution)/shard_map/ppermute | solution.py:392
  66.2 2.2 %collective-permute-start.13 = (f32[8,128]{1,0:T(8,128)S(1)}, f32[8,128]{1,0:T(8,128)S(1)}, u32[]{:S(2)}, u32[]{:S(2)}) collective-permute-start(f32[8,128]{1,0:T(8,128)S(1)} %add.22), channel_id=1, source_target_pairs={{0,6},{1,7},{2,4},{3,5},{4,2},{5,3},{6,0},{7,1},{8,14},{9,15},{10,... | collective-permute-start | bytes 12296 | tf_op jit(solution)/shard_map/ppermute | solution.py:392
  68.4 1.7 %collective-permute-done.13 = f32[8,128]{1,0:T(8,128)S(1)} collective-permute-done((f32[8,128]{1,0:T(8,128)S(1)}, f32[8,128]{1,0:T(8,128)S(1)}, u32[]{:S(2)}, u32[]{:S(2)}) %collective-permute-start.13) | collective-permute-done | bytes 4128 | tf_op jit(solution)/shard_map/ppermute | solution.py:392
  70.1 4.1 %factor_apply.1 = (f32[32,16384]{1,0:T(8,128)}, f32[32,32]{1,0:T(8,128)}) custom-call(f32[8,128]{1,0:T(8,128)S(1)} %add.23.gram_ref, f32[32,8192]{1,0:T(8,128)S(1)} %get-tuple-element.18.refs_0_, f32[32,8192]{1,0:T(8,128)S(1)} %get-tuple-element.19.refs_1_), custom_call_target="tpu_custom_call" | custom-call | flops 201326592 | bytes 4194304 | tf_op jit(solution)/shard_map/factor_apply/pallas_call | solution.py:490
  (20 shorter events, 1.1 us)
Async XLA Ops:
  0.6 18.2 %collective-permute-start.2 = (f32[32,16384]{1,0:T(8,128)}, f32[32,16384]{1,0:T(8,128)}, u32[]{:S(2)}, u32[]{:S(2)}) collective-permute-start(f32[32,16384]{1,0:T(8,128)} %own_ref.3), channel_id=1, source_target_pairs={{0,4},{1,5},{2,6},{3,7},{4,0},{5,1},{6,2},{7,3},{8,12},{9,13},{10,... | collective-permute-start | bytes 6291464 | tf_op jit(solution)/shard_map/ppermute | solution.py:392
  3.1 6.7 %copy-start.2 = (s32[18]{0:T(128)S(1)}, s32[18]{0:T(128)}, u32[]{:S(2)}) copy-start(s32[18]{0:T(128)} %bond_ref.13) | copy-start | bytes 220
  3.1 6.7 %copy-start.3 = (s32[19]{0:T(128)S(1)}, s32[19]{0:T(128)}, u32[]{:S(2)}) copy-start(s32[19]{0:T(128)} %field_ref.1) | copy-start | bytes 232
  3.2 15.7 %collective-permute-start = (f32[32,8192]{1,0:T(8,128)}, f32[32,8192]{1,0:T(8,128)}, u32[]{:S(2)}, u32[]{:S(2)}) collective-permute-start(f32[32,8192]{1,0:T(8,128)} %cut_0.1), channel_id=1, source_target_pairs={{0,4},{1,0},{2,1},{3,2},{4,5},{5,6},{6,7},{7,3},{8,12},{9,8},{10,9... | collective-permute-start | bytes 3145736 | tf_op jit(solution)/shard_map/ppermute | solution.py:392
  3.2 19.9 %collective-permute-start.1 = (f32[32,8192]{1,0:T(8,128)}, f32[32,8192]{1,0:T(8,128)}, u32[]{:S(2)}, u32[]{:S(2)}) collective-permute-start(f32[32,8192]{1,0:T(8,128)} %cut_0.1), channel_id=1, source_target_pairs={{0,16},{1,17},{2,18},{3,19},{4,8},{5,9},{6,10},{7,11},{8,4},{9,5},... | collective-permute-start | bytes 3145736 | tf_op jit(solution)/shard_map/ppermute | solution.py:392
  8.2 21.8 %collective-permute-start.5 = (f32[32,8192]{1,0:T(8,128)}, f32[32,8192]{1,0:T(8,128)S(1)}, u32[]{:S(2)}, u32[]{:S(2)}) collective-permute-start(f32[32,8192]{1,0:T(8,128)} %cut_8192.1), channel_id=1, source_target_pairs={{0,4},{1,0},{2,1},{3,2},{4,5},{5,6},{6,7},{7,3},{8,12},{9,8},{10,9... | collective-permute-start | bytes 3145736 | tf_op jit(solution)/shard_map/ppermute | solution.py:392
  8.3 26.3 %collective-permute-start.6 = (f32[32,8192]{1,0:T(8,128)}, f32[32,8192]{1,0:T(8,128)S(1)}, u32[]{:S(2)}, u32[]{:S(2)}) collective-permute-start(f32[32,8192]{1,0:T(8,128)} %cut_8192.1), channel_id=1, source_target_pairs={{0,16},{1,17},{2,18},{3,19},{4,8},{5,9},{6,10},{7,11},{8,4},{9,5},... | collective-permute-start | bytes 3145736 | tf_op jit(solution)/shard_map/ppermute | solution.py:392
  9.8 1.6 %copy-start = (f32[32,16384]{1,0:T(8,128)S(1)}, f32[32,16384]{1,0:T(8,128)}, u32[]{:S(2)}) copy-start(f32[32,16384]{1,0:T(8,128)} %own_ref.3) | copy-start | bytes 6291460
  11.4 7.5 %copy-start.1 = (f32[32,16384]{1,0:T(8,128)S(1)}, f32[32,16384]{1,0:T(8,128)}, u32[]{:S(2)}) copy-start(f32[32,16384]{1,0:T(8,128)} %own_ref.3) | copy-start | bytes 6291460
  21.0 19.3 %collective-permute-start.3 = (f32[32,8192]{1,0:T(8,128)S(1)}, f32[32,8192]{1,0:T(8,128)S(1)}, u32[]{:S(2)}, u32[]{:S(2)}) collective-permute-start(f32[32,8192]{1,0:T(8,128)S(1)} %sent_on_0.1), channel_id=1, source_target_pairs={{0,1},{1,4},{2,5},{3,7},{4,0},{5,2},{6,3},{7,6},{8,9},{9,12},{10,1... | collective-permute-start | bytes 3145736 | tf_op jit(solution)/shard_map/ppermute | solution.py:392
  23.1 20.0 %collective-permute-start.4 = (f32[32,8192]{1,0:T(8,128)}, f32[32,8192]{1,0:T(8,128)S(1)}, u32[]{:S(2)}, u32[]{:S(2)}) collective-permute-start(f32[32,8192]{1,0:T(8,128)} %collective-permute-done.1.refs_0_), channel_id=1, source_target_pairs={{0,8},{1,9},{2,10},{3,11},{4,16},{5,17},{6,18},{7,19},{8,0},{9,1},... | collective-permute-start | bytes 3145736 | tf_op jit(solution)/shard_map/ppermute | solution.py:392
  31.9 19.6 %collective-permute-start.7 = (f32[32,8192]{1,0:T(8,128)S(1)}, f32[32,8192]{1,0:T(8,128)S(1)}, u32[]{:S(2)}, u32[]{:S(2)}) collective-permute-start(f32[32,8192]{1,0:T(8,128)S(1)} %sent_on_2.1), channel_id=1, source_target_pairs={{0,1},{1,4},{2,5},{3,7},{4,0},{5,2},{6,3},{7,6},{8,9},{9,12},{10,1... | collective-permute-start | bytes 3145736 | tf_op jit(solution)/shard_map/ppermute | solution.py:392
  34.6 19.7 %collective-permute-start.8 = (f32[32,8192]{1,0:T(8,128)S(1)}, f32[32,8192]{1,0:T(8,128)S(1)}, u32[]{:S(2)}, u32[]{:S(2)}) collective-permute-start(f32[32,8192]{1,0:T(8,128)S(1)} %collective-permute-done.6.refs_0_), channel_id=1, source_target_pairs={{0,8},{1,9},{2,10},{3,11},{4,16},{5,17},{6,18},{7,19},{8,0},{9,1},... | collective-permute-start | bytes 3145736 | tf_op jit(solution)/shard_map/ppermute | solution.py:392
  55.7 1.2 %collective-permute-start.9 = (f32[8,128]{1,0:T(8,128)S(1)}, f32[8,128]{1,0:T(8,128)S(1)}, u32[]{:S(2)}, u32[]{:S(2)}) collective-permute-start(f32[8,128]{1,0:T(8,128)S(1)} %get-tuple-element.17), channel_id=1, source_target_pairs={{0,4},{1,5},{2,6},{3,7},{4,0},{5,1},{6,2},{7,3},{8,12},{9,13},{10,... | collective-permute-start | bytes 12296 | tf_op jit(solution)/shard_map/ppermute | solution.py:392
  56.9 3.0 %collective-permute-start.10 = (f32[8,128]{1,0:T(8,128)S(1)}, f32[8,128]{1,0:T(8,128)S(1)}, u32[]{:S(2)}, u32[]{:S(2)}) collective-permute-start(f32[8,128]{1,0:T(8,128)S(1)} %add.19), channel_id=1, source_target_pairs={{0,12},{1,13},{2,14},{3,15},{4,8},{5,9},{6,10},{7,11},{8,4},{9,5},... | collective-permute-start | bytes 12296 | tf_op jit(solution)/shard_map/ppermute | solution.py:392
  60.0 3.0 %collective-permute-start.11 = (f32[8,128]{1,0:T(8,128)S(1)}, f32[8,128]{1,0:T(8,128)S(1)}, u32[]{:S(2)}, u32[]{:S(2)}) collective-permute-start(f32[8,128]{1,0:T(8,128)S(1)} %add.20), channel_id=1, source_target_pairs={{0,20},{1,21},{2,22},{3,23},{4,16},{5,17},{6,18},{7,19},{8,28},{9,... | collective-permute-start | bytes 12296 | tf_op jit(solution)/shard_map/ppermute | solution.py:392
  63.0 3.2 %collective-permute-start.12 = (f32[8,128]{1,0:T(8,128)S(1)}, f32[8,128]{1,0:T(8,128)S(1)}, u32[]{:S(2)}, u32[]{:S(2)}) collective-permute-start(f32[8,128]{1,0:T(8,128)S(1)} %add.21), channel_id=1, source_target_pairs={{0,5},{1,4},{2,7},{3,6},{4,1},{5,0},{6,3},{7,2},{8,13},{9,12},{10,... | collective-permute-start | bytes 12296 | tf_op jit(solution)/shard_map/ppermute | solution.py:392
  66.2 3.9 %collective-permute-start.13 = (f32[8,128]{1,0:T(8,128)S(1)}, f32[8,128]{1,0:T(8,128)S(1)}, u32[]{:S(2)}, u32[]{:S(2)}) collective-permute-start(f32[8,128]{1,0:T(8,128)S(1)} %add.22), channel_id=1, source_target_pairs={{0,6},{1,7},{2,4},{3,5},{4,2},{5,3},{6,0},{7,1},{8,14},{9,15},{10,... | collective-permute-start | bytes 12296 | tf_op jit(solution)/shard_map/ppermute | solution.py:392

commit v4 on v3

--- a/solution.py
+++ b/solution.py
@@ -16,8 +16,10 @@
 GROUP = 256
 CHUNK = 1024
 OUT_CHUNK = 2048
+PANEL = 16
 GROUP_BITS = 8
 VMEM_LIMIT = 48 * 1024 * 1024
+CUT_LIMIT = 56 * 1024 * 1024
 
 
 def pieces(values, count):
@@ -192,60 +194,54 @@
         out_ref[:, t * LANES : (t + 1) * LANES] = total
 
 
-def cut_kernel(x_ref, out_ref, held_ref, in_sems, out_sems, *, start):
-    rows, width = held_ref.shape
-    strips = [pl.ds(k * SUBLANES, SUBLANES) for k in range(rows // SUBLANES)]
-    loads = [
-        pltpu.make_async_copy(x_ref.at[strip, pl.ds(start, width)], held_ref.at[strip], in_sems.at[k])
-        for k, strip in enumerate(strips)
-    ]
-    stores = [
-        pltpu.make_async_copy(held_ref.at[strip], out_ref.at[strip], out_sems.at[k]) for k, strip in enumerate(strips)
-    ]
-    for load in loads:
-        load.start()
-    for load, store in zip(loads, stores):
-        load.wait()
-        store.start()
-    for store in stores:
-        store.wait()
+def cut_kernel(x_ref, out_ref, sems, *, start):
+    rows, width = out_ref.shape
+    copies = []
+    for k in range(rows // SUBLANES):
+        strip = pl.ds(k * SUBLANES, SUBLANES)
+        copies.append(
+            pltpu.make_async_copy(x_ref.at[strip, pl.ds(start, width)], out_ref.at[strip], sems.at[k])
+        )
+        copies[-1].start()
+    for copy in copies:
+        copy.wait()
 
 
 def cut(values, start, width):
     rows = values.shape[0]
-    hbm = pl.BlockSpec(memory_space=pltpu.HBM)
-    strips = rows // SUBLANES
     return pl.pallas_call(
         functools.partial(cut_kernel, start=start),
         out_shape=jax.ShapeDtypeStruct((rows, width), values.dtype),
-        in_specs=[hbm],
-        out_specs=hbm,
-        scratch_shapes=[
-            pltpu.VMEM((rows, width), values.dtype),
-            pltpu.SemaphoreType.DMA((strips,)),
-            pltpu.SemaphoreType.DMA((strips,)),
-        ],
-        compiler_params=params(63 * 1024 * 1024),
+        in_specs=[pl.BlockSpec(memory_space=pltpu.HBM)],
+        out_specs=pl.BlockSpec(memory_space=pltpu.VMEM),
+        scratch_shapes=[pltpu.SemaphoreType.DMA((rows // SUBLANES,))],
+        compiler_params=params(CUT_LIMIT),
         cost_estimate=cost(0, 8 * rows * width),
         name=f"cut_{start}",
     )(values)
 
 
-def sent_kernel(device_ref, bond_ref, own_ref, swap_ref, arrived_ref, out_ref, *, start, bit, bond, scale):
+def ready_kernel(device_ref, bond_ref, own_ref, swap_ref, *out_refs, bit, bond, scale):
     p, m, q = (bit_of(device_ref, k) for k in range(3))
-    joint, low, high = (strength_of(bond_ref, bond + k, scale) for k in range(3))
-    at_sum = (p != m) & (q != m)
+    joint, low = (strength_of(bond_ref, bond + k, scale) for k in range(2))
+    low = jnp.where((p != m) & (q != m), low, 0.0)
     passing = (p != m) & (q == m)
     corner = (p == m) & (q == m)
-    low = jnp.where(at_sum, low, 0.0)
-    high = jnp.where(p != m, high, 0.0)
     swap_pair = [jnp.where(passing & (p == side), joint, 0.0) for side in (0, 1)]
     own_pair = [jnp.where(corner & (p == side), joint, 0.0) for side in (0, 1)]
-    for t in range(out_ref.shape[1] // LANES):
-        total = low * tile_of(swap_ref, start + t) + high * tile_of(arrived_ref, t)
-        total = total + sided(swap_pair, t, bit) * across(swap_ref, start + t, bit)
-        total = total + sided(own_pair, t, bit) * across(own_ref, start + t, bit)
-        out_ref[:, t * LANES : (t + 1) * LANES] = total
+    t = 0
+    for out_ref in out_refs:
+        for place in range(out_ref.shape[1] // LANES):
+            total = low * tile_of(swap_ref, t) + sided(swap_pair, t, bit) * across(swap_ref, t, bit)
+            total = total + sided(own_pair, t, bit) * across(own_ref, t, bit)
+            out_ref[:, place * LANES : (place + 1) * LANES] = total
+            t += 1
+
+
+def sent_kernel(device_ref, bond_ref, ready_ref, arrived_ref, out_ref, *, bond, scale):
+    high = strength_of(bond_ref, bond + 2, scale)
+    high = jnp.where(bit_of(device_ref, 0) != bit_of(device_ref, 1), high, 0.0)
+    out_ref[...] = ready_ref[...] + high * arrived_ref[...]
 
 
 def gather_kernel(device_ref, bond_ref, local_ref, first_ref, *refs, start, bit, local_bits, scale):
@@ -309,7 +305,6 @@
 
 def reciprocal(values):
     guess = pl.reciprocal(values, approx=True)
-    guess = guess * (2.0 - values * guess)
     return guess * (2.0 - values * guess)
 
 
@@ -320,15 +315,22 @@
     cols = lax.broadcasted_iota(jnp.int32, (vectors, lanes), 1)
     rest = jnp.concatenate([gram, jnp.zeros((vectors, lanes - vectors), jnp.float32)], axis=1)
     rest = rest + (cols == rows + vectors).astype(jnp.float32)
-    for i in range(0, vectors, 2):
-        j = i + 1
-        left = jnp.broadcast_to(rest[:, i:j], rest.shape)
-        right = jnp.broadcast_to(rest[:, j : j + 1], rest.shape)
-        one, two = rest[i:j, :], rest[j : j + 1, :]
-        a, b, d = left[i:j, :], left[j : j + 1, :], right[j : j + 1, :]
-        scale = reciprocal(a * d - b * b)
-        update = left * ((d * one - b * two) * scale) + right * ((a * two - b * one) * scale)
-        rest = rest - jnp.where(rows > j, update, 0.0)
+    for panel in range(0, vectors, PANEL):
+        columns = [jnp.broadcast_to(rest[:, k : k + 1], rest.shape) for k in range(panel, min(panel + PANEL, vectors))]
+        for k in range(0, len(columns), 2):
+            i, j = panel + k, panel + k + 1
+            left, right = columns[k : k + 2]
+            a, b, d = left[i:j, :], left[j : j + 1, :], right[j : j + 1, :]
+            scale = reciprocal(a * d - b * b)
+            left = jnp.where(rows > j, left, 0.0)
+            right = jnp.where(rows > j, right, 0.0)
+
+            def eliminate(values):
+                one, two = values[i:j, :], values[j : j + 1, :]
+                return values - (left * ((d * one - b * two) * scale) + right * ((a * two - b * one) * scale))
+
+            columns[k + 2 :] = [eliminate(values) for values in columns[k + 2 :]]
+            rest = eliminate(rest)
     diagonal = jnp.sum(jnp.where(cols == rows, rest, 0.0), axis=1, keepdims=True)
     odd = (rows & 1) == 1
     corner = jnp.sum(jnp.where((cols == rows - 1) & odd, rest, 0.0), axis=1, keepdims=True)
@@ -348,9 +350,8 @@
     none = jnp.zeros_like(high)
     left = jnp.concatenate(
         [
-            jnp.concatenate([high, high, high], axis=1),
-            jnp.concatenate([middle, middle, none], axis=1),
-            jnp.concatenate([low, none, none], axis=1),
+            jnp.concatenate([high, high, high, low], axis=1),
+            jnp.concatenate([middle, middle, none, none], axis=1),
         ],
         axis=0,
     )
@@ -359,11 +360,9 @@
     for ref in refs[:-4]:
         for first in range(0, ref.shape[1], OUT_CHUNK):
             count = min(OUT_CHUNK, ref.shape[1] - first)
-            right = jnp.concatenate(pieces(ref[:, first : first + count], 3), axis=0)
-            product = jnp.dot(left, right, preferred_element_type=jnp.float32)
-            held_ref[:, place : place + count] = product[:vectors] + (
-                product[vectors : 2 * vectors] + product[2 * vectors :]
-            )
+            right = pieces(ref[:, first : first + count], 3)
+            product = jnp.dot(left, jnp.concatenate(right + right[:1], axis=0), preferred_element_type=jnp.float32)
+            held_ref[:, place : place + count] = product[:vectors] + product[vectors:]
             cols = pl.ds(place, count)
             copies.append(
                 pltpu.make_async_copy(held_ref.at[:, cols], out_ref.at[:, cols], sems.at[len(copies)])
@@ -398,14 +397,16 @@
         return (scale * 0.5 * COUPLING_STEP) * bond_levels[bond].astype(jnp.float32)
 
     middles = tuple(range(3, global_bits - 1, 2))
-    width = amp_count // 4
-    parts = [(0, 2), (2, 2)]
+    width = amp_count // 32
+    parts = [(0, 20), (20, 12)]
     swap = permute(current, flips(4))
     firsts, boths = [], []
     for start, count in parts:
         piece = cut(current, start * width, count * width)
         firsts.append(permute(piece, route(devices, 1, FIRST)))
         boths.append([permute(piece, route(devices, m, BOTH)) for m in middles])
+
+    current, _ = lax.optimization_barrier((current, piece))
 
     here = pl.pallas_call(
         functools.partial(local_kernel, global_bits=global_bits, scale=scale),
@@ -416,32 +417,42 @@
         cost_estimate=cost(6 * size * GROUP, 12 * size),
         name="local_bonds",
     )(place, field_levels, bond_levels, current, previous)
-    firsts[0], here = lax.optimization_barrier((firsts[0], here))
+    ready = pl.pallas_call(
+        functools.partial(ready_kernel, bit=rest_bits - 1, bond=local_bits - 1, scale=scale),
+        out_shape=tuple(jax.ShapeDtypeStruct((vectors, count * width), jnp.float32) for _, count in parts),
+        in_specs=[smem()] * 2 + [vmem] * 2,
+        out_specs=tuple(vmem for _ in parts),
+        compiler_params=params(),
+        cost_estimate=cost(6 * size, 12 * size),
+        name="ready",
+    )(place, bond_levels, current, swap)
+    firsts[0], here, ready = lax.optimization_barrier((firsts[0], here, ready))
     if global_bits % 2 == 0:
         top = global_bits - 1
         moved = permute(current, flips(3 << top - 1, lambda i: (i >> top & 1) != (i >> top - 1 & 1)))
         here = here + strength(site_count - 2) * moved
 
-    seconds, ons, accs = [], [], []
-    for (start, count), first, both in zip(parts, firsts, boths):
+    seconds, ons, accs, sents = [], [], [], []
+    for (start, count), first, both, base in zip(parts, firsts, boths, ready):
         shape = jax.ShapeDtypeStruct((vectors, count * width), jnp.float32)
         part_size = vectors * count * width
-        if accs:
-            first, _ = lax.optimization_barrier((first, accs[-1]))
         sent = pl.pallas_call(
-            functools.partial(
-                sent_kernel, start=start * width // LANES, bit=rest_bits - 1, bond=local_bits - 1, scale=scale
-            ),
+            functools.partial(sent_kernel, bond=local_bits - 1, scale=scale),
             out_shape=shape,
-            in_specs=[smem()] * 2 + [vmem] * 3,
+            in_specs=[smem()] * 2 + [vmem] * 2,
             out_specs=vmem,
             compiler_params=params(),
             cost_estimate=cost(0, 0),
             name=f"sent_on_{start}",
-        )(place, bond_levels, current, swap, first)
+        )(place, bond_levels, base, first)
         seconds.append(permute(sent, route(devices, 1, SECOND)))
+        sents.append(sent)
         both, sent = lax.optimization_barrier((both, sent))
         ons.append([permute(values, route(devices, m, ON)) for m, values in zip(middles, both)])
+    firsts, sents = lax.optimization_barrier((firsts, sents))
+    for (start, count), first, both in zip(parts, firsts, boths):
+        shape = jax.ShapeDtypeStruct((vectors, count * width), jnp.float32)
+        part_size = vectors * count * width
         accs.append(
             pl.pallas_call(
                 functools.partial(

time: 74.4 us -> 73.6 us (0.989)
  local copies, waits for them, and re-layouts: 1.61 us -> 0.02 us
    unnamed x8 -> x6, local copies, waits for them, and re-layouts: 1.61 us -> 0.02 us
    pallas_call x1, Pallas kernels: 4.09 us -> 3 us  [local(): pl.pallas_call(finish_kernel, out_shape=(whole, jax.ShapeDtypeStruct((vec...]
    pallas_call x2 -> x3, Pallas kernels: 4.05 us -> 3.96 us  [the longest x1 2.03 us: local(): pl.pallas_call(functools.partial(ready_kernel, bit=rest_bits - 1, bond=lo...]
  transfers between devices with their start and end apart: 14 -> 14, of which waited for: 12 -> 11; matrix products, arithmetic and copies ran while one was open for 0% -> 0% of each run, Pallas kernels for 21% -> 23%
where the time goes in v4:
time: 73.6 us; the launch traced here: 73.2 us
  waiting for transfers between devices  34.2 us (46%)
  Pallas kernels  21 us (29%)
  starting transfers between devices  17.3 us (24%)
  between operations  0.74 us (1%)
    ppermute x14, waiting for transfers between devices, permute(): return lax.ppermute(values, AXES, pairs)  34.2 us
    ppermute x14, starting transfers between devices, permute(): return lax.ppermute(values, AXES, pairs)  17.3 us
    pallas_call x2, Pallas kernels, cut(): pl.pallas_call(functools.partial(cut_kernel, start=start), out_shape=jax....  4.5 us
    pallas_call x1, Pallas kernels, local(): pl.pallas_call(functools.partial(local_kernel, global_bits=global_bits, s...  3.6 us
    pallas_call x2, Pallas kernels, local(): pl.pallas_call(functools.partial(gather_kernel, start=start * width // LA...  3.28 us
    pallas_call x1, Pallas kernels, local(): pl.pallas_call(finish_kernel, out_shape=(whole, jax.ShapeDtypeStruct((vec...  3 us
    pallas_call x2, Pallas kernels, local(): pl.pallas_call(functools.partial(filter_kernel, local_bits=local_bits, sc...  2.61 us
    pallas_call x1, Pallas kernels, local(): pl.pallas_call(functools.partial(ready_kernel, bit=rest_bits - 1, bond=lo...  2.03 us
  transfers between devices with their start and end apart: 14, of which 11 were waited for; matrix products, arithmetic and copies ran while one was open for 0% of the time, Pallas kernels for 23%

profile of v4, /device:TPU:0, one launch (start us, length us, event | category | flops | bytes accessed | tf_op | source)
XLA Modules:
  0.0 73.2 jit_solution(5353456535060213913)
XLA Ops:
  0.6 0.5 collective-permute-start.1
  1.1 2.4 %cut_0.1 = f32[32,10240]{1,0:T(8,128)} custom-call(f32[32,16384]{1,0:T(8,128)} %own_ref), custom_call_target="tpu_custom_call" | custom-call | bytes 2621440 | tf_op jit(solution)/shard_map/cut_0/pallas_call | solution.py:212
  3.6 3.0 %collective-permute-start.3 = (f32[32,10240]{1,0:T(8,128)}, f32[32,10240]{1,0:T(8,128)}, u32[]{:S(2)}, u32[]{:S(2)}) collective-permute-start(f32[32,10240]{1,0:T(8,128)} %cut_0.1), channel_id=1, source_target_pairs={{0,16},{1,17},{2,18},{3,19},{4,8},{5,9},{6,10},{7,11},{8,4},{9,5},... | collective-permute-start | bytes 3932168 | tf_op jit(solution)/shard_map/ppermute | solution.py:391
  6.6 2.1 %cut_10240.1 = f32[32,6144]{1,0:T(8,128)} custom-call(f32[32,16384]{1,0:T(8,128)} %own_ref), custom_call_target="tpu_custom_call" | custom-call | bytes 1572864 | tf_op jit(solution)/shard_map/cut_10240/pallas_call | solution.py:212
  8.8 1.5 %collective-permute-start.6 = (f32[32,6144]{1,0:T(8,128)}, f32[32,6144]{1,0:T(8,128)}, u32[]{:S(2)}, u32[]{:S(2)}) collective-permute-start(f32[32,6144]{1,0:T(8,128)} %cut_10240.1), channel_id=1, source_target_pairs={{0,16},{1,17},{2,18},{3,19},{4,8},{5,9},{6,10},{7,11},{8,4},{9,5},... | collective-permute-start | bytes 2359304 | tf_op jit(solution)/shard_map/ppermute | solution.py:391
  10.4 3.6 %local_bonds.1.local_ref = f32[32,16384]{1,0:T(8,128)S(1)} custom-call(s32[1]{0:T(128)} %bitcast.device_ref, s32[19]{0:T(128)S(1)} %copy-done.2, s32[18]{0:T(128)S(1)} %copy-done.1, f32[32,16384]{1,0:T(8,128)S(1)} %copy-done, f32[32,16384]{1,0:T(8,128)} %prev_ref.1), custom_call_target="tpu_custom_call" | custom-call | flops 805306368 | bytes 6291456 | tf_op jit(solution)/shard_map/local_bonds/pallas_call | solution.py:411
  14.0 2.0 %ready.1 = (f32[32,10240]{1,0:T(8,128)S(1)}, f32[32,6144]{1,0:T(8,128)S(1)}) custom-call(s32[1]{0:T(128)} %bitcast.device_ref, s32[18]{0:T(128)S(1)} %copy-done.1, f32[32,16384]{1,0:T(8,128)S(1)} %copy-done, f32[32,16384]{1,0:T(8,128)} %collective-permute-done.1.swap_ref), custom_call_target="tpu_custom_call" | custom-call | flops 3145728 | bytes 6291456 | tf_op jit(solution)/shard_map/ready/pallas_call | solution.py:420
  16.0 5.9 %collective-permute-done.arrived_ref.first_ref = f32[32,10240]{1,0:T(8,128)S(1)} collective-permute-done((f32[32,10240]{1,0:T(8,128)}, f32[32,10240]{1,0:T(8,128)S(1)}, u32[]{:S(2)}, u32[]{:S(2)}) %collective-permute-start) | collective-permute-done | bytes 1310752 | tf_op jit(solution)/shard_map/ppermute | solution.py:391
  22.0 0.7 sent_on_0.1
  22.6 2.1 %collective-permute-start.4 = (f32[32,10240]{1,0:T(8,128)S(1)}, f32[32,10240]{1,0:T(8,128)S(1)}, u32[]{:S(2)}, u32[]{:S(2)}) collective-permute-start(f32[32,10240]{1,0:T(8,128)S(1)} %sent_on_0.1), channel_id=1, source_target_pairs={{0,1},{1,4},{2,5},{3,7},{4,0},{5,2},{6,3},{7,6},{8,9},{9,12},{10,1... | collective-permute-start | bytes 3932168 | tf_op jit(solution)/shard_map/ppermute | solution.py:391
  24.7 1.5 %collective-permute-start.5 = (f32[32,10240]{1,0:T(8,128)}, f32[32,10240]{1,0:T(8,128)S(1)}, u32[]{:S(2)}, u32[]{:S(2)}) collective-permute-start(f32[32,10240]{1,0:T(8,128)} %collective-permute-done.3.refs_0_), channel_id=1, source_target_pairs={{0,8},{1,9},{2,10},{3,11},{4,16},{5,17},{6,18},{7,19},{8,0},{9,1},... | collective-permute-start | bytes 3932168 | tf_op jit(solution)/shard_map/ppermute | solution.py:391
  26.2 4.3 %collective-permute-done.2.arrived_ref.first_ref = f32[32,6144]{1,0:T(8,128)} collective-permute-done((f32[32,6144]{1,0:T(8,128)}, f32[32,6144]{1,0:T(8,128)}, u32[]{:S(2)}, u32[]{:S(2)}) %collective-permute-start.2) | collective-permute-done | bytes 786464 | tf_op jit(solution)/shard_map/ppermute | solution.py:391
  30.5 1.3 %sent_on_20.1 = f32[32,6144]{1,0:T(8,128)S(1)} custom-call(s32[1]{0:T(128)} %bitcast.device_ref, s32[18]{0:T(128)S(1)} %copy-done.1, f32[32,6144]{1,0:T(8,128)S(1)} %get-tuple-element.23.ready_ref, f32[32,6144]{1,0:T(8,128)} %collective-permute-done.2.arrived_ref.first_ref), custom_call_target="tpu_custom_call" | custom-call | tf_op jit(solution)/shard_map/sent_on_20/pallas_call | solution.py:439
  31.7 2.1 %collective-permute-start.7 = (f32[32,6144]{1,0:T(8,128)S(1)}, f32[32,6144]{1,0:T(8,128)S(1)}, u32[]{:S(2)}, u32[]{:S(2)}) collective-permute-start(f32[32,6144]{1,0:T(8,128)S(1)} %sent_on_20.1), channel_id=1, source_target_pairs={{0,1},{1,4},{2,5},{3,7},{4,0},{5,2},{6,3},{7,6},{8,9},{9,12},{10,1... | collective-permute-start | bytes 2359304 | tf_op jit(solution)/shard_map/ppermute | solution.py:391
  33.8 1.5 %collective-permute-start.8 = (f32[32,6144]{1,0:T(8,128)}, f32[32,6144]{1,0:T(8,128)S(1)}, u32[]{:S(2)}, u32[]{:S(2)}) collective-permute-start(f32[32,6144]{1,0:T(8,128)} %collective-permute-done.6.refs_0_), channel_id=1, source_target_pairs={{0,8},{1,9},{2,10},{3,11},{4,16},{5,17},{6,18},{7,19},{8,0},{9,1},... | collective-permute-start | bytes 2359304 | tf_op jit(solution)/shard_map/ppermute | solution.py:391
  35.3 1.7 %gather_first_0.1.acc_ref = f32[32,10240]{1,0:T(8,128)S(1)} custom-call(s32[1]{0:T(128)} %bitcast.device_ref, s32[18]{0:T(128)S(1)} %copy-done.1, f32[32,16384]{1,0:T(8,128)S(1)} %local_bonds.1.local_ref, f32[32,10240]{1,0:T(8,128)S(1)} %collective-permute-done.arrived_ref.first_ref, f32[32,10240]{1,0:T(8,128)} %collective-permute-done.3.refs_0_), custom_call_target="tpu_custom_call" | custom-call | tf_op jit(solution)/shard_map/gather_first_0/pallas_call | solution.py:457
  37.0 1.6 %gather_first_20.1.acc_ref = f32[32,6144]{1,0:T(8,128)S(1)} custom-call(s32[1]{0:T(128)} %bitcast.device_ref, s32[18]{0:T(128)S(1)} %copy-done.1, f32[32,16384]{1,0:T(8,128)S(1)} %local_bonds.1.local_ref, f32[32,6144]{1,0:T(8,128)} %collective-permute-done.2.arrived_ref.first_ref, f32[32,6144]{1,0:T(8,128)} %collective-permute-done.6.refs_0_), custom_call_target="tpu_custom_call" | custom-call | tf_op jit(solution)/shard_map/gather_first_20/pallas_call | solution.py:457
  38.6 4.9 %collective-permute-done.4.second_ref = f32[32,10240]{1,0:T(8,128)S(1)} collective-permute-done((f32[32,10240]{1,0:T(8,128)S(1)}, f32[32,10240]{1,0:T(8,128)S(1)}, u32[]{:S(2)}, u32[]{:S(2)}) %collective-permute-start.4) | collective-permute-done | bytes 1310752 | tf_op jit(solution)/shard_map/ppermute | solution.py:391
  43.5 2.8 %collective-permute-done.5.refs_0_ = f32[32,10240]{1,0:T(8,128)S(1)} collective-permute-done((f32[32,10240]{1,0:T(8,128)}, f32[32,10240]{1,0:T(8,128)S(1)}, u32[]{:S(2)}, u32[]{:S(2)}) %collective-permute-start.5) | collective-permute-done | bytes 1310752 | tf_op jit(solution)/shard_map/ppermute | solution.py:391
  46.3 1.3 %filter_gram_0.1 = (f32[32,10240]{1,0:T(8,128)S(1)}, f32[96,96]{1,0:T(8,128)S(1)}) custom-call(s32[1]{0:T(128)} %bitcast.device_ref, s32[18]{0:T(128)S(1)} %copy-done.1, f32[96,96]{1,0:T(8,128)S(1)} %broadcast_in_dim.3.before_ref, f32[32,10240]{1,0:T(8,128)S(1)} %gather_first_0.1.acc_ref, f32[32,10240]{1,0:T(8,128)S(1)} %collective-permute-done.4.second_ref, ...), custom_call_target="tpu_custom_call" | custom-call | flops 62914560 | bytes 5242880 | tf_op jit(solution)/shard_map/filter_gram_0/pallas_call | solution.py:478
  47.6 4.4 %collective-permute-done.7.second_ref = f32[32,6144]{1,0:T(8,128)S(1)} collective-permute-done((f32[32,6144]{1,0:T(8,128)S(1)}, f32[32,6144]{1,0:T(8,128)S(1)}, u32[]{:S(2)}, u32[]{:S(2)}) %collective-permute-start.7) | collective-permute-done | bytes 786464 | tf_op jit(solution)/shard_map/ppermute | solution.py:391
  51.9 2.8 %collective-permute-done.8.refs_0_ = f32[32,6144]{1,0:T(8,128)S(1)} collective-permute-done((f32[32,6144]{1,0:T(8,128)}, f32[32,6144]{1,0:T(8,128)S(1)}, u32[]{:S(2)}, u32[]{:S(2)}) %collective-permute-start.8) | collective-permute-done | bytes 786464 | tf_op jit(solution)/shard_map/ppermute | solution.py:391
  54.7 1.3 %filter_gram_20.1 = (f32[32,6144]{1,0:T(8,128)S(1)}, f32[8,128]{1,0:T(8,128)S(1)}) custom-call(s32[1]{0:T(128)} %bitcast.device_ref, s32[18]{0:T(128)S(1)} %copy-done.1, f32[96,96]{1,0:T(8,128)S(1)} %get-tuple-element.26.before_ref, f32[32,6144]{1,0:T(8,128)S(1)} %gather_first_20.1.acc_ref, f32[32,6144]{1,0:T(8,128)S(1)} %collective-permute-done.7.second_ref, ...), custom_call_target="tpu_custom_call" | custom-call | flops 37748736 | bytes 3145728 | tf_op jit(solution)/shard_map/filter_gram_20/pallas_call | solution.py:478
  56.0 1.2 %collective-permute-done.9 = f32[8,128]{1,0:T(8,128)S(1)} collective-permute-done((f32[8,128]{1,0:T(8,128)S(1)}, f32[8,128]{1,0:T(8,128)S(1)}, u32[]{:S(2)}, u32[]{:S(2)}) %collective-permute-start.9) | collective-permute-done | bytes 4128 | tf_op jit(solution)/shard_map/ppermute | solution.py:391
  57.5 2.7 %collective-permute-done.10 = f32[8,128]{1,0:T(8,128)S(1)} collective-permute-done((f32[8,128]{1,0:T(8,128)S(1)}, f32[8,128]{1,0:T(8,128)S(1)}, u32[]{:S(2)}, u32[]{:S(2)}) %collective-permute-start.10) | collective-permute-done | bytes 4128 | tf_op jit(solution)/shard_map/ppermute | solution.py:391
  60.2 0.9 %collective-permute-start.11 = (f32[8,128]{1,0:T(8,128)S(1)}, f32[8,128]{1,0:T(8,128)S(1)}, u32[]{:S(2)}, u32[]{:S(2)}) collective-permute-start(f32[8,128]{1,0:T(8,128)S(1)} %add.20), channel_id=1, source_target_pairs={{0,20},{1,21},{2,22},{3,23},{4,16},{5,17},{6,18},{7,19},{8,28},{9,... | collective-permute-start | bytes 12296 | tf_op jit(solution)/shard_map/ppermute | solution.py:391
  61.2 2.1 %collective-permute-done.11 = f32[8,128]{1,0:T(8,128)S(1)} collective-permute-done((f32[8,128]{1,0:T(8,128)S(1)}, f32[8,128]{1,0:T(8,128)S(1)}, u32[]{:S(2)}, u32[]{:S(2)}) %collective-permute-start.11) | collective-permute-done | bytes 4128 | tf_op jit(solution)/shard_map/ppermute | solution.py:391
  63.3 1.4 %collective-permute-start.12 = (f32[8,128]{1,0:T(8,128)S(1)}, f32[8,128]{1,0:T(8,128)S(1)}, u32[]{:S(2)}, u32[]{:S(2)}) collective-permute-start(f32[8,128]{1,0:T(8,128)S(1)} %add.21), channel_id=1, source_target_pairs={{0,5},{1,4},{2,7},{3,6},{4,1},{5,0},{6,3},{7,2},{8,13},{9,12},{10,... | collective-permute-start | bytes 12296 | tf_op jit(solution)/shard_map/ppermute | solution.py:391
  64.6 1.7 %collective-permute-done.12 = f32[8,128]{1,0:T(8,128)S(1)} collective-permute-done((f32[8,128]{1,0:T(8,128)S(1)}, f32[8,128]{1,0:T(8,128)S(1)}, u32[]{:S(2)}, u32[]{:S(2)}) %collective-permute-start.12) | collective-permute-done | bytes 4128 | tf_op jit(solution)/shard_map/ppermute | solution.py:391
  66.3 2.4 %collective-permute-start.13 = (f32[8,128]{1,0:T(8,128)S(1)}, f32[8,128]{1,0:T(8,128)S(1)}, u32[]{:S(2)}, u32[]{:S(2)}) collective-permute-start(f32[8,128]{1,0:T(8,128)S(1)} %add.22), channel_id=1, source_target_pairs={{0,6},{1,7},{2,4},{3,5},{4,2},{5,3},{6,0},{7,1},{8,14},{9,15},{10,... | collective-permute-start | bytes 12296 | tf_op jit(solution)/shard_map/ppermute | solution.py:391
  68.7 1.6 %collective-permute-done.13 = f32[8,128]{1,0:T(8,128)S(1)} collective-permute-done((f32[8,128]{1,0:T(8,128)S(1)}, f32[8,128]{1,0:T(8,128)S(1)}, u32[]{:S(2)}, u32[]{:S(2)}) %collective-permute-start.13) | collective-permute-done | bytes 4128 | tf_op jit(solution)/shard_map/ppermute | solution.py:391
  70.2 3.0 %factor_apply.1 = (f32[32,16384]{1,0:T(8,128)}, f32[32,32]{1,0:T(8,128)}) custom-call(f32[8,128]{1,0:T(8,128)S(1)} %add.23.gram_ref, f32[32,10240]{1,0:T(8,128)S(1)} %get-tuple-element.30.refs_0_, f32[32,6144]{1,0:T(8,128)S(1)} %get-tuple-element.31.refs_1_), custom_call_target="tpu_custom_call" | custom-call | flops 201326592 | bytes 4194304 | tf_op jit(solution)/shard_map/factor_apply/pallas_call | solution.py:501
  (19 shorter events, 0.6 us)
Async XLA Ops:
  0.6 13.4 %collective-permute-start.1 = (f32[32,16384]{1,0:T(8,128)}, f32[32,16384]{1,0:T(8,128)}, u32[]{:S(2)}, u32[]{:S(2)}) collective-permute-start(f32[32,16384]{1,0:T(8,128)} %own_ref), channel_id=1, source_target_pairs={{0,4},{1,5},{2,6},{3,7},{4,0},{5,1},{6,2},{7,3},{8,12},{9,13},{10,... | collective-permute-start | bytes 6291464 | tf_op jit(solution)/shard_map/ppermute | solution.py:391
  3.5 6.9 %copy-start = (f32[32,16384]{1,0:T(8,128)S(1)}, f32[32,16384]{1,0:T(8,128)}, u32[]{:S(2)}) copy-start(f32[32,16384]{1,0:T(8,128)} %own_ref) | copy-start | bytes 6291460
  3.5 6.8 %copy-start.1 = (s32[18]{0:T(128)S(1)}, s32[18]{0:T(128)}, u32[]{:S(2)}) copy-start(s32[18]{0:T(128)} %bond_ref.15) | copy-start | bytes 220
  3.5 6.8 %copy-start.2 = (s32[19]{0:T(128)S(1)}, s32[19]{0:T(128)}, u32[]{:S(2)}) copy-start(s32[19]{0:T(128)} %field_ref.1) | copy-start | bytes 232
  3.5 18.4 %collective-permute-start = (f32[32,10240]{1,0:T(8,128)}, f32[32,10240]{1,0:T(8,128)S(1)}, u32[]{:S(2)}, u32[]{:S(2)}) collective-permute-start(f32[32,10240]{1,0:T(8,128)} %cut_0.1), channel_id=1, source_target_pairs={{0,4},{1,0},{2,1},{3,2},{4,5},{5,6},{6,7},{7,3},{8,12},{9,8},{10,9... | collective-permute-start | bytes 3932168 | tf_op jit(solution)/shard_map/ppermute | solution.py:391
  3.6 21.1 %collective-permute-start.3 = (f32[32,10240]{1,0:T(8,128)}, f32[32,10240]{1,0:T(8,128)}, u32[]{:S(2)}, u32[]{:S(2)}) collective-permute-start(f32[32,10240]{1,0:T(8,128)} %cut_0.1), channel_id=1, source_target_pairs={{0,16},{1,17},{2,18},{3,19},{4,8},{5,9},{6,10},{7,11},{8,4},{9,5},... | collective-permute-start | bytes 3932168 | tf_op jit(solution)/shard_map/ppermute | solution.py:391
  8.7 21.7 %collective-permute-start.2 = (f32[32,6144]{1,0:T(8,128)}, f32[32,6144]{1,0:T(8,128)}, u32[]{:S(2)}, u32[]{:S(2)}) collective-permute-start(f32[32,6144]{1,0:T(8,128)} %cut_10240.1), channel_id=1, source_target_pairs={{0,4},{1,0},{2,1},{3,2},{4,5},{5,6},{6,7},{7,3},{8,12},{9,8},{10,9... | collective-permute-start | bytes 2359304 | tf_op jit(solution)/shard_map/ppermute | solution.py:391
  8.8 25.0 %collective-permute-start.6 = (f32[32,6144]{1,0:T(8,128)}, f32[32,6144]{1,0:T(8,128)}, u32[]{:S(2)}, u32[]{:S(2)}) collective-permute-start(f32[32,6144]{1,0:T(8,128)} %cut_10240.1), channel_id=1, source_target_pairs={{0,16},{1,17},{2,18},{3,19},{4,8},{5,9},{6,10},{7,11},{8,4},{9,5},... | collective-permute-start | bytes 2359304 | tf_op jit(solution)/shard_map/ppermute | solution.py:391
  22.6 20.9 %collective-permute-start.4 = (f32[32,10240]{1,0:T(8,128)S(1)}, f32[32,10240]{1,0:T(8,128)S(1)}, u32[]{:S(2)}, u32[]{:S(2)}) collective-permute-start(f32[32,10240]{1,0:T(8,128)S(1)} %sent_on_0.1), channel_id=1, source_target_pairs={{0,1},{1,4},{2,5},{3,7},{4,0},{5,2},{6,3},{7,6},{8,9},{9,12},{10,1... | collective-permute-start | bytes 3932168 | tf_op jit(solution)/shard_map/ppermute | solution.py:391
  24.7 21.5 %collective-permute-start.5 = (f32[32,10240]{1,0:T(8,128)}, f32[32,10240]{1,0:T(8,128)S(1)}, u32[]{:S(2)}, u32[]{:S(2)}) collective-permute-start(f32[32,10240]{1,0:T(8,128)} %collective-permute-done.3.refs_0_), channel_id=1, source_target_pairs={{0,8},{1,9},{2,10},{3,11},{4,16},{5,17},{6,18},{7,19},{8,0},{9,1},... | collective-permute-start | bytes 3932168 | tf_op jit(solution)/shard_map/ppermute | solution.py:391
  31.7 20.2 %collective-permute-start.7 = (f32[32,6144]{1,0:T(8,128)S(1)}, f32[32,6144]{1,0:T(8,128)S(1)}, u32[]{:S(2)}, u32[]{:S(2)}) collective-permute-start(f32[32,6144]{1,0:T(8,128)S(1)} %sent_on_20.1), channel_id=1, source_target_pairs={{0,1},{1,4},{2,5},{3,7},{4,0},{5,2},{6,3},{7,6},{8,9},{9,12},{10,1... | collective-permute-start | bytes 2359304 | tf_op jit(solution)/shard_map/ppermute | solution.py:391
  33.8 20.9 %collective-permute-start.8 = (f32[32,6144]{1,0:T(8,128)}, f32[32,6144]{1,0:T(8,128)S(1)}, u32[]{:S(2)}, u32[]{:S(2)}) collective-permute-start(f32[32,6144]{1,0:T(8,128)} %collective-permute-done.6.refs_0_), channel_id=1, source_target_pairs={{0,8},{1,9},{2,10},{3,11},{4,16},{5,17},{6,18},{7,19},{8,0},{9,1},... | collective-permute-start | bytes 2359304 | tf_op jit(solution)/shard_map/ppermute | solution.py:391
  56.0 1.2 %collective-permute-start.9 = (f32[8,128]{1,0:T(8,128)S(1)}, f32[8,128]{1,0:T(8,128)S(1)}, u32[]{:S(2)}, u32[]{:S(2)}) collective-permute-start(f32[8,128]{1,0:T(8,128)S(1)} %get-tuple-element.29), channel_id=1, source_target_pairs={{0,4},{1,5},{2,6},{3,7},{4,0},{5,1},{6,2},{7,3},{8,12},{9,13},{10,... | collective-permute-start | bytes 12296 | tf_op jit(solution)/shard_map/ppermute | solution.py:391
  57.2 3.0 %collective-permute-start.10 = (f32[8,128]{1,0:T(8,128)S(1)}, f32[8,128]{1,0:T(8,128)S(1)}, u32[]{:S(2)}, u32[]{:S(2)}) collective-permute-start(f32[8,128]{1,0:T(8,128)S(1)} %add.19), channel_id=1, source_target_pairs={{0,12},{1,13},{2,14},{3,15},{4,8},{5,9},{6,10},{7,11},{8,4},{9,5},... | collective-permute-start | bytes 12296 | tf_op jit(solution)/shard_map/ppermute | solution.py:391
  60.2 3.0 %collective-permute-start.11 = (f32[8,128]{1,0:T(8,128)S(1)}, f32[8,128]{1,0:T(8,128)S(1)}, u32[]{:S(2)}, u32[]{:S(2)}) collective-permute-start(f32[8,128]{1,0:T(8,128)S(1)} %add.20), channel_id=1, source_target_pairs={{0,20},{1,21},{2,22},{3,23},{4,16},{5,17},{6,18},{7,19},{8,28},{9,... | collective-permute-start | bytes 12296 | tf_op jit(solution)/shard_map/ppermute | solution.py:391
  63.3 3.0 %collective-permute-start.12 = (f32[8,128]{1,0:T(8,128)S(1)}, f32[8,128]{1,0:T(8,128)S(1)}, u32[]{:S(2)}, u32[]{:S(2)}) collective-permute-start(f32[8,128]{1,0:T(8,128)S(1)} %add.21), channel_id=1, source_target_pairs={{0,5},{1,4},{2,7},{3,6},{4,1},{5,0},{6,3},{7,2},{8,13},{9,12},{10,... | collective-permute-start | bytes 12296 | tf_op jit(solution)/shard_map/ppermute | solution.py:391
  66.3 3.9 %collective-permute-start.13 = (f32[8,128]{1,0:T(8,128)S(1)}, f32[8,128]{1,0:T(8,128)S(1)}, u32[]{:S(2)}, u32[]{:S(2)}) collective-permute-start(f32[8,128]{1,0:T(8,128)S(1)} %add.22), channel_id=1, source_target_pairs={{0,6},{1,7},{2,4},{3,5},{4,2},{5,3},{6,0},{7,1},{8,14},{9,15},{10,... | collective-permute-start | bytes 12296 | tf_op jit(solution)/shard_map/ppermute | solution.py:391

commit v5 on v4

--- a/solution.py
+++ b/solution.py
@@ -18,7 +18,8 @@
 OUT_CHUNK = 2048
 PANEL = 16
 GROUP_BITS = 8
-VMEM_LIMIT = 48 * 1024 * 1024
+VMEM_LIMIT = 28 * 1024 * 1024
+ADD_COST = 10**9
 CUT_LIMIT = 56 * 1024 * 1024
 
 
@@ -41,8 +42,8 @@
 
 FIRST = {(0, 1, 0): (1, 0, 0), (1, 1, 0): (0, 1, 0), (1, 0, 0): (0, 0, 0), (0, 0, 0): (0, 0, 1)}
 SECOND = {(0, 1, 0): (1, 0, 1), (1, 0, 0): (0, 0, 1), (0, 0, 0): (1, 0, 0), (1, 1, 0): (1, 1, 1)}
-BOTH = {(0, 1, 0): (1, 0, 0), (1, 0, 0): (0, 1, 0), (1, 1, 0): (1, 1, 1), (0, 0, 0): (0, 0, 1)}
-ON = {(1, 0, 1): (1, 1, 1), (0, 0, 0): (0, 1, 0), (1, 0, 0): (0, 0, 1), (0, 0, 1): (1, 0, 0)}
+LATER_FIRST = {(0, 1, 0): (1, 0, 0), (1, 1, 0): (1, 1, 1)}
+LATER_SECOND = {(1, 1, 1): (1, 0, 1), (1, 0, 0): (0, 0, 1)}
 
 
 def route(devices, m, table):
@@ -52,7 +53,9 @@
         full[tuple(1 - b for b in one)] = tuple(1 - b for b in two)
     pairs = []
     for device in range(devices):
-        goal = full[tuple(device >> m + j & 1 for j in (-1, 0, 1))]
+        goal = full.get(tuple(device >> m + j & 1 for j in (-1, 0, 1)))
+        if goal is None:
+            continue
         pairs.append((device, device & ~(7 << m - 1) | goal[0] << m - 1 | goal[1] << m | goal[2] << m + 1))
     return pairs
 
@@ -238,6 +241,19 @@
             t += 1
 
 
+def later_ready_kernel(device_ref, bond_ref, swap_ref, *out_refs, middle, bond, scale):
+    p, m, q = (bit_of(device_ref, middle + k) for k in (-1, 0, 1))
+    low = jnp.where((p == m) & (q == m), strength_of(bond_ref, bond, scale), 0.0)
+    first = 0
+    for out_ref in out_refs:
+        out_ref[...] = low * swap_ref[:, first : first + out_ref.shape[1]]
+        first += out_ref.shape[1]
+
+
+def later_sent_kernel(bond_ref, ready_ref, arrived_ref, out_ref, *, bond, scale):
+    out_ref[...] = ready_ref[...] + strength_of(bond_ref, bond, scale) * arrived_ref[...]
+
+
 def sent_kernel(device_ref, bond_ref, ready_ref, arrived_ref, out_ref, *, bond, scale):
     high = strength_of(bond_ref, bond + 2, scale)
     high = jnp.where(bit_of(device_ref, 0) != bit_of(device_ref, 1), high, 0.0)
@@ -253,8 +269,9 @@
     pair = [jnp.where(halves & (p != side), joint, 0.0) for side in (0, 1)]
     weights = []
     for k in range(len(refs) - 1):
-        differ = bit_of(device_ref, 2 * k + 2) != bit_of(device_ref, 2 * k + 3)
-        weights.append(jnp.where(differ, strength_of(bond_ref, local_bits + 2 * k + 2, scale), 0.0))
+        p, m, q = (bit_of(device_ref, 2 * k + j) for j in (2, 3, 4))
+        weight = strength_of(bond_ref, local_bits + 2 * k + 2, scale)
+        weights.append(jnp.where((p != m) & (q == m), weight, 0.0))
     for t in range(out_ref.shape[1] // LANES):
         total = tile_of(local_ref, start + t) + low * tile_of(first_ref, t)
         total = total + sided(pair, t, bit) * across(first_ref, t, bit)
@@ -274,19 +291,19 @@
     return jnp.concatenate([table[:, k * vectors : (k + 1) * vectors] for k in range(fold)], axis=0)
 
 
-def filter_kernel(device_ref, bond_ref, before_ref, acc_ref, second_ref, *refs, local_bits, scale, share, last):
+def add_kernel(one_ref, two_ref, out_ref):
+    out_ref[...] = one_ref[...] + two_ref[...]
+
+
+def filter_kernel(before_ref, acc_ref, *refs, share, last):
     out_ref, gram_ref = refs[-2:]
     vectors, amp_count = acc_ref.shape
-    weights = []
-    for k in range(len(refs) - 2):
-        differ = bit_of(device_ref, 2 * k + 3) != bit_of(device_ref, 2 * k + 4)
-        weights.append(jnp.where(differ, strength_of(bond_ref, local_bits + 2 * k + 3, scale), 0.0))
     table = before_ref[...]
     for first in range(0, amp_count, CHUNK):
         cols = slice(first, min(first + CHUNK, amp_count))
-        total = acc_ref[:, cols] + second_ref[:, cols]
-        for weight, ref in zip(weights, refs):
-            total = total + weight * ref[:, cols]
+        total = acc_ref[:, cols]
+        for ref in refs[:-2]:
+            total = total + ref[:, cols]
         out_ref[:, cols] = total
         stacked = jnp.concatenate(pieces(total, 3), axis=0)
         table = table + lax.dot_general(
@@ -399,12 +416,12 @@
     middles = tuple(range(3, global_bits - 1, 2))
     width = amp_count // 32
     parts = [(0, 20), (20, 12)]
-    swap = permute(current, flips(4))
+    swaps = [permute(current, flips(1 << m - 1)) for m in middles or (3,)]
     firsts, boths = [], []
     for start, count in parts:
         piece = cut(current, start * width, count * width)
         firsts.append(permute(piece, route(devices, 1, FIRST)))
-        boths.append([permute(piece, route(devices, m, BOTH)) for m in middles])
+        boths.append([permute(piece, route(devices, m, LATER_FIRST)) for m in middles])
 
     current, _ = lax.optimization_barrier((current, piece))
 
@@ -425,15 +442,27 @@
         compiler_params=params(),
         cost_estimate=cost(6 * size, 12 * size),
         name="ready",
-    )(place, bond_levels, current, swap)
-    firsts[0], here, ready = lax.optimization_barrier((firsts[0], here, ready))
+    )(place, bond_levels, current, swaps[0])
+    later_ready = [
+        pl.pallas_call(
+            functools.partial(later_ready_kernel, middle=m, bond=local_bits + m - 1, scale=scale),
+            out_shape=tuple(jax.ShapeDtypeStruct((vectors, count * width), jnp.float32) for _, count in parts),
+            in_specs=[smem()] * 2 + [vmem],
+            out_specs=tuple(vmem for _ in parts),
+            compiler_params=params(),
+            cost_estimate=cost(size, 8 * size),
+            name=f"ready_{m}",
+        )(place, bond_levels, swap)
+        for m, swap in zip(middles, swaps)
+    ]
+    firsts[0], here, ready, later_ready = lax.optimization_barrier((firsts[0], here, ready, later_ready))
     if global_bits % 2 == 0:
         top = global_bits - 1
         moved = permute(current, flips(3 << top - 1, lambda i: (i >> top & 1) != (i >> top - 1 & 1)))
         here = here + strength(site_count - 2) * moved
 
     seconds, ons, accs, sents = [], [], [], []
-    for (start, count), first, both, base in zip(parts, firsts, boths, ready):
+    for number, ((start, count), first, both, base) in enumerate(zip(parts, firsts, boths, ready)):
         shape = jax.ShapeDtypeStruct((vectors, count * width), jnp.float32)
         part_size = vectors * count * width
         sent = pl.pallas_call(
@@ -447,8 +476,20 @@
         )(place, bond_levels, base, first)
         seconds.append(permute(sent, route(devices, 1, SECOND)))
         sents.append(sent)
-        both, sent = lax.optimization_barrier((both, sent))
-        ons.append([permute(values, route(devices, m, ON)) for m, values in zip(middles, both)])
+        arrived, sent = lax.optimization_barrier((both, sent))
+        on = []
+        for m, values, bases in zip(middles, arrived, later_ready):
+            sent = pl.pallas_call(
+                functools.partial(later_sent_kernel, bond=local_bits + m, scale=scale),
+                out_shape=shape,
+                in_specs=[smem()] + [vmem] * 2,
+                out_specs=vmem,
+                compiler_params=params(),
+                cost_estimate=cost(0, 0),
+                name=f"sent_{m}_{start}",
+            )(bond_levels, bases[number], values)
+            on.append(permute(sent, route(devices, m, LATER_SECOND)))
+        ons.append(on)
     firsts, sents = lax.optimization_barrier((firsts, sents))
     for (start, count), first, both in zip(parts, firsts, boths):
         shape = jax.ShapeDtypeStruct((vectors, count * width), jnp.float32)
@@ -475,20 +516,28 @@
     for number, ((start, count), acc, second, on) in enumerate(zip(parts, accs, seconds, ons)):
         last = number == len(parts) - 1
         part_size = vectors * count * width
+        second, products = lax.optimization_barrier((second, products))
+        acc = pl.pallas_call(
+            add_kernel,
+            out_shape=jax.ShapeDtypeStruct((vectors, count * width), jnp.float32),
+            in_specs=[vmem] * 2,
+            out_specs=vmem,
+            compiler_params=params(),
+            cost_estimate=cost(ADD_COST, 0),
+            name=f"add_{start}",
+        )(acc, second)
         done, products = pl.pallas_call(
-            functools.partial(
-                filter_kernel, local_bits=local_bits, scale=scale, share=1.0 / (amp_count * devices), last=last
-            ),
+            functools.partial(filter_kernel, share=1.0 / (amp_count * devices), last=last),
             out_shape=(
                 jax.ShapeDtypeStruct((vectors, count * width), jnp.float32),
                 jax.ShapeDtypeStruct(table if last else square, jnp.float32),
             ),
-            in_specs=[smem()] * 2 + [vmem] * (3 + len(on)),
+            in_specs=[vmem] * (2 + len(on)),
             out_specs=(vmem, vmem),
             compiler_params=params(),
             cost_estimate=cost(6 * part_size * vectors, 16 * part_size),
             name=f"filter_gram_{start}",
-        )(place, bond_levels, products, acc, second, *on)
+        )(products, acc, *on)
         filtered.append(done)
     gram = products
 

time: 73.6 us -> 72.2 us (0.981)
  waiting for transfers between devices: 34.2 us -> 21.5 us
  starting transfers between devices: 17.3 us -> 24.7 us
  Pallas kernels: 21 us -> 23 us
  local copies, waits for them, and re-layouts: 0.02 us -> 1.61 us
    ppermute x14, waiting for transfers between devices: 34.2 us -> 21.5 us  [permute(): return lax.ppermute(values, AXES, pairs)]
    ppermute x14, starting transfers between devices: 17.3 us -> 24.7 us  [permute(): return lax.ppermute(values, AXES, pairs)]
    pallas_call x2 -> x7, Pallas kernels: 2.61 us -> 6.06 us  [the longest x2 2.68 us: local(): pl.pallas_call(functools.partial(later_sent_kernel, bond=local_bits + m,...]
    unnamed x6 -> x8, local copies, waits for them, and re-layouts: 0.02 us -> 1.61 us
    pallas_call x1, Pallas kernels: 3.6 us -> 2.49 us  [local(): pl.pallas_call(functools.partial(local_kernel, global_bits=global_bits, s...]
  transfers between devices with their start and end apart: 14 -> 14, of which waited for: 11 -> 11; matrix products, arithmetic and copies ran while one was open for 0% -> 0% of each run, Pallas kernels for 23% -> 27%
where the time goes in v5:
time: 72.2 us; the launch traced here: 71.7 us
  starting transfers between devices  24.7 us (34%)
  Pallas kernels  23 us (32%)
  waiting for transfers between devices  21.5 us (30%)
  local copies, waits for them, and re-layouts  1.61 us (2%)
  between operations  0.85 us (1%)
    ppermute x14, starting transfers between devices, permute(): return lax.ppermute(values, AXES, pairs)  24.7 us
    ppermute x14, waiting for transfers between devices, permute(): return lax.ppermute(values, AXES, pairs)  21.5 us
    pallas_call x2, Pallas kernels, cut(): pl.pallas_call(functools.partial(cut_kernel, start=start), out_shape=jax....  4.49 us
    pallas_call x2, Pallas kernels, local(): pl.pallas_call(functools.partial(gather_kernel, start=start * width // LA...  3.14 us
    pallas_call x1, Pallas kernels, local(): pl.pallas_call(finish_kernel, out_shape=(whole, jax.ShapeDtypeStruct((vec...  3 us
    pallas_call x2, Pallas kernels, local(): pl.pallas_call(functools.partial(later_sent_kernel, bond=local_bits + m,...  2.68 us
    pallas_call x1, Pallas kernels, local(): pl.pallas_call(functools.partial(local_kernel, global_bits=global_bits, s...  2.49 us
    pallas_call x1, Pallas kernels, local(): pl.pallas_call(functools.partial(ready_kernel, bit=rest_bits - 1, bond=lo...  1.97 us
  transfers between devices with their start and end apart: 14, of which 11 were waited for; matrix products, arithmetic and copies ran while one was open for 0% of the time, Pallas kernels for 27%

profile of v5, /device:TPU:0, one launch (start us, length us, event | category | flops | bytes accessed | tf_op | source)
XLA Modules:
  0.0 71.7 jit_solution(9307790320514960647)
XLA Ops:
  1.1 2.4 %cut_0.1 = f32[32,10240]{1,0:T(8,128)} custom-call(f32[32,16384]{1,0:T(8,128)} %own_ref), custom_call_target="tpu_custom_call" | custom-call | bytes 2621440 | tf_op jit(solution)/shard_map/cut_0/pallas_call | solution.py:215
  3.6 1.4 %collective-permute-start.5 = (f32[32,10240]{1,0:T(8,128)}, f32[32,10240]{1,0:T(8,128)}, u32[]{:S(2)}, u32[]{:S(2)}) collective-permute-start(f32[32,10240]{1,0:T(8,128)} %cut_0.1), channel_id=1, source_target_pairs={{8,4},{9,5},{10,6},{11,7},{12,28},{13,29},{14,30},{15,31},{16,0},{... | collective-permute-start | bytes 3932168 | tf_op jit(solution)/shard_map/ppermute | solution.py:408
  5.0 2.1 %cut_10240.1 = f32[32,6144]{1,0:T(8,128)} custom-call(f32[32,16384]{1,0:T(8,128)} %own_ref), custom_call_target="tpu_custom_call" | custom-call | bytes 1572864 | tf_op jit(solution)/shard_map/cut_10240/pallas_call | solution.py:215
  7.2 2.6 %collective-permute-start.2 = (f32[32,6144]{1,0:T(8,128)}, f32[32,6144]{1,0:T(8,128)}, u32[]{:S(2)}, u32[]{:S(2)}) collective-permute-start(f32[32,6144]{1,0:T(8,128)} %cut_10240.1), channel_id=1, source_target_pairs={{0,4},{1,0},{2,1},{3,2},{4,5},{5,6},{6,7},{7,3},{8,12},{9,8},{10,9... | collective-permute-start | bytes 2359304 | tf_op jit(solution)/shard_map/ppermute | solution.py:408
  9.8 1.3 %collective-permute-start.7 = (f32[32,6144]{1,0:T(8,128)}, f32[32,6144]{1,0:T(8,128)}, u32[]{:S(2)}, u32[]{:S(2)}) collective-permute-start(f32[32,6144]{1,0:T(8,128)} %cut_10240.1), channel_id=1, source_target_pairs={{8,4},{9,5},{10,6},{11,7},{12,28},{13,29},{14,30},{15,31},{16,0},{... | collective-permute-start | bytes 2359304 | tf_op jit(solution)/shard_map/ppermute | solution.py:408
  11.1 1.6 %copy-done.1 = f32[32,16384]{1,0:T(8,128)S(1)} copy-done((f32[32,16384]{1,0:T(8,128)S(1)}, f32[32,16384]{1,0:T(8,128)}, u32[]{:S(2)}) %copy-start.1) | copy-done | bytes 2097176
  12.7 2.5 %local_bonds.1.local_ref = f32[32,16384]{1,0:T(8,128)S(1)} custom-call(s32[1]{0:T(128)} %bitcast.device_ref, s32[19]{0:T(128)S(1)} %copy-done.3, s32[18]{0:T(128)S(1)} %copy-done.2, f32[32,16384]{1,0:T(8,128)S(1)} %copy-done, f32[32,16384]{1,0:T(8,128)S(1)} %copy-done.1), custom_call_target="tpu_custom_call" | custom-call | flops 805306368 | bytes 6291456 | tf_op jit(solution)/shard_map/local_bonds/pallas_call | solution.py:428
  15.2 1.7 %ready_3.1 = (f32[32,10240]{1,0:T(8,128)S(1)}, f32[32,6144]{1,0:T(8,128)S(1)}) custom-call(s32[1]{0:T(128)} %bitcast.device_ref, s32[18]{0:T(128)S(1)} %copy-done.2, f32[32,16384]{1,0:T(8,128)} %collective-permute-done.1.swap_ref), custom_call_target="tpu_custom_call" | custom-call | flops 524288 | bytes 4194304 | tf_op jit(solution)/shard_map/ready_3/pallas_call | solution.py:447
  17.0 2.0 %ready.1 = (f32[32,10240]{1,0:T(8,128)S(1)}, f32[32,6144]{1,0:T(8,128)S(1)}) custom-call(s32[1]{0:T(128)} %bitcast.device_ref, s32[18]{0:T(128)S(1)} %copy-done.2, f32[32,16384]{1,0:T(8,128)S(1)} %copy-done, f32[32,16384]{1,0:T(8,128)} %collective-permute-done.1.swap_ref), custom_call_target="tpu_custom_call" | custom-call | flops 3145728 | bytes 6291456 | tf_op jit(solution)/shard_map/ready/pallas_call | solution.py:437
  19.0 3.0 %collective-permute-done.arrived_ref.first_ref = f32[32,10240]{1,0:T(8,128)S(1)} collective-permute-done((f32[32,10240]{1,0:T(8,128)}, f32[32,10240]{1,0:T(8,128)S(1)}, u32[]{:S(2)}, u32[]{:S(2)}) %collective-permute-start) | collective-permute-done | bytes 1310752 | tf_op jit(solution)/shard_map/ppermute | solution.py:408
  22.6 2.1 %collective-permute-start.4 = (f32[32,10240]{1,0:T(8,128)S(1)}, f32[32,10240]{1,0:T(8,128)S(1)}, u32[]{:S(2)}, u32[]{:S(2)}) collective-permute-start(f32[32,10240]{1,0:T(8,128)S(1)} %sent_on_0.1), channel_id=1, source_target_pairs={{0,1},{1,4},{2,5},{3,7},{4,0},{5,2},{6,3},{7,6},{8,9},{9,12},{10,1... | collective-permute-start | bytes 3932168 | tf_op jit(solution)/shard_map/ppermute | solution.py:408
  24.7 1.5 %sent_3_0.1 = f32[32,10240]{1,0:T(8,128)S(1)} custom-call(s32[18]{0:T(128)S(1)} %copy-done.2, f32[32,10240]{1,0:T(8,128)S(1)} %get-tuple-element.37.ready_ref, f32[32,10240]{1,0:T(8,128)} %collective-permute-done.5.refs_0_.arrived_ref), custom_call_target="tpu_custom_call" | custom-call | tf_op jit(solution)/shard_map/sent_3_0/pallas_call | solution.py:482
  26.2 3.5 %collective-permute-start.6 = (f32[32,10240]{1,0:T(8,128)S(1)}, f32[32,10240]{1,0:T(8,128)S(1)}, u32[]{:S(2)}, u32[]{:S(2)}) collective-permute-start(f32[32,10240]{1,0:T(8,128)S(1)} %sent_3_0.1), channel_id=1, source_target_pairs={{0,8},{1,9},{2,10},{3,11},{4,16},{5,17},{6,18},{7,19},{24,12},{25,... | collective-permute-start | bytes 3932168 | tf_op jit(solution)/shard_map/ppermute | solution.py:408
  30.5 1.2 %sent_on_20.1 = f32[32,6144]{1,0:T(8,128)S(1)} custom-call(s32[1]{0:T(128)} %bitcast.device_ref, s32[18]{0:T(128)S(1)} %copy-done.2, f32[32,6144]{1,0:T(8,128)S(1)} %get-tuple-element.30.ready_ref, f32[32,6144]{1,0:T(8,128)} %collective-permute-done.2.arrived_ref.first_ref), custom_call_target="tpu_custom_call" | custom-call | tf_op jit(solution)/shard_map/sent_on_20/pallas_call | solution.py:468
  31.7 2.1 %collective-permute-start.3 = (f32[32,6144]{1,0:T(8,128)S(1)}, f32[32,6144]{1,0:T(8,128)S(1)}, u32[]{:S(2)}, u32[]{:S(2)}) collective-permute-start(f32[32,6144]{1,0:T(8,128)S(1)} %sent_on_20.1), channel_id=1, source_target_pairs={{0,1},{1,4},{2,5},{3,7},{4,0},{5,2},{6,3},{7,6},{8,9},{9,12},{10,1... | collective-permute-start | bytes 2359304 | tf_op jit(solution)/shard_map/ppermute | solution.py:408
  33.8 1.2 %sent_3_20.1 = f32[32,6144]{1,0:T(8,128)S(1)} custom-call(s32[18]{0:T(128)S(1)} %copy-done.2, f32[32,6144]{1,0:T(8,128)S(1)} %get-tuple-element.43.ready_ref, f32[32,6144]{1,0:T(8,128)} %collective-permute-done.7.refs_0_.arrived_ref), custom_call_target="tpu_custom_call" | custom-call | tf_op jit(solution)/shard_map/sent_3_20/pallas_call | solution.py:482
  35.0 3.4 %collective-permute-start.8 = (f32[32,6144]{1,0:T(8,128)S(1)}, f32[32,6144]{1,0:T(8,128)S(1)}, u32[]{:S(2)}, u32[]{:S(2)}) collective-permute-start(f32[32,6144]{1,0:T(8,128)S(1)} %sent_3_20.1), channel_id=1, source_target_pairs={{0,8},{1,9},{2,10},{3,11},{4,16},{5,17},{6,18},{7,19},{24,12},{25,... | collective-permute-start | bytes 2359304 | tf_op jit(solution)/shard_map/ppermute | solution.py:408
  38.5 1.5 %gather_first_20.1.one_ref = f32[32,6144]{1,0:T(8,128)S(1)} custom-call(s32[1]{0:T(128)} %bitcast.device_ref, s32[18]{0:T(128)S(1)} %copy-done.2, f32[32,16384]{1,0:T(8,128)S(1)} %local_bonds.1.local_ref, f32[32,6144]{1,0:T(8,128)} %collective-permute-done.2.arrived_ref.first_ref, f32[32,6144]{1,0:T(8,128)} %collective-permute-done.7.refs_0_.arrived_ref), custom_call_target="tpu_custom_call" | custom-call | tf_op jit(solution)/shard_map/gather_first_20/pallas_call | solution.py:498
  40.0 1.6 %gather_first_0.1.one_ref = f32[32,10240]{1,0:T(8,128)S(1)} custom-call(s32[1]{0:T(128)} %bitcast.device_ref, s32[18]{0:T(128)S(1)} %copy-done.2, f32[32,16384]{1,0:T(8,128)S(1)} %local_bonds.1.local_ref, f32[32,10240]{1,0:T(8,128)S(1)} %collective-permute-done.arrived_ref.first_ref, f32[32,10240]{1,0:T(8,128)} %collective-permute-done.5.refs_0_.arrived_ref), custom_call_target="tpu_custom_call" | custom-call | tf_op jit(solution)/shard_map/gather_first_0/pallas_call | solution.py:498
  41.6 1.9 %collective-permute-done.4.two_ref = f32[32,10240]{1,0:T(8,128)S(1)} collective-permute-done((f32[32,10240]{1,0:T(8,128)S(1)}, f32[32,10240]{1,0:T(8,128)S(1)}, u32[]{:S(2)}, u32[]{:S(2)}) %collective-permute-start.4) | collective-permute-done | bytes 1310752 | tf_op jit(solution)/shard_map/ppermute | solution.py:408
  45.4 6.5 %collective-permute-done.3.two_ref = f32[32,6144]{1,0:T(8,128)S(1)} collective-permute-done((f32[32,6144]{1,0:T(8,128)S(1)}, f32[32,6144]{1,0:T(8,128)S(1)}, u32[]{:S(2)}, u32[]{:S(2)}) %collective-permute-start.3) | collective-permute-done | bytes 786464 | tf_op jit(solution)/shard_map/ppermute | solution.py:408
  52.0 1.1 %collective-permute-done.8.refs_0_ = f32[32,6144]{1,0:T(8,128)S(1)} collective-permute-done((f32[32,6144]{1,0:T(8,128)S(1)}, f32[32,6144]{1,0:T(8,128)S(1)}, u32[]{:S(2)}, u32[]{:S(2)}) %collective-permute-start.8) | collective-permute-done | bytes 786464 | tf_op jit(solution)/shard_map/ppermute | solution.py:408
  53.9 1.2 %collective-permute-done.9 = f32[8,128]{1,0:T(8,128)S(1)} collective-permute-done((f32[8,128]{1,0:T(8,128)S(1)}, f32[8,128]{1,0:T(8,128)S(1)}, u32[]{:S(2)}, u32[]{:S(2)}) %collective-permute-start.9) | collective-permute-done | bytes 4128 | tf_op jit(solution)/shard_map/ppermute | solution.py:408
  55.0 2.3 %collective-permute-start.10 = (f32[8,128]{1,0:T(8,128)S(1)}, f32[8,128]{1,0:T(8,128)S(1)}, u32[]{:S(2)}, u32[]{:S(2)}) collective-permute-start(f32[8,128]{1,0:T(8,128)S(1)} %add.19), channel_id=1, source_target_pairs={{0,12},{1,13},{2,14},{3,15},{4,8},{5,9},{6,10},{7,11},{8,4},{9,5},... | collective-permute-start | bytes 12296 | tf_op jit(solution)/shard_map/ppermute | solution.py:408
  57.3 1.3 %collective-permute-done.10 = f32[8,128]{1,0:T(8,128)S(1)} collective-permute-done((f32[8,128]{1,0:T(8,128)S(1)}, f32[8,128]{1,0:T(8,128)S(1)}, u32[]{:S(2)}, u32[]{:S(2)}) %collective-permute-start.10) | collective-permute-done | bytes 4128 | tf_op jit(solution)/shard_map/ppermute | solution.py:408
  58.6 1.2 %collective-permute-start.11 = (f32[8,128]{1,0:T(8,128)S(1)}, f32[8,128]{1,0:T(8,128)S(1)}, u32[]{:S(2)}, u32[]{:S(2)}) collective-permute-start(f32[8,128]{1,0:T(8,128)S(1)} %add.20), channel_id=1, source_target_pairs={{0,20},{1,21},{2,22},{3,23},{4,16},{5,17},{6,18},{7,19},{8,28},{9,... | collective-permute-start | bytes 12296 | tf_op jit(solution)/shard_map/ppermute | solution.py:408
  59.8 1.9 %collective-permute-done.11 = f32[8,128]{1,0:T(8,128)S(1)} collective-permute-done((f32[8,128]{1,0:T(8,128)S(1)}, f32[8,128]{1,0:T(8,128)S(1)}, u32[]{:S(2)}, u32[]{:S(2)}) %collective-permute-start.11) | collective-permute-done | bytes 4128 | tf_op jit(solution)/shard_map/ppermute | solution.py:408
  61.7 1.7 %collective-permute-start.12 = (f32[8,128]{1,0:T(8,128)S(1)}, f32[8,128]{1,0:T(8,128)S(1)}, u32[]{:S(2)}, u32[]{:S(2)}) collective-permute-start(f32[8,128]{1,0:T(8,128)S(1)} %add.21), channel_id=1, source_target_pairs={{0,5},{1,4},{2,7},{3,6},{4,1},{5,0},{6,3},{7,2},{8,13},{9,12},{10,... | collective-permute-start | bytes 12296 | tf_op jit(solution)/shard_map/ppermute | solution.py:408
  63.3 1.4 %collective-permute-done.12 = f32[8,128]{1,0:T(8,128)S(1)} collective-permute-done((f32[8,128]{1,0:T(8,128)S(1)}, f32[8,128]{1,0:T(8,128)S(1)}, u32[]{:S(2)}, u32[]{:S(2)}) %collective-permute-start.12) | collective-permute-done | bytes 4128 | tf_op jit(solution)/shard_map/ppermute | solution.py:408
  64.7 2.7 %collective-permute-start.13 = (f32[8,128]{1,0:T(8,128)S(1)}, f32[8,128]{1,0:T(8,128)S(1)}, u32[]{:S(2)}, u32[]{:S(2)}) collective-permute-start(f32[8,128]{1,0:T(8,128)S(1)} %add.22), channel_id=1, source_target_pairs={{0,6},{1,7},{2,4},{3,5},{4,2},{5,3},{6,0},{7,1},{8,14},{9,15},{10,... | collective-permute-start | bytes 12296 | tf_op jit(solution)/shard_map/ppermute | solution.py:408
  67.4 1.3 %collective-permute-done.13 = f32[8,128]{1,0:T(8,128)S(1)} collective-permute-done((f32[8,128]{1,0:T(8,128)S(1)}, f32[8,128]{1,0:T(8,128)S(1)}, u32[]{:S(2)}, u32[]{:S(2)}) %collective-permute-start.13) | collective-permute-done | bytes 4128 | tf_op jit(solution)/shard_map/ppermute | solution.py:408
  68.7 3.0 %factor_apply.1 = (f32[32,16384]{1,0:T(8,128)}, f32[32,32]{1,0:T(8,128)}) custom-call(f32[8,128]{1,0:T(8,128)S(1)} %add.23.gram_ref, f32[32,10240]{1,0:T(8,128)S(1)} %get-tuple-element.46.refs_0_, f32[32,6144]{1,0:T(8,128)S(1)} %get-tuple-element.47.refs_1_), custom_call_target="tpu_custom_call" | custom-call | flops 201326592 | bytes 4194304 | tf_op jit(solution)/shard_map/factor_apply/pallas_call | solution.py:550
  (26 shorter events, 4.9 us)
Async XLA Ops:
  0.6 14.6 %collective-permute-start.1 = (f32[32,16384]{1,0:T(8,128)}, f32[32,16384]{1,0:T(8,128)}, u32[]{:S(2)}, u32[]{:S(2)}) collective-permute-start(f32[32,16384]{1,0:T(8,128)} %own_ref), channel_id=1, source_target_pairs={{0,4},{1,5},{2,6},{3,7},{4,0},{5,1},{6,2},{7,3},{8,12},{9,13},{10,... | collective-permute-start | bytes 6291464 | tf_op jit(solution)/shard_map/ppermute | solution.py:408
  3.5 7.6 %copy-start = (f32[32,16384]{1,0:T(8,128)S(1)}, f32[32,16384]{1,0:T(8,128)}, u32[]{:S(2)}) copy-start(f32[32,16384]{1,0:T(8,128)} %own_ref) | copy-start | bytes 6291460
  3.5 7.6 %copy-start.2 = (s32[18]{0:T(128)S(1)}, s32[18]{0:T(128)}, u32[]{:S(2)}) copy-start(s32[18]{0:T(128)} %bond_ref.17) | copy-start | bytes 220
  3.5 7.6 %copy-start.3 = (s32[19]{0:T(128)S(1)}, s32[19]{0:T(128)}, u32[]{:S(2)}) copy-start(s32[19]{0:T(128)} %field_ref.1) | copy-start | bytes 232
  3.5 18.4 %collective-permute-start = (f32[32,10240]{1,0:T(8,128)}, f32[32,10240]{1,0:T(8,128)S(1)}, u32[]{:S(2)}, u32[]{:S(2)}) collective-permute-start(f32[32,10240]{1,0:T(8,128)} %cut_0.1), channel_id=1, source_target_pairs={{0,4},{1,0},{2,1},{3,2},{4,5},{5,6},{6,7},{7,3},{8,12},{9,8},{10,9... | collective-permute-start | bytes 3932168 | tf_op jit(solution)/shard_map/ppermute | solution.py:408
  3.6 21.1 %collective-permute-start.5 = (f32[32,10240]{1,0:T(8,128)}, f32[32,10240]{1,0:T(8,128)}, u32[]{:S(2)}, u32[]{:S(2)}) collective-permute-start(f32[32,10240]{1,0:T(8,128)} %cut_0.1), channel_id=1, source_target_pairs={{8,4},{9,5},{10,6},{11,7},{12,28},{13,29},{14,30},{15,31},{16,0},{... | collective-permute-start | bytes 3932168 | tf_op jit(solution)/shard_map/ppermute | solution.py:408
  7.2 23.3 %collective-permute-start.2 = (f32[32,6144]{1,0:T(8,128)}, f32[32,6144]{1,0:T(8,128)}, u32[]{:S(2)}, u32[]{:S(2)}) collective-permute-start(f32[32,6144]{1,0:T(8,128)} %cut_10240.1), channel_id=1, source_target_pairs={{0,4},{1,0},{2,1},{3,2},{4,5},{5,6},{6,7},{7,3},{8,12},{9,8},{10,9... | collective-permute-start | bytes 2359304 | tf_op jit(solution)/shard_map/ppermute | solution.py:408
  9.8 24.0 %collective-permute-start.7 = (f32[32,6144]{1,0:T(8,128)}, f32[32,6144]{1,0:T(8,128)}, u32[]{:S(2)}, u32[]{:S(2)}) collective-permute-start(f32[32,6144]{1,0:T(8,128)} %cut_10240.1), channel_id=1, source_target_pairs={{8,4},{9,5},{10,6},{11,7},{12,28},{13,29},{14,30},{15,31},{16,0},{... | collective-permute-start | bytes 2359304 | tf_op jit(solution)/shard_map/ppermute | solution.py:408
  11.1 1.6 %copy-start.1 = (f32[32,16384]{1,0:T(8,128)S(1)}, f32[32,16384]{1,0:T(8,128)}, u32[]{:S(2)}) copy-start(f32[32,16384]{1,0:T(8,128)} %prev_ref.1) | copy-start | bytes 6291460
  22.6 20.9 %collective-permute-start.4 = (f32[32,10240]{1,0:T(8,128)S(1)}, f32[32,10240]{1,0:T(8,128)S(1)}, u32[]{:S(2)}, u32[]{:S(2)}) collective-permute-start(f32[32,10240]{1,0:T(8,128)S(1)} %sent_on_0.1), channel_id=1, source_target_pairs={{0,1},{1,4},{2,5},{3,7},{4,0},{5,2},{6,3},{7,6},{8,9},{9,12},{10,1... | collective-permute-start | bytes 3932168 | tf_op jit(solution)/shard_map/ppermute | solution.py:408
  26.2 18.5 %collective-permute-start.6 = (f32[32,10240]{1,0:T(8,128)S(1)}, f32[32,10240]{1,0:T(8,128)S(1)}, u32[]{:S(2)}, u32[]{:S(2)}) collective-permute-start(f32[32,10240]{1,0:T(8,128)S(1)} %sent_3_0.1), channel_id=1, source_target_pairs={{0,8},{1,9},{2,10},{3,11},{4,16},{5,17},{6,18},{7,19},{24,12},{25,... | collective-permute-start | bytes 3932168 | tf_op jit(solution)/shard_map/ppermute | solution.py:408
  31.7 20.2 %collective-permute-start.3 = (f32[32,6144]{1,0:T(8,128)S(1)}, f32[32,6144]{1,0:T(8,128)S(1)}, u32[]{:S(2)}, u32[]{:S(2)}) collective-permute-start(f32[32,6144]{1,0:T(8,128)S(1)} %sent_on_20.1), channel_id=1, source_target_pairs={{0,1},{1,4},{2,5},{3,7},{4,0},{5,2},{6,3},{7,6},{8,9},{9,12},{10,1... | collective-permute-start | bytes 2359304 | tf_op jit(solution)/shard_map/ppermute | solution.py:408
  35.0 18.1 %collective-permute-start.8 = (f32[32,6144]{1,0:T(8,128)S(1)}, f32[32,6144]{1,0:T(8,128)S(1)}, u32[]{:S(2)}, u32[]{:S(2)}) collective-permute-start(f32[32,6144]{1,0:T(8,128)S(1)} %sent_3_20.1), channel_id=1, source_target_pairs={{0,8},{1,9},{2,10},{3,11},{4,16},{5,17},{6,18},{7,19},{24,12},{25,... | collective-permute-start | bytes 2359304 | tf_op jit(solution)/shard_map/ppermute | solution.py:408
  53.9 1.2 %collective-permute-start.9 = (f32[8,128]{1,0:T(8,128)S(1)}, f32[8,128]{1,0:T(8,128)S(1)}, u32[]{:S(2)}, u32[]{:S(2)}) collective-permute-start(f32[8,128]{1,0:T(8,128)S(1)} %get-tuple-element.45), channel_id=1, source_target_pairs={{0,4},{1,5},{2,6},{3,7},{4,0},{5,1},{6,2},{7,3},{8,12},{9,13},{10,... | collective-permute-start | bytes 12296 | tf_op jit(solution)/shard_map/ppermute | solution.py:408
  55.0 3.6 %collective-permute-start.10 = (f32[8,128]{1,0:T(8,128)S(1)}, f32[8,128]{1,0:T(8,128)S(1)}, u32[]{:S(2)}, u32[]{:S(2)}) collective-permute-start(f32[8,128]{1,0:T(8,128)S(1)} %add.19), channel_id=1, source_target_pairs={{0,12},{1,13},{2,14},{3,15},{4,8},{5,9},{6,10},{7,11},{8,4},{9,5},... | collective-permute-start | bytes 12296 | tf_op jit(solution)/shard_map/ppermute | solution.py:408
  58.6 3.0 %collective-permute-start.11 = (f32[8,128]{1,0:T(8,128)S(1)}, f32[8,128]{1,0:T(8,128)S(1)}, u32[]{:S(2)}, u32[]{:S(2)}) collective-permute-start(f32[8,128]{1,0:T(8,128)S(1)} %add.20), channel_id=1, source_target_pairs={{0,20},{1,21},{2,22},{3,23},{4,16},{5,17},{6,18},{7,19},{8,28},{9,... | collective-permute-start | bytes 12296 | tf_op jit(solution)/shard_map/ppermute | solution.py:408
  61.7 3.0 %collective-permute-start.12 = (f32[8,128]{1,0:T(8,128)S(1)}, f32[8,128]{1,0:T(8,128)S(1)}, u32[]{:S(2)}, u32[]{:S(2)}) collective-permute-start(f32[8,128]{1,0:T(8,128)S(1)} %add.21), channel_id=1, source_target_pairs={{0,5},{1,4},{2,7},{3,6},{4,1},{5,0},{6,3},{7,2},{8,13},{9,12},{10,... | collective-permute-start | bytes 12296 | tf_op jit(solution)/shard_map/ppermute | solution.py:408
  64.7 4.0 %collective-permute-start.13 = (f32[8,128]{1,0:T(8,128)S(1)}, f32[8,128]{1,0:T(8,128)S(1)}, u32[]{:S(2)}, u32[]{:S(2)}) collective-permute-start(f32[8,128]{1,0:T(8,128)S(1)} %add.22), channel_id=1, source_target_pairs={{0,6},{1,7},{2,4},{3,5},{4,2},{5,3},{6,0},{7,1},{8,14},{9,15},{10,... | collective-permute-start | bytes 12296 | tf_op jit(solution)/shard_map/ppermute | solution.py:408

commit v6 on v5

--- a/solution.py
+++ b/solution.py
@@ -197,27 +197,39 @@
         out_ref[:, t * LANES : (t + 1) * LANES] = total
 
 
-def cut_kernel(x_ref, out_ref, sems, *, start):
-    rows, width = out_ref.shape
-    copies = []
-    for k in range(rows // SUBLANES):
-        strip = pl.ds(k * SUBLANES, SUBLANES)
-        copies.append(
-            pltpu.make_async_copy(x_ref.at[strip, pl.ds(start, width)], out_ref.at[strip], sems.at[k])
-        )
-        copies[-1].start()
-    for copy in copies:
-        copy.wait()
+def cut_kernel(x_ref, out_ref, held_ref, in_sems, out_sems, *, start):
+    rows, width = held_ref.shape
+    strips = [pl.ds(k * SUBLANES, SUBLANES) for k in range(rows // SUBLANES)]
+    loads = [
+        pltpu.make_async_copy(x_ref.at[strip, pl.ds(start, width)], held_ref.at[strip], in_sems.at[k])
+        for k, strip in enumerate(strips)
+    ]
+    stores = [
+        pltpu.make_async_copy(held_ref.at[strip], out_ref.at[strip], out_sems.at[k]) for k, strip in enumerate(strips)
+    ]
+    for load in loads:
+        load.start()
+    for load, store in zip(loads, stores):
+        load.wait()
+        store.start()
+    for store in stores:
+        store.wait()
 
 
 def cut(values, start, width):
     rows = values.shape[0]
+    hbm = pl.BlockSpec(memory_space=pltpu.HBM)
+    strips = rows // SUBLANES
     return pl.pallas_call(
         functools.partial(cut_kernel, start=start),
         out_shape=jax.ShapeDtypeStruct((rows, width), values.dtype),
-        in_specs=[pl.BlockSpec(memory_space=pltpu.HBM)],
-        out_specs=pl.BlockSpec(memory_space=pltpu.VMEM),
-        scratch_shapes=[pltpu.SemaphoreType.DMA((rows // SUBLANES,))],
+        in_specs=[hbm],
+        out_specs=hbm,
+        scratch_shapes=[
+            pltpu.VMEM((rows, width), values.dtype),
+            pltpu.SemaphoreType.DMA((strips,)),
+            pltpu.SemaphoreType.DMA((strips,)),
+        ],
         compiler_params=params(CUT_LIMIT),
         cost_estimate=cost(0, 8 * rows * width),
         name=f"cut_{start}",
@@ -542,9 +554,14 @@
     gram = products
 
     hub = 1 << lo_bits
-    gram = gram + permute(gram, flips(hub))
-    for k in [k for k in range(global_bits) if k > lo_bits] + list(range(lo_bits)):
-        gram = gram + permute(gram, flips(1 << k | hub))
+    upper = [1 << k for k in range(lo_bits + 1, global_bits)]
+    steps = [[hub]]
+    if len(upper) > 1:
+        steps.append([upper[0] | hub, upper[1] | hub, upper[0] | upper[1] | hub])
+        upper = upper[2:]
+    steps += [[mask | hub] for mask in upper + [1 << k for k in range(lo_bits)]]
+    for masks in steps:
+        gram = gram + sum(permute(gram, flips(mask)) for mask in masks)
 
     chunks = sum(-(-values.shape[1] // OUT_CHUNK) for values in filtered)
     return pl.pallas_call(

time: 72.2 us -> 71.7 us (level)
    ppermute x14 -> x15, waiting for transfers between devices: 21.5 us -> 21.4 us  [permute(): return lax.ppermute(values, AXES, pairs)]
    ppermute x14 -> x15, starting transfers between devices: 24.7 us -> 24.7 us  [permute(): return lax.ppermute(values, AXES, pairs)]
  transfers between devices with their start and end apart: 14 -> 15, of which waited for: 11 -> 11; matrix products, arithmetic and copies ran while one was open for 0% -> 0% of each run, Pallas kernels for 27% -> 26%
where the time goes in v6:
time: 71.7 us; the launch traced here: 71.2 us
  starting transfers between devices  24.7 us (34%)
  Pallas kernels  22.6 us (32%)
  waiting for transfers between devices  21.4 us (30%)
  local copies, waits for them, and re-layouts  1.61 us (2%)
  between operations  0.85 us (1%)
    ppermute x15, starting transfers between devices, permute(): return lax.ppermute(values, AXES, pairs)  24.7 us
    ppermute x15, waiting for transfers between devices, permute(): return lax.ppermute(values, AXES, pairs)  21.4 us
    pallas_call x2, Pallas kernels, cut(): pl.pallas_call(functools.partial(cut_kernel, start=start), out_shape=jax....  4.05 us
    pallas_call x2, Pallas kernels, local(): pl.pallas_call(functools.partial(gather_kernel, start=start * width // LA...  3.14 us
    pallas_call x1, Pallas kernels, local(): pl.pallas_call(finish_kernel, out_shape=(whole, jax.ShapeDtypeStruct((vec...  3 us
    pallas_call x2, Pallas kernels, local(): pl.pallas_call(functools.partial(later_sent_kernel, bond=local_bits + m,...  2.68 us
    pallas_call x1, Pallas kernels, local(): pl.pallas_call(functools.partial(local_kernel, global_bits=global_bits, s...  2.49 us
    pallas_call x1, Pallas kernels, local(): pl.pallas_call(functools.partial(ready_kernel, bit=rest_bits - 1, bond=lo...  1.97 us
  transfers between devices with their start and end apart: 15, of which 11 were waited for; matrix products, arithmetic and copies ran while one was open for 0% of the time, Pallas kernels for 26%

profile of v6, /device:TPU:0, one launch (start us, length us, event | category | flops | bytes accessed | tf_op | source)
XLA Modules:
  0.0 71.2 jit_solution(8479240550459465496)
XLA Ops:
  1.1 2.1 %cut_0.1 = f32[32,10240]{1,0:T(8,128)} custom-call(f32[32,16384]{1,0:T(8,128)} %own_ref), custom_call_target="tpu_custom_call" | custom-call | bytes 2621440 | tf_op jit(solution)/shard_map/cut_0/pallas_call | solution.py:223
  3.4 1.4 %collective-permute-start.5 = (f32[32,10240]{1,0:T(8,128)}, f32[32,10240]{1,0:T(8,128)}, u32[]{:S(2)}, u32[]{:S(2)}) collective-permute-start(f32[32,10240]{1,0:T(8,128)} %cut_0.1), channel_id=1, source_target_pairs={{8,4},{9,5},{10,6},{11,7},{12,28},{13,29},{14,30},{15,31},{16,0},{... | collective-permute-start | bytes 3932168 | tf_op jit(solution)/shard_map/ppermute | solution.py:420
  4.8 2.0 %cut_10240.1 = f32[32,6144]{1,0:T(8,128)} custom-call(f32[32,16384]{1,0:T(8,128)} %own_ref), custom_call_target="tpu_custom_call" | custom-call | bytes 1572864 | tf_op jit(solution)/shard_map/cut_10240/pallas_call | solution.py:223
  6.7 2.6 %collective-permute-start.2 = (f32[32,6144]{1,0:T(8,128)}, f32[32,6144]{1,0:T(8,128)}, u32[]{:S(2)}, u32[]{:S(2)}) collective-permute-start(f32[32,6144]{1,0:T(8,128)} %cut_10240.1), channel_id=1, source_target_pairs={{0,4},{1,0},{2,1},{3,2},{4,5},{5,6},{6,7},{7,3},{8,12},{9,8},{10,9... | collective-permute-start | bytes 2359304 | tf_op jit(solution)/shard_map/ppermute | solution.py:420
  9.4 1.3 %collective-permute-start.7 = (f32[32,6144]{1,0:T(8,128)}, f32[32,6144]{1,0:T(8,128)}, u32[]{:S(2)}, u32[]{:S(2)}) collective-permute-start(f32[32,6144]{1,0:T(8,128)} %cut_10240.1), channel_id=1, source_target_pairs={{8,4},{9,5},{10,6},{11,7},{12,28},{13,29},{14,30},{15,31},{16,0},{... | collective-permute-start | bytes 2359304 | tf_op jit(solution)/shard_map/ppermute | solution.py:420
  10.7 1.6 %copy-done.1 = f32[32,16384]{1,0:T(8,128)S(1)} copy-done((f32[32,16384]{1,0:T(8,128)S(1)}, f32[32,16384]{1,0:T(8,128)}, u32[]{:S(2)}) %copy-start.1) | copy-done | bytes 2097176
  12.3 2.5 %local_bonds.1.local_ref = f32[32,16384]{1,0:T(8,128)S(1)} custom-call(s32[1]{0:T(128)} %bitcast.device_ref, s32[19]{0:T(128)S(1)} %copy-done.3, s32[18]{0:T(128)S(1)} %copy-done.2, f32[32,16384]{1,0:T(8,128)S(1)} %copy-done, f32[32,16384]{1,0:T(8,128)S(1)} %copy-done.1), custom_call_target="tpu_custom_call" | custom-call | flops 805306368 | bytes 6291456 | tf_op jit(solution)/shard_map/local_bonds/pallas_call | solution.py:440
  14.8 1.7 %ready_3.1 = (f32[32,10240]{1,0:T(8,128)S(1)}, f32[32,6144]{1,0:T(8,128)S(1)}) custom-call(s32[1]{0:T(128)} %bitcast.device_ref, s32[18]{0:T(128)S(1)} %copy-done.2, f32[32,16384]{1,0:T(8,128)} %collective-permute-done.1.swap_ref), custom_call_target="tpu_custom_call" | custom-call | flops 524288 | bytes 4194304 | tf_op jit(solution)/shard_map/ready_3/pallas_call | solution.py:459
  16.6 2.0 %ready.1 = (f32[32,10240]{1,0:T(8,128)S(1)}, f32[32,6144]{1,0:T(8,128)S(1)}) custom-call(s32[1]{0:T(128)} %bitcast.device_ref, s32[18]{0:T(128)S(1)} %copy-done.2, f32[32,16384]{1,0:T(8,128)S(1)} %copy-done, f32[32,16384]{1,0:T(8,128)} %collective-permute-done.1.swap_ref), custom_call_target="tpu_custom_call" | custom-call | flops 3145728 | bytes 6291456 | tf_op jit(solution)/shard_map/ready/pallas_call | solution.py:449
  18.5 3.2 %collective-permute-done.arrived_ref.first_ref = f32[32,10240]{1,0:T(8,128)S(1)} collective-permute-done((f32[32,10240]{1,0:T(8,128)}, f32[32,10240]{1,0:T(8,128)S(1)}, u32[]{:S(2)}, u32[]{:S(2)}) %collective-permute-start) | collective-permute-done | bytes 1310752 | tf_op jit(solution)/shard_map/ppermute | solution.py:420
  22.4 2.1 %collective-permute-start.4 = (f32[32,10240]{1,0:T(8,128)S(1)}, f32[32,10240]{1,0:T(8,128)S(1)}, u32[]{:S(2)}, u32[]{:S(2)}) collective-permute-start(f32[32,10240]{1,0:T(8,128)S(1)} %sent_on_0.1), channel_id=1, source_target_pairs={{0,1},{1,4},{2,5},{3,7},{4,0},{5,2},{6,3},{7,6},{8,9},{9,12},{10,1... | collective-permute-start | bytes 3932168 | tf_op jit(solution)/shard_map/ppermute | solution.py:420
  24.4 1.5 %sent_3_0.1 = f32[32,10240]{1,0:T(8,128)S(1)} custom-call(s32[18]{0:T(128)S(1)} %copy-done.2, f32[32,10240]{1,0:T(8,128)S(1)} %get-tuple-element.37.ready_ref, f32[32,10240]{1,0:T(8,128)} %collective-permute-done.5.refs_0_.arrived_ref), custom_call_target="tpu_custom_call" | custom-call | tf_op jit(solution)/shard_map/sent_3_0/pallas_call | solution.py:494
  25.9 3.5 %collective-permute-start.6 = (f32[32,10240]{1,0:T(8,128)S(1)}, f32[32,10240]{1,0:T(8,128)S(1)}, u32[]{:S(2)}, u32[]{:S(2)}) collective-permute-start(f32[32,10240]{1,0:T(8,128)S(1)} %sent_3_0.1), channel_id=1, source_target_pairs={{0,8},{1,9},{2,10},{3,11},{4,16},{5,17},{6,18},{7,19},{24,12},{25,... | collective-permute-start | bytes 3932168 | tf_op jit(solution)/shard_map/ppermute | solution.py:420
  30.2 1.2 %sent_on_20.1 = f32[32,6144]{1,0:T(8,128)S(1)} custom-call(s32[1]{0:T(128)} %bitcast.device_ref, s32[18]{0:T(128)S(1)} %copy-done.2, f32[32,6144]{1,0:T(8,128)S(1)} %get-tuple-element.30.ready_ref, f32[32,6144]{1,0:T(8,128)} %collective-permute-done.2.arrived_ref.first_ref), custom_call_target="tpu_custom_call" | custom-call | tf_op jit(solution)/shard_map/sent_on_20/pallas_call | solution.py:480
  31.4 2.1 %collective-permute-start.3 = (f32[32,6144]{1,0:T(8,128)S(1)}, f32[32,6144]{1,0:T(8,128)S(1)}, u32[]{:S(2)}, u32[]{:S(2)}) collective-permute-start(f32[32,6144]{1,0:T(8,128)S(1)} %sent_on_20.1), channel_id=1, source_target_pairs={{0,1},{1,4},{2,5},{3,7},{4,0},{5,2},{6,3},{7,6},{8,9},{9,12},{10,1... | collective-permute-start | bytes 2359304 | tf_op jit(solution)/shard_map/ppermute | solution.py:420
  33.5 1.2 %sent_3_20.1 = f32[32,6144]{1,0:T(8,128)S(1)} custom-call(s32[18]{0:T(128)S(1)} %copy-done.2, f32[32,6144]{1,0:T(8,128)S(1)} %get-tuple-element.43.ready_ref, f32[32,6144]{1,0:T(8,128)} %collective-permute-done.7.refs_0_.arrived_ref), custom_call_target="tpu_custom_call" | custom-call | tf_op jit(solution)/shard_map/sent_3_20/pallas_call | solution.py:494
  34.8 3.4 %collective-permute-start.8 = (f32[32,6144]{1,0:T(8,128)S(1)}, f32[32,6144]{1,0:T(8,128)S(1)}, u32[]{:S(2)}, u32[]{:S(2)}) collective-permute-start(f32[32,6144]{1,0:T(8,128)S(1)} %sent_3_20.1), channel_id=1, source_target_pairs={{0,8},{1,9},{2,10},{3,11},{4,16},{5,17},{6,18},{7,19},{24,12},{25,... | collective-permute-start | bytes 2359304 | tf_op jit(solution)/shard_map/ppermute | solution.py:420
  38.2 1.5 %gather_first_20.1.one_ref = f32[32,6144]{1,0:T(8,128)S(1)} custom-call(s32[1]{0:T(128)} %bitcast.device_ref, s32[18]{0:T(128)S(1)} %copy-done.2, f32[32,16384]{1,0:T(8,128)S(1)} %local_bonds.1.local_ref, f32[32,6144]{1,0:T(8,128)} %collective-permute-done.2.arrived_ref.first_ref, f32[32,6144]{1,0:T(8,128)} %collective-permute-done.7.refs_0_.arrived_ref), custom_call_target="tpu_custom_call" | custom-call | tf_op jit(solution)/shard_map/gather_first_20/pallas_call | solution.py:510
  39.8 1.6 %gather_first_0.1.one_ref = f32[32,10240]{1,0:T(8,128)S(1)} custom-call(s32[1]{0:T(128)} %bitcast.device_ref, s32[18]{0:T(128)S(1)} %copy-done.2, f32[32,16384]{1,0:T(8,128)S(1)} %local_bonds.1.local_ref, f32[32,10240]{1,0:T(8,128)S(1)} %collective-permute-done.arrived_ref.first_ref, f32[32,10240]{1,0:T(8,128)} %collective-permute-done.5.refs_0_.arrived_ref), custom_call_target="tpu_custom_call" | custom-call | tf_op jit(solution)/shard_map/gather_first_0/pallas_call | solution.py:510
  41.4 1.9 %collective-permute-done.4.two_ref = f32[32,10240]{1,0:T(8,128)S(1)} collective-permute-done((f32[32,10240]{1,0:T(8,128)S(1)}, f32[32,10240]{1,0:T(8,128)S(1)}, u32[]{:S(2)}, u32[]{:S(2)}) %collective-permute-start.4) | collective-permute-done | bytes 1310752 | tf_op jit(solution)/shard_map/ppermute | solution.py:420
  45.1 6.5 %collective-permute-done.3.two_ref = f32[32,6144]{1,0:T(8,128)S(1)} collective-permute-done((f32[32,6144]{1,0:T(8,128)S(1)}, f32[32,6144]{1,0:T(8,128)S(1)}, u32[]{:S(2)}, u32[]{:S(2)}) %collective-permute-start.3) | collective-permute-done | bytes 786464 | tf_op jit(solution)/shard_map/ppermute | solution.py:420
  51.7 1.1 %collective-permute-done.8.refs_0_ = f32[32,6144]{1,0:T(8,128)S(1)} collective-permute-done((f32[32,6144]{1,0:T(8,128)S(1)}, f32[32,6144]{1,0:T(8,128)S(1)}, u32[]{:S(2)}, u32[]{:S(2)}) %collective-permute-start.8) | collective-permute-done | bytes 786464 | tf_op jit(solution)/shard_map/ppermute | solution.py:420
  53.6 1.2 %collective-permute-done.9 = f32[8,128]{1,0:T(8,128)S(1)} collective-permute-done((f32[8,128]{1,0:T(8,128)S(1)}, f32[8,128]{1,0:T(8,128)S(1)}, u32[]{:S(2)}, u32[]{:S(2)}) %collective-permute-start.9) | collective-permute-done | bytes 4128 | tf_op jit(solution)/shard_map/ppermute | solution.py:420
  54.8 2.3 %collective-permute-start.10 = (f32[8,128]{1,0:T(8,128)S(1)}, f32[8,128]{1,0:T(8,128)S(1)}, u32[]{:S(2)}, u32[]{:S(2)}) collective-permute-start(f32[8,128]{1,0:T(8,128)S(1)} %add.22), channel_id=1, source_target_pairs={{0,12},{1,13},{2,14},{3,15},{4,8},{5,9},{6,10},{7,11},{8,4},{9,5},... | collective-permute-start | bytes 12296 | tf_op jit(solution)/shard_map/ppermute | solution.py:420
  57.3 1.2 %collective-permute-start.12 = (f32[8,128]{1,0:T(8,128)S(1)}, f32[8,128]{1,0:T(8,128)S(1)}, u32[]{:S(2)}, u32[]{:S(2)}) collective-permute-start(f32[8,128]{1,0:T(8,128)S(1)} %add.22), channel_id=1, source_target_pairs={{0,28},{1,29},{2,30},{3,31},{4,24},{5,25},{6,26},{7,27},{8,20},{9,... | collective-permute-start | bytes 12296 | tf_op jit(solution)/shard_map/ppermute | solution.py:420
  58.4 1.6 %collective-permute-done.11 = f32[8,128]{1,0:T(8,128)S(1)} collective-permute-done((f32[8,128]{1,0:T(8,128)S(1)}, f32[8,128]{1,0:T(8,128)S(1)}, u32[]{:S(2)}, u32[]{:S(2)}) %collective-permute-start.11) | collective-permute-done | bytes 4128 | tf_op jit(solution)/shard_map/ppermute | solution.py:420
  60.1 1.1 %collective-permute-done.12 = f32[8,128]{1,0:T(8,128)S(1)} collective-permute-done((f32[8,128]{1,0:T(8,128)S(1)}, f32[8,128]{1,0:T(8,128)S(1)}, u32[]{:S(2)}, u32[]{:S(2)}) %collective-permute-start.12) | collective-permute-done | bytes 4128 | tf_op jit(solution)/shard_map/ppermute | solution.py:420
  61.2 1.5 %collective-permute-start.13 = (f32[8,128]{1,0:T(8,128)S(1)}, f32[8,128]{1,0:T(8,128)S(1)}, u32[]{:S(2)}, u32[]{:S(2)}) collective-permute-start(f32[8,128]{1,0:T(8,128)S(1)} %add_add_fusion), channel_id=1, source_target_pairs={{0,5},{1,4},{2,7},{3,6},{4,1},{5,0},{6,3},{7,2},{8,13},{9,12},{10,... | collective-permute-start | bytes 12296 | tf_op jit(solution)/shard_map/ppermute | solution.py:420
  62.7 1.5 %collective-permute-done.13 = f32[8,128]{1,0:T(8,128)S(1)} collective-permute-done((f32[8,128]{1,0:T(8,128)S(1)}, f32[8,128]{1,0:T(8,128)S(1)}, u32[]{:S(2)}, u32[]{:S(2)}) %collective-permute-start.13) | collective-permute-done | bytes 4128 | tf_op jit(solution)/shard_map/ppermute | solution.py:420
  64.2 2.5 %collective-permute-start.14 = (f32[8,128]{1,0:T(8,128)S(1)}, f32[8,128]{1,0:T(8,128)S(1)}, u32[]{:S(2)}, u32[]{:S(2)}) collective-permute-start(f32[8,128]{1,0:T(8,128)S(1)} %add.26), channel_id=1, source_target_pairs={{0,6},{1,7},{2,4},{3,5},{4,2},{5,3},{6,0},{7,1},{8,14},{9,15},{10,... | collective-permute-start | bytes 12296 | tf_op jit(solution)/shard_map/ppermute | solution.py:420
  66.8 1.4 %collective-permute-done.14 = f32[8,128]{1,0:T(8,128)S(1)} collective-permute-done((f32[8,128]{1,0:T(8,128)S(1)}, f32[8,128]{1,0:T(8,128)S(1)}, u32[]{:S(2)}, u32[]{:S(2)}) %collective-permute-start.14) | collective-permute-done | bytes 4128 | tf_op jit(solution)/shard_map/ppermute | solution.py:420
  68.2 3.0 %factor_apply.1 = (f32[32,16384]{1,0:T(8,128)}, f32[32,32]{1,0:T(8,128)}) custom-call(f32[8,128]{1,0:T(8,128)S(1)} %add.27.gram_ref, f32[32,10240]{1,0:T(8,128)S(1)} %get-tuple-element.46.refs_0_, f32[32,6144]{1,0:T(8,128)S(1)} %get-tuple-element.47.refs_1_), custom_call_target="tpu_custom_call" | custom-call | flops 201326592 | bytes 4194304 | tf_op jit(solution)/shard_map/factor_apply/pallas_call | solution.py:567
  (27 shorter events, 5.1 us)
Async XLA Ops:
  0.6 14.2 %collective-permute-start.1 = (f32[32,16384]{1,0:T(8,128)}, f32[32,16384]{1,0:T(8,128)}, u32[]{:S(2)}, u32[]{:S(2)}) collective-permute-start(f32[32,16384]{1,0:T(8,128)} %own_ref), channel_id=1, source_target_pairs={{0,4},{1,5},{2,6},{3,7},{4,0},{5,1},{6,2},{7,3},{8,12},{9,13},{10,... | collective-permute-start | bytes 6291464 | tf_op jit(solution)/shard_map/ppermute | solution.py:420
  3.2 7.4 %copy-start = (f32[32,16384]{1,0:T(8,128)S(1)}, f32[32,16384]{1,0:T(8,128)}, u32[]{:S(2)}) copy-start(f32[32,16384]{1,0:T(8,128)} %own_ref) | copy-start | bytes 6291460
  3.3 7.4 %copy-start.2 = (s32[18]{0:T(128)S(1)}, s32[18]{0:T(128)}, u32[]{:S(2)}) copy-start(s32[18]{0:T(128)} %bond_ref.17) | copy-start | bytes 220
  3.3 7.4 %copy-start.3 = (s32[19]{0:T(128)S(1)}, s32[19]{0:T(128)}, u32[]{:S(2)}) copy-start(s32[19]{0:T(128)} %field_ref.1) | copy-start | bytes 232
  3.3 18.4 %collective-permute-start = (f32[32,10240]{1,0:T(8,128)}, f32[32,10240]{1,0:T(8,128)S(1)}, u32[]{:S(2)}, u32[]{:S(2)}) collective-permute-start(f32[32,10240]{1,0:T(8,128)} %cut_0.1), channel_id=1, source_target_pairs={{0,4},{1,0},{2,1},{3,2},{4,5},{5,6},{6,7},{7,3},{8,12},{9,8},{10,9... | collective-permute-start | bytes 3932168 | tf_op jit(solution)/shard_map/ppermute | solution.py:420
  3.4 21.1 %collective-permute-start.5 = (f32[32,10240]{1,0:T(8,128)}, f32[32,10240]{1,0:T(8,128)}, u32[]{:S(2)}, u32[]{:S(2)}) collective-permute-start(f32[32,10240]{1,0:T(8,128)} %cut_0.1), channel_id=1, source_target_pairs={{8,4},{9,5},{10,6},{11,7},{12,28},{13,29},{14,30},{15,31},{16,0},{... | collective-permute-start | bytes 3932168 | tf_op jit(solution)/shard_map/ppermute | solution.py:420
  6.7 23.5 %collective-permute-start.2 = (f32[32,6144]{1,0:T(8,128)}, f32[32,6144]{1,0:T(8,128)}, u32[]{:S(2)}, u32[]{:S(2)}) collective-permute-start(f32[32,6144]{1,0:T(8,128)} %cut_10240.1), channel_id=1, source_target_pairs={{0,4},{1,0},{2,1},{3,2},{4,5},{5,6},{6,7},{7,3},{8,12},{9,8},{10,9... | collective-permute-start | bytes 2359304 | tf_op jit(solution)/shard_map/ppermute | solution.py:420
  9.4 24.1 %collective-permute-start.7 = (f32[32,6144]{1,0:T(8,128)}, f32[32,6144]{1,0:T(8,128)}, u32[]{:S(2)}, u32[]{:S(2)}) collective-permute-start(f32[32,6144]{1,0:T(8,128)} %cut_10240.1), channel_id=1, source_target_pairs={{8,4},{9,5},{10,6},{11,7},{12,28},{13,29},{14,30},{15,31},{16,0},{... | collective-permute-start | bytes 2359304 | tf_op jit(solution)/shard_map/ppermute | solution.py:420
  10.7 1.6 %copy-start.1 = (f32[32,16384]{1,0:T(8,128)S(1)}, f32[32,16384]{1,0:T(8,128)}, u32[]{:S(2)}) copy-start(f32[32,16384]{1,0:T(8,128)} %prev_ref.1) | copy-start | bytes 6291460
  22.4 20.9 %collective-permute-start.4 = (f32[32,10240]{1,0:T(8,128)S(1)}, f32[32,10240]{1,0:T(8,128)S(1)}, u32[]{:S(2)}, u32[]{:S(2)}) collective-permute-start(f32[32,10240]{1,0:T(8,128)S(1)} %sent_on_0.1), channel_id=1, source_target_pairs={{0,1},{1,4},{2,5},{3,7},{4,0},{5,2},{6,3},{7,6},{8,9},{9,12},{10,1... | collective-permute-start | bytes 3932168 | tf_op jit(solution)/shard_map/ppermute | solution.py:420
  25.9 18.5 %collective-permute-start.6 = (f32[32,10240]{1,0:T(8,128)S(1)}, f32[32,10240]{1,0:T(8,128)S(1)}, u32[]{:S(2)}, u32[]{:S(2)}) collective-permute-start(f32[32,10240]{1,0:T(8,128)S(1)} %sent_3_0.1), channel_id=1, source_target_pairs={{0,8},{1,9},{2,10},{3,11},{4,16},{5,17},{6,18},{7,19},{24,12},{25,... | collective-permute-start | bytes 3932168 | tf_op jit(solution)/shard_map/ppermute | solution.py:420
  31.4 20.2 %collective-permute-start.3 = (f32[32,6144]{1,0:T(8,128)S(1)}, f32[32,6144]{1,0:T(8,128)S(1)}, u32[]{:S(2)}, u32[]{:S(2)}) collective-permute-start(f32[32,6144]{1,0:T(8,128)S(1)} %sent_on_20.1), channel_id=1, source_target_pairs={{0,1},{1,4},{2,5},{3,7},{4,0},{5,2},{6,3},{7,6},{8,9},{9,12},{10,1... | collective-permute-start | bytes 2359304 | tf_op jit(solution)/shard_map/ppermute | solution.py:420
  34.8 18.1 %collective-permute-start.8 = (f32[32,6144]{1,0:T(8,128)S(1)}, f32[32,6144]{1,0:T(8,128)S(1)}, u32[]{:S(2)}, u32[]{:S(2)}) collective-permute-start(f32[32,6144]{1,0:T(8,128)S(1)} %sent_3_20.1), channel_id=1, source_target_pairs={{0,8},{1,9},{2,10},{3,11},{4,16},{5,17},{6,18},{7,19},{24,12},{25,... | collective-permute-start | bytes 2359304 | tf_op jit(solution)/shard_map/ppermute | solution.py:420
  53.6 1.2 %collective-permute-start.9 = (f32[8,128]{1,0:T(8,128)S(1)}, f32[8,128]{1,0:T(8,128)S(1)}, u32[]{:S(2)}, u32[]{:S(2)}) collective-permute-start(f32[8,128]{1,0:T(8,128)S(1)} %get-tuple-element.45), channel_id=1, source_target_pairs={{0,4},{1,5},{2,6},{3,7},{4,0},{5,1},{6,2},{7,3},{8,12},{9,13},{10,... | collective-permute-start | bytes 12296 | tf_op jit(solution)/shard_map/ppermute | solution.py:420
  54.8 3.7 %collective-permute-start.10 = (f32[8,128]{1,0:T(8,128)S(1)}, f32[8,128]{1,0:T(8,128)S(1)}, u32[]{:S(2)}, u32[]{:S(2)}) collective-permute-start(f32[8,128]{1,0:T(8,128)S(1)} %add.22), channel_id=1, source_target_pairs={{0,12},{1,13},{2,14},{3,15},{4,8},{5,9},{6,10},{7,11},{8,4},{9,5},... | collective-permute-start | bytes 12296 | tf_op jit(solution)/shard_map/ppermute | solution.py:420
  57.0 3.0 %collective-permute-start.11 = (f32[8,128]{1,0:T(8,128)S(1)}, f32[8,128]{1,0:T(8,128)S(1)}, u32[]{:S(2)}, u32[]{:S(2)}) collective-permute-start(f32[8,128]{1,0:T(8,128)S(1)} %add.22), channel_id=1, source_target_pairs={{0,20},{1,21},{2,22},{3,23},{4,16},{5,17},{6,18},{7,19},{8,28},{9,... | collective-permute-start | bytes 12296 | tf_op jit(solution)/shard_map/ppermute | solution.py:420
  57.3 3.9 %collective-permute-start.12 = (f32[8,128]{1,0:T(8,128)S(1)}, f32[8,128]{1,0:T(8,128)S(1)}, u32[]{:S(2)}, u32[]{:S(2)}) collective-permute-start(f32[8,128]{1,0:T(8,128)S(1)} %add.22), channel_id=1, source_target_pairs={{0,28},{1,29},{2,30},{3,31},{4,24},{5,25},{6,26},{7,27},{8,20},{9,... | collective-permute-start | bytes 12296 | tf_op jit(solution)/shard_map/ppermute | solution.py:420
  61.2 3.0 %collective-permute-start.13 = (f32[8,128]{1,0:T(8,128)S(1)}, f32[8,128]{1,0:T(8,128)S(1)}, u32[]{:S(2)}, u32[]{:S(2)}) collective-permute-start(f32[8,128]{1,0:T(8,128)S(1)} %add_add_fusion), channel_id=1, source_target_pairs={{0,5},{1,4},{2,7},{3,6},{4,1},{5,0},{6,3},{7,2},{8,13},{9,12},{10,... | collective-permute-start | bytes 12296 | tf_op jit(solution)/shard_map/ppermute | solution.py:420
  64.2 3.9 %collective-permute-start.14 = (f32[8,128]{1,0:T(8,128)S(1)}, f32[8,128]{1,0:T(8,128)S(1)}, u32[]{:S(2)}, u32[]{:S(2)}) collective-permute-start(f32[8,128]{1,0:T(8,128)S(1)} %add.26), channel_id=1, source_target_pairs={{0,6},{1,7},{2,4},{3,5},{4,2},{5,3},{6,0},{7,1},{8,14},{9,15},{10,... | collective-permute-start | bytes 12296 | tf_op jit(solution)/shard_map/ppermute | solution.py:420

commit v7 on v6

--- a/solution.py
+++ b/solution.py
@@ -535,7 +535,7 @@
             in_specs=[vmem] * 2,
             out_specs=vmem,
             compiler_params=params(),
-            cost_estimate=cost(ADD_COST, 0),
+            cost_estimate=cost(0 if last else ADD_COST, 0),
             name=f"add_{start}",
         )(acc, second)
         done, products = pl.pallas_call(

time: 71.7 us -> 71.7 us (level)
  no operation moved by 1% of the time
where the time goes in v7:
time: 71.7 us; the launch traced here: 71.2 us
  starting transfers between devices  24.7 us (34%)
  Pallas kernels  22.6 us (32%)
  waiting for transfers between devices  21.4 us (30%)
  local copies, waits for them, and re-layouts  1.61 us (2%)
  between operations  0.85 us (1%)
    ppermute x15, starting transfers between devices, permute(): return lax.ppermute(values, AXES, pairs)  24.7 us
    ppermute x15, waiting for transfers between devices, permute(): return lax.ppermute(values, AXES, pairs)  21.4 us
    pallas_call x2, Pallas kernels, cut(): pl.pallas_call(functools.partial(cut_kernel, start=start), out_shape=jax....  4.05 us
    pallas_call x2, Pallas kernels, local(): pl.pallas_call(functools.partial(gather_kernel, start=start * width // LA...  3.14 us
    pallas_call x1, Pallas kernels, local(): pl.pallas_call(finish_kernel, out_shape=(whole, jax.ShapeDtypeStruct((vec...  3 us
    pallas_call x2, Pallas kernels, local(): pl.pallas_call(functools.partial(later_sent_kernel, bond=local_bits + m,...  2.68 us
    pallas_call x1, Pallas kernels, local(): pl.pallas_call(functools.partial(local_kernel, global_bits=global_bits, s...  2.49 us
    pallas_call x1, Pallas kernels, local(): pl.pallas_call(functools.partial(ready_kernel, bit=rest_bits - 1, bond=lo...  1.97 us
  transfers between devices with their start and end apart: 15, of which 11 were waited for; matrix products, arithmetic and copies ran while one was open for 0% of the time, Pallas kernels for 26%

profile of v7, /device:TPU:0, one launch (start us, length us, event | category | flops | bytes accessed | tf_op | source)
XLA Modules:
  0.0 71.2 jit_solution(8479240550459465496)
XLA Ops:
  1.1 2.1 %cut_0.1 = f32[32,10240]{1,0:T(8,128)} custom-call(f32[32,16384]{1,0:T(8,128)} %own_ref), custom_call_target="tpu_custom_call" | custom-call | bytes 2621440 | tf_op jit(solution)/shard_map/cut_0/pallas_call | solution.py:223
  3.4 1.4 %collective-permute-start.5 = (f32[32,10240]{1,0:T(8,128)}, f32[32,10240]{1,0:T(8,128)}, u32[]{:S(2)}, u32[]{:S(2)}) collective-permute-start(f32[32,10240]{1,0:T(8,128)} %cut_0.1), channel_id=1, source_target_pairs={{8,4},{9,5},{10,6},{11,7},{12,28},{13,29},{14,30},{15,31},{16,0},{... | collective-permute-start | bytes 3932168 | tf_op jit(solution)/shard_map/ppermute | solution.py:420
  4.8 2.0 %cut_10240.1 = f32[32,6144]{1,0:T(8,128)} custom-call(f32[32,16384]{1,0:T(8,128)} %own_ref), custom_call_target="tpu_custom_call" | custom-call | bytes 1572864 | tf_op jit(solution)/shard_map/cut_10240/pallas_call | solution.py:223
  6.7 2.6 %collective-permute-start.2 = (f32[32,6144]{1,0:T(8,128)}, f32[32,6144]{1,0:T(8,128)}, u32[]{:S(2)}, u32[]{:S(2)}) collective-permute-start(f32[32,6144]{1,0:T(8,128)} %cut_10240.1), channel_id=1, source_target_pairs={{0,4},{1,0},{2,1},{3,2},{4,5},{5,6},{6,7},{7,3},{8,12},{9,8},{10,9... | collective-permute-start | bytes 2359304 | tf_op jit(solution)/shard_map/ppermute | solution.py:420
  9.4 1.3 %collective-permute-start.7 = (f32[32,6144]{1,0:T(8,128)}, f32[32,6144]{1,0:T(8,128)}, u32[]{:S(2)}, u32[]{:S(2)}) collective-permute-start(f32[32,6144]{1,0:T(8,128)} %cut_10240.1), channel_id=1, source_target_pairs={{8,4},{9,5},{10,6},{11,7},{12,28},{13,29},{14,30},{15,31},{16,0},{... | collective-permute-start | bytes 2359304 | tf_op jit(solution)/shard_map/ppermute | solution.py:420
  10.7 1.6 %copy-done.1 = f32[32,16384]{1,0:T(8,128)S(1)} copy-done((f32[32,16384]{1,0:T(8,128)S(1)}, f32[32,16384]{1,0:T(8,128)}, u32[]{:S(2)}) %copy-start.1) | copy-done | bytes 2097176
  12.3 2.5 %local_bonds.1.local_ref = f32[32,16384]{1,0:T(8,128)S(1)} custom-call(s32[1]{0:T(128)} %bitcast.device_ref, s32[19]{0:T(128)S(1)} %copy-done.3, s32[18]{0:T(128)S(1)} %copy-done.2, f32[32,16384]{1,0:T(8,128)S(1)} %copy-done, f32[32,16384]{1,0:T(8,128)S(1)} %copy-done.1), custom_call_target="tpu_custom_call" | custom-call | flops 805306368 | bytes 6291456 | tf_op jit(solution)/shard_map/local_bonds/pallas_call | solution.py:440
  14.8 1.7 %ready_3.1 = (f32[32,10240]{1,0:T(8,128)S(1)}, f32[32,6144]{1,0:T(8,128)S(1)}) custom-call(s32[1]{0:T(128)} %bitcast.device_ref, s32[18]{0:T(128)S(1)} %copy-done.2, f32[32,16384]{1,0:T(8,128)} %collective-permute-done.1.swap_ref), custom_call_target="tpu_custom_call" | custom-call | flops 524288 | bytes 4194304 | tf_op jit(solution)/shard_map/ready_3/pallas_call | solution.py:459
  16.6 2.0 %ready.1 = (f32[32,10240]{1,0:T(8,128)S(1)}, f32[32,6144]{1,0:T(8,128)S(1)}) custom-call(s32[1]{0:T(128)} %bitcast.device_ref, s32[18]{0:T(128)S(1)} %copy-done.2, f32[32,16384]{1,0:T(8,128)S(1)} %copy-done, f32[32,16384]{1,0:T(8,128)} %collective-permute-done.1.swap_ref), custom_call_target="tpu_custom_call" | custom-call | flops 3145728 | bytes 6291456 | tf_op jit(solution)/shard_map/ready/pallas_call | solution.py:449
  18.5 3.2 %collective-permute-done.arrived_ref.first_ref = f32[32,10240]{1,0:T(8,128)S(1)} collective-permute-done((f32[32,10240]{1,0:T(8,128)}, f32[32,10240]{1,0:T(8,128)S(1)}, u32[]{:S(2)}, u32[]{:S(2)}) %collective-permute-start) | collective-permute-done | bytes 1310752 | tf_op jit(solution)/shard_map/ppermute | solution.py:420
  22.4 2.1 %collective-permute-start.4 = (f32[32,10240]{1,0:T(8,128)S(1)}, f32[32,10240]{1,0:T(8,128)S(1)}, u32[]{:S(2)}, u32[]{:S(2)}) collective-permute-start(f32[32,10240]{1,0:T(8,128)S(1)} %sent_on_0.1), channel_id=1, source_target_pairs={{0,1},{1,4},{2,5},{3,7},{4,0},{5,2},{6,3},{7,6},{8,9},{9,12},{10,1... | collective-permute-start | bytes 3932168 | tf_op jit(solution)/shard_map/ppermute | solution.py:420
  24.4 1.5 %sent_3_0.1 = f32[32,10240]{1,0:T(8,128)S(1)} custom-call(s32[18]{0:T(128)S(1)} %copy-done.2, f32[32,10240]{1,0:T(8,128)S(1)} %get-tuple-element.37.ready_ref, f32[32,10240]{1,0:T(8,128)} %collective-permute-done.5.refs_0_.arrived_ref), custom_call_target="tpu_custom_call" | custom-call | tf_op jit(solution)/shard_map/sent_3_0/pallas_call | solution.py:494
  25.9 3.5 %collective-permute-start.6 = (f32[32,10240]{1,0:T(8,128)S(1)}, f32[32,10240]{1,0:T(8,128)S(1)}, u32[]{:S(2)}, u32[]{:S(2)}) collective-permute-start(f32[32,10240]{1,0:T(8,128)S(1)} %sent_3_0.1), channel_id=1, source_target_pairs={{0,8},{1,9},{2,10},{3,11},{4,16},{5,17},{6,18},{7,19},{24,12},{25,... | collective-permute-start | bytes 3932168 | tf_op jit(solution)/shard_map/ppermute | solution.py:420
  30.2 1.2 %sent_on_20.1 = f32[32,6144]{1,0:T(8,128)S(1)} custom-call(s32[1]{0:T(128)} %bitcast.device_ref, s32[18]{0:T(128)S(1)} %copy-done.2, f32[32,6144]{1,0:T(8,128)S(1)} %get-tuple-element.30.ready_ref, f32[32,6144]{1,0:T(8,128)} %collective-permute-done.2.arrived_ref.first_ref), custom_call_target="tpu_custom_call" | custom-call | tf_op jit(solution)/shard_map/sent_on_20/pallas_call | solution.py:480
  31.4 2.1 %collective-permute-start.3 = (f32[32,6144]{1,0:T(8,128)S(1)}, f32[32,6144]{1,0:T(8,128)S(1)}, u32[]{:S(2)}, u32[]{:S(2)}) collective-permute-start(f32[32,6144]{1,0:T(8,128)S(1)} %sent_on_20.1), channel_id=1, source_target_pairs={{0,1},{1,4},{2,5},{3,7},{4,0},{5,2},{6,3},{7,6},{8,9},{9,12},{10,1... | collective-permute-start | bytes 2359304 | tf_op jit(solution)/shard_map/ppermute | solution.py:420
  33.5 1.2 %sent_3_20.1 = f32[32,6144]{1,0:T(8,128)S(1)} custom-call(s32[18]{0:T(128)S(1)} %copy-done.2, f32[32,6144]{1,0:T(8,128)S(1)} %get-tuple-element.43.ready_ref, f32[32,6144]{1,0:T(8,128)} %collective-permute-done.7.refs_0_.arrived_ref), custom_call_target="tpu_custom_call" | custom-call | tf_op jit(solution)/shard_map/sent_3_20/pallas_call | solution.py:494
  34.8 3.4 %collective-permute-start.8 = (f32[32,6144]{1,0:T(8,128)S(1)}, f32[32,6144]{1,0:T(8,128)S(1)}, u32[]{:S(2)}, u32[]{:S(2)}) collective-permute-start(f32[32,6144]{1,0:T(8,128)S(1)} %sent_3_20.1), channel_id=1, source_target_pairs={{0,8},{1,9},{2,10},{3,11},{4,16},{5,17},{6,18},{7,19},{24,12},{25,... | collective-permute-start | bytes 2359304 | tf_op jit(solution)/shard_map/ppermute | solution.py:420
  38.2 1.5 %gather_first_20.1.one_ref = f32[32,6144]{1,0:T(8,128)S(1)} custom-call(s32[1]{0:T(128)} %bitcast.device_ref, s32[18]{0:T(128)S(1)} %copy-done.2, f32[32,16384]{1,0:T(8,128)S(1)} %local_bonds.1.local_ref, f32[32,6144]{1,0:T(8,128)} %collective-permute-done.2.arrived_ref.first_ref, f32[32,6144]{1,0:T(8,128)} %collective-permute-done.7.refs_0_.arrived_ref), custom_call_target="tpu_custom_call" | custom-call | tf_op jit(solution)/shard_map/gather_first_20/pallas_call | solution.py:510
  39.8 1.6 %gather_first_0.1.one_ref = f32[32,10240]{1,0:T(8,128)S(1)} custom-call(s32[1]{0:T(128)} %bitcast.device_ref, s32[18]{0:T(128)S(1)} %copy-done.2, f32[32,16384]{1,0:T(8,128)S(1)} %local_bonds.1.local_ref, f32[32,10240]{1,0:T(8,128)S(1)} %collective-permute-done.arrived_ref.first_ref, f32[32,10240]{1,0:T(8,128)} %collective-permute-done.5.refs_0_.arrived_ref), custom_call_target="tpu_custom_call" | custom-call | tf_op jit(solution)/shard_map/gather_first_0/pallas_call | solution.py:510
  41.4 1.9 %collective-permute-done.4.two_ref = f32[32,10240]{1,0:T(8,128)S(1)} collective-permute-done((f32[32,10240]{1,0:T(8,128)S(1)}, f32[32,10240]{1,0:T(8,128)S(1)}, u32[]{:S(2)}, u32[]{:S(2)}) %collective-permute-start.4) | collective-permute-done | bytes 1310752 | tf_op jit(solution)/shard_map/ppermute | solution.py:420
  45.1 6.5 %collective-permute-done.3.two_ref = f32[32,6144]{1,0:T(8,128)S(1)} collective-permute-done((f32[32,6144]{1,0:T(8,128)S(1)}, f32[32,6144]{1,0:T(8,128)S(1)}, u32[]{:S(2)}, u32[]{:S(2)}) %collective-permute-start.3) | collective-permute-done | bytes 786464 | tf_op jit(solution)/shard_map/ppermute | solution.py:420
  51.7 1.1 %collective-permute-done.8.refs_0_ = f32[32,6144]{1,0:T(8,128)S(1)} collective-permute-done((f32[32,6144]{1,0:T(8,128)S(1)}, f32[32,6144]{1,0:T(8,128)S(1)}, u32[]{:S(2)}, u32[]{:S(2)}) %collective-permute-start.8) | collective-permute-done | bytes 786464 | tf_op jit(solution)/shard_map/ppermute | solution.py:420
  53.6 1.2 %collective-permute-done.9 = f32[8,128]{1,0:T(8,128)S(1)} collective-permute-done((f32[8,128]{1,0:T(8,128)S(1)}, f32[8,128]{1,0:T(8,128)S(1)}, u32[]{:S(2)}, u32[]{:S(2)}) %collective-permute-start.9) | collective-permute-done | bytes 4128 | tf_op jit(solution)/shard_map/ppermute | solution.py:420
  54.8 2.3 %collective-permute-start.10 = (f32[8,128]{1,0:T(8,128)S(1)}, f32[8,128]{1,0:T(8,128)S(1)}, u32[]{:S(2)}, u32[]{:S(2)}) collective-permute-start(f32[8,128]{1,0:T(8,128)S(1)} %add.22), channel_id=1, source_target_pairs={{0,12},{1,13},{2,14},{3,15},{4,8},{5,9},{6,10},{7,11},{8,4},{9,5},... | collective-permute-start | bytes 12296 | tf_op jit(solution)/shard_map/ppermute | solution.py:420
  57.3 1.2 %collective-permute-start.12 = (f32[8,128]{1,0:T(8,128)S(1)}, f32[8,128]{1,0:T(8,128)S(1)}, u32[]{:S(2)}, u32[]{:S(2)}) collective-permute-start(f32[8,128]{1,0:T(8,128)S(1)} %add.22), channel_id=1, source_target_pairs={{0,28},{1,29},{2,30},{3,31},{4,24},{5,25},{6,26},{7,27},{8,20},{9,... | collective-permute-start | bytes 12296 | tf_op jit(solution)/shard_map/ppermute | solution.py:420
  58.4 1.6 %collective-permute-done.11 = f32[8,128]{1,0:T(8,128)S(1)} collective-permute-done((f32[8,128]{1,0:T(8,128)S(1)}, f32[8,128]{1,0:T(8,128)S(1)}, u32[]{:S(2)}, u32[]{:S(2)}) %collective-permute-start.11) | collective-permute-done | bytes 4128 | tf_op jit(solution)/shard_map/ppermute | solution.py:420
  60.1 1.1 %collective-permute-done.12 = f32[8,128]{1,0:T(8,128)S(1)} collective-permute-done((f32[8,128]{1,0:T(8,128)S(1)}, f32[8,128]{1,0:T(8,128)S(1)}, u32[]{:S(2)}, u32[]{:S(2)}) %collective-permute-start.12) | collective-permute-done | bytes 4128 | tf_op jit(solution)/shard_map/ppermute | solution.py:420
  61.2 1.5 %collective-permute-start.13 = (f32[8,128]{1,0:T(8,128)S(1)}, f32[8,128]{1,0:T(8,128)S(1)}, u32[]{:S(2)}, u32[]{:S(2)}) collective-permute-start(f32[8,128]{1,0:T(8,128)S(1)} %add_add_fusion), channel_id=1, source_target_pairs={{0,5},{1,4},{2,7},{3,6},{4,1},{5,0},{6,3},{7,2},{8,13},{9,12},{10,... | collective-permute-start | bytes 12296 | tf_op jit(solution)/shard_map/ppermute | solution.py:420
  62.7 1.5 %collective-permute-done.13 = f32[8,128]{1,0:T(8,128)S(1)} collective-permute-done((f32[8,128]{1,0:T(8,128)S(1)}, f32[8,128]{1,0:T(8,128)S(1)}, u32[]{:S(2)}, u32[]{:S(2)}) %collective-permute-start.13) | collective-permute-done | bytes 4128 | tf_op jit(solution)/shard_map/ppermute | solution.py:420
  64.2 2.5 %collective-permute-start.14 = (f32[8,128]{1,0:T(8,128)S(1)}, f32[8,128]{1,0:T(8,128)S(1)}, u32[]{:S(2)}, u32[]{:S(2)}) collective-permute-start(f32[8,128]{1,0:T(8,128)S(1)} %add.26), channel_id=1, source_target_pairs={{0,6},{1,7},{2,4},{3,5},{4,2},{5,3},{6,0},{7,1},{8,14},{9,15},{10,... | collective-permute-start | bytes 12296 | tf_op jit(solution)/shard_map/ppermute | solution.py:420
  66.8 1.4 %collective-permute-done.14 = f32[8,128]{1,0:T(8,128)S(1)} collective-permute-done((f32[8,128]{1,0:T(8,128)S(1)}, f32[8,128]{1,0:T(8,128)S(1)}, u32[]{:S(2)}, u32[]{:S(2)}) %collective-permute-start.14) | collective-permute-done | bytes 4128 | tf_op jit(solution)/shard_map/ppermute | solution.py:420
  68.2 3.0 %factor_apply.1 = (f32[32,16384]{1,0:T(8,128)}, f32[32,32]{1,0:T(8,128)}) custom-call(f32[8,128]{1,0:T(8,128)S(1)} %add.27.gram_ref, f32[32,10240]{1,0:T(8,128)S(1)} %get-tuple-element.46.refs_0_, f32[32,6144]{1,0:T(8,128)S(1)} %get-tuple-element.47.refs_1_), custom_call_target="tpu_custom_call" | custom-call | flops 201326592 | bytes 4194304 | tf_op jit(solution)/shard_map/factor_apply/pallas_call | solution.py:567
  (27 shorter events, 5.1 us)
Async XLA Ops:
  0.6 14.2 %collective-permute-start.1 = (f32[32,16384]{1,0:T(8,128)}, f32[32,16384]{1,0:T(8,128)}, u32[]{:S(2)}, u32[]{:S(2)}) collective-permute-start(f32[32,16384]{1,0:T(8,128)} %own_ref), channel_id=1, source_target_pairs={{0,4},{1,5},{2,6},{3,7},{4,0},{5,1},{6,2},{7,3},{8,12},{9,13},{10,... | collective-permute-start | bytes 6291464 | tf_op jit(solution)/shard_map/ppermute | solution.py:420
  3.2 7.4 %copy-start = (f32[32,16384]{1,0:T(8,128)S(1)}, f32[32,16384]{1,0:T(8,128)}, u32[]{:S(2)}) copy-start(f32[32,16384]{1,0:T(8,128)} %own_ref) | copy-start | bytes 6291460
  3.3 7.4 %copy-start.2 = (s32[18]{0:T(128)S(1)}, s32[18]{0:T(128)}, u32[]{:S(2)}) copy-start(s32[18]{0:T(128)} %bond_ref.17) | copy-start | bytes 220
  3.3 7.4 %copy-start.3 = (s32[19]{0:T(128)S(1)}, s32[19]{0:T(128)}, u32[]{:S(2)}) copy-start(s32[19]{0:T(128)} %field_ref.1) | copy-start | bytes 232
  3.3 18.4 %collective-permute-start = (f32[32,10240]{1,0:T(8,128)}, f32[32,10240]{1,0:T(8,128)S(1)}, u32[]{:S(2)}, u32[]{:S(2)}) collective-permute-start(f32[32,10240]{1,0:T(8,128)} %cut_0.1), channel_id=1, source_target_pairs={{0,4},{1,0},{2,1},{3,2},{4,5},{5,6},{6,7},{7,3},{8,12},{9,8},{10,9... | collective-permute-start | bytes 3932168 | tf_op jit(solution)/shard_map/ppermute | solution.py:420
  3.4 21.1 %collective-permute-start.5 = (f32[32,10240]{1,0:T(8,128)}, f32[32,10240]{1,0:T(8,128)}, u32[]{:S(2)}, u32[]{:S(2)}) collective-permute-start(f32[32,10240]{1,0:T(8,128)} %cut_0.1), channel_id=1, source_target_pairs={{8,4},{9,5},{10,6},{11,7},{12,28},{13,29},{14,30},{15,31},{16,0},{... | collective-permute-start | bytes 3932168 | tf_op jit(solution)/shard_map/ppermute | solution.py:420
  6.7 23.5 %collective-permute-start.2 = (f32[32,6144]{1,0:T(8,128)}, f32[32,6144]{1,0:T(8,128)}, u32[]{:S(2)}, u32[]{:S(2)}) collective-permute-start(f32[32,6144]{1,0:T(8,128)} %cut_10240.1), channel_id=1, source_target_pairs={{0,4},{1,0},{2,1},{3,2},{4,5},{5,6},{6,7},{7,3},{8,12},{9,8},{10,9... | collective-permute-start | bytes 2359304 | tf_op jit(solution)/shard_map/ppermute | solution.py:420
  9.4 24.1 %collective-permute-start.7 = (f32[32,6144]{1,0:T(8,128)}, f32[32,6144]{1,0:T(8,128)}, u32[]{:S(2)}, u32[]{:S(2)}) collective-permute-start(f32[32,6144]{1,0:T(8,128)} %cut_10240.1), channel_id=1, source_target_pairs={{8,4},{9,5},{10,6},{11,7},{12,28},{13,29},{14,30},{15,31},{16,0},{... | collective-permute-start | bytes 2359304 | tf_op jit(solution)/shard_map/ppermute | solution.py:420
  10.7 1.6 %copy-start.1 = (f32[32,16384]{1,0:T(8,128)S(1)}, f32[32,16384]{1,0:T(8,128)}, u32[]{:S(2)}) copy-start(f32[32,16384]{1,0:T(8,128)} %prev_ref.1) | copy-start | bytes 6291460
  22.4 20.9 %collective-permute-start.4 = (f32[32,10240]{1,0:T(8,128)S(1)}, f32[32,10240]{1,0:T(8,128)S(1)}, u32[]{:S(2)}, u32[]{:S(2)}) collective-permute-start(f32[32,10240]{1,0:T(8,128)S(1)} %sent_on_0.1), channel_id=1, source_target_pairs={{0,1},{1,4},{2,5},{3,7},{4,0},{5,2},{6,3},{7,6},{8,9},{9,12},{10,1... | collective-permute-start | bytes 3932168 | tf_op jit(solution)/shard_map/ppermute | solution.py:420
  25.9 18.5 %collective-permute-start.6 = (f32[32,10240]{1,0:T(8,128)S(1)}, f32[32,10240]{1,0:T(8,128)S(1)}, u32[]{:S(2)}, u32[]{:S(2)}) collective-permute-start(f32[32,10240]{1,0:T(8,128)S(1)} %sent_3_0.1), channel_id=1, source_target_pairs={{0,8},{1,9},{2,10},{3,11},{4,16},{5,17},{6,18},{7,19},{24,12},{25,... | collective-permute-start | bytes 3932168 | tf_op jit(solution)/shard_map/ppermute | solution.py:420
  31.4 20.2 %collective-permute-start.3 = (f32[32,6144]{1,0:T(8,128)S(1)}, f32[32,6144]{1,0:T(8,128)S(1)}, u32[]{:S(2)}, u32[]{:S(2)}) collective-permute-start(f32[32,6144]{1,0:T(8,128)S(1)} %sent_on_20.1), channel_id=1, source_target_pairs={{0,1},{1,4},{2,5},{3,7},{4,0},{5,2},{6,3},{7,6},{8,9},{9,12},{10,1... | collective-permute-start | bytes 2359304 | tf_op jit(solution)/shard_map/ppermute | solution.py:420
  34.8 18.1 %collective-permute-start.8 = (f32[32,6144]{1,0:T(8,128)S(1)}, f32[32,6144]{1,0:T(8,128)S(1)}, u32[]{:S(2)}, u32[]{:S(2)}) collective-permute-start(f32[32,6144]{1,0:T(8,128)S(1)} %sent_3_20.1), channel_id=1, source_target_pairs={{0,8},{1,9},{2,10},{3,11},{4,16},{5,17},{6,18},{7,19},{24,12},{25,... | collective-permute-start | bytes 2359304 | tf_op jit(solution)/shard_map/ppermute | solution.py:420
  53.6 1.2 %collective-permute-start.9 = (f32[8,128]{1,0:T(8,128)S(1)}, f32[8,128]{1,0:T(8,128)S(1)}, u32[]{:S(2)}, u32[]{:S(2)}) collective-permute-start(f32[8,128]{1,0:T(8,128)S(1)} %get-tuple-element.45), channel_id=1, source_target_pairs={{0,4},{1,5},{2,6},{3,7},{4,0},{5,1},{6,2},{7,3},{8,12},{9,13},{10,... | collective-permute-start | bytes 12296 | tf_op jit(solution)/shard_map/ppermute | solution.py:420
  54.8 3.7 %collective-permute-start.10 = (f32[8,128]{1,0:T(8,128)S(1)}, f32[8,128]{1,0:T(8,128)S(1)}, u32[]{:S(2)}, u32[]{:S(2)}) collective-permute-start(f32[8,128]{1,0:T(8,128)S(1)} %add.22), channel_id=1, source_target_pairs={{0,12},{1,13},{2,14},{3,15},{4,8},{5,9},{6,10},{7,11},{8,4},{9,5},... | collective-permute-start | bytes 12296 | tf_op jit(solution)/shard_map/ppermute | solution.py:420
  57.0 3.0 %collective-permute-start.11 = (f32[8,128]{1,0:T(8,128)S(1)}, f32[8,128]{1,0:T(8,128)S(1)}, u32[]{:S(2)}, u32[]{:S(2)}) collective-permute-start(f32[8,128]{1,0:T(8,128)S(1)} %add.22), channel_id=1, source_target_pairs={{0,20},{1,21},{2,22},{3,23},{4,16},{5,17},{6,18},{7,19},{8,28},{9,... | collective-permute-start | bytes 12296 | tf_op jit(solution)/shard_map/ppermute | solution.py:420
  57.3 3.9 %collective-permute-start.12 = (f32[8,128]{1,0:T(8,128)S(1)}, f32[8,128]{1,0:T(8,128)S(1)}, u32[]{:S(2)}, u32[]{:S(2)}) collective-permute-start(f32[8,128]{1,0:T(8,128)S(1)} %add.22), channel_id=1, source_target_pairs={{0,28},{1,29},{2,30},{3,31},{4,24},{5,25},{6,26},{7,27},{8,20},{9,... | collective-permute-start | bytes 12296 | tf_op jit(solution)/shard_map/ppermute | solution.py:420
  61.2 3.0 %collective-permute-start.13 = (f32[8,128]{1,0:T(8,128)S(1)}, f32[8,128]{1,0:T(8,128)S(1)}, u32[]{:S(2)}, u32[]{:S(2)}) collective-permute-start(f32[8,128]{1,0:T(8,128)S(1)} %add_add_fusion), channel_id=1, source_target_pairs={{0,5},{1,4},{2,7},{3,6},{4,1},{5,0},{6,3},{7,2},{8,13},{9,12},{10,... | collective-permute-start | bytes 12296 | tf_op jit(solution)/shard_map/ppermute | solution.py:420
  64.2 3.9 %collective-permute-start.14 = (f32[8,128]{1,0:T(8,128)S(1)}, f32[8,128]{1,0:T(8,128)S(1)}, u32[]{:S(2)}, u32[]{:S(2)}) collective-permute-start(f32[8,128]{1,0:T(8,128)S(1)} %add.26), channel_id=1, source_target_pairs={{0,6},{1,7},{2,4},{3,5},{4,2},{5,3},{6,0},{7,1},{8,14},{9,15},{10,... | collective-permute-start | bytes 12296 | tf_op jit(solution)/shard_map/ppermute | solution.py:420

commit v8 on v7

--- a/solution.py
+++ b/solution.py
@@ -488,7 +488,9 @@
         )(place, bond_levels, base, first)
         seconds.append(permute(sent, route(devices, 1, SECOND)))
         sents.append(sent)
-        arrived, sent = lax.optimization_barrier((both, sent))
+        arrived = both
+        if start == 0:
+            arrived, sent = lax.optimization_barrier((both, sent))
         on = []
         for m, values, bases in zip(middles, arrived, later_ready):
             sent = pl.pallas_call(

time: 71.7 us -> 71.7 us (level)
  no operation moved by 1% of the time
where the time goes in v8:
time: 71.7 us; the launch traced here: 71.2 us
  starting transfers between devices  24.7 us (34%)
  Pallas kernels  22.6 us (32%)
  waiting for transfers between devices  21.4 us (30%)
  local copies, waits for them, and re-layouts  1.61 us (2%)
  between operations  0.85 us (1%)
    ppermute x15, starting transfers between devices, permute(): return lax.ppermute(values, AXES, pairs)  24.7 us
    ppermute x15, waiting for transfers between devices, permute(): return lax.ppermute(values, AXES, pairs)  21.4 us
    pallas_call x2, Pallas kernels, cut(): pl.pallas_call(functools.partial(cut_kernel, start=start), out_shape=jax....  4.05 us
    pallas_call x2, Pallas kernels, local(): pl.pallas_call(functools.partial(gather_kernel, start=start * width // LA...  3.14 us
    pallas_call x1, Pallas kernels, local(): pl.pallas_call(finish_kernel, out_shape=(whole, jax.ShapeDtypeStruct((vec...  3 us
    pallas_call x2, Pallas kernels, local(): pl.pallas_call(functools.partial(later_sent_kernel, bond=local_bits + m,...  2.68 us
    pallas_call x1, Pallas kernels, local(): pl.pallas_call(functools.partial(local_kernel, global_bits=global_bits, s...  2.49 us
    pallas_call x1, Pallas kernels, local(): pl.pallas_call(functools.partial(ready_kernel, bit=rest_bits - 1, bond=lo...  1.97 us
  transfers between devices with their start and end apart: 15, of which 11 were waited for; matrix products, arithmetic and copies ran while one was open for 0% of the time, Pallas kernels for 26%

profile of v8, /device:TPU:0, one launch (start us, length us, event | category | flops | bytes accessed | tf_op | source)
XLA Modules:
  0.0 71.2 jit_solution(8479240550459465496)
XLA Ops:
  1.1 2.1 %cut_0.1 = f32[32,10240]{1,0:T(8,128)} custom-call(f32[32,16384]{1,0:T(8,128)} %own_ref), custom_call_target="tpu_custom_call" | custom-call | bytes 2621440 | tf_op jit(solution)/shard_map/cut_0/pallas_call | solution.py:223
  3.4 1.4 %collective-permute-start.5 = (f32[32,10240]{1,0:T(8,128)}, f32[32,10240]{1,0:T(8,128)}, u32[]{:S(2)}, u32[]{:S(2)}) collective-permute-start(f32[32,10240]{1,0:T(8,128)} %cut_0.1), channel_id=1, source_target_pairs={{8,4},{9,5},{10,6},{11,7},{12,28},{13,29},{14,30},{15,31},{16,0},{... | collective-permute-start | bytes 3932168 | tf_op jit(solution)/shard_map/ppermute | solution.py:420
  4.8 2.0 %cut_10240.1 = f32[32,6144]{1,0:T(8,128)} custom-call(f32[32,16384]{1,0:T(8,128)} %own_ref), custom_call_target="tpu_custom_call" | custom-call | bytes 1572864 | tf_op jit(solution)/shard_map/cut_10240/pallas_call | solution.py:223
  6.7 2.6 %collective-permute-start.2 = (f32[32,6144]{1,0:T(8,128)}, f32[32,6144]{1,0:T(8,128)}, u32[]{:S(2)}, u32[]{:S(2)}) collective-permute-start(f32[32,6144]{1,0:T(8,128)} %cut_10240.1), channel_id=1, source_target_pairs={{0,4},{1,0},{2,1},{3,2},{4,5},{5,6},{6,7},{7,3},{8,12},{9,8},{10,9... | collective-permute-start | bytes 2359304 | tf_op jit(solution)/shard_map/ppermute | solution.py:420
  9.4 1.3 %collective-permute-start.7 = (f32[32,6144]{1,0:T(8,128)}, f32[32,6144]{1,0:T(8,128)}, u32[]{:S(2)}, u32[]{:S(2)}) collective-permute-start(f32[32,6144]{1,0:T(8,128)} %cut_10240.1), channel_id=1, source_target_pairs={{8,4},{9,5},{10,6},{11,7},{12,28},{13,29},{14,30},{15,31},{16,0},{... | collective-permute-start | bytes 2359304 | tf_op jit(solution)/shard_map/ppermute | solution.py:420
  10.7 1.6 %copy-done.1 = f32[32,16384]{1,0:T(8,128)S(1)} copy-done((f32[32,16384]{1,0:T(8,128)S(1)}, f32[32,16384]{1,0:T(8,128)}, u32[]{:S(2)}) %copy-start.1) | copy-done | bytes 2097176
  12.3 2.5 %local_bonds.1.local_ref = f32[32,16384]{1,0:T(8,128)S(1)} custom-call(s32[1]{0:T(128)} %bitcast.device_ref, s32[19]{0:T(128)S(1)} %copy-done.3, s32[18]{0:T(128)S(1)} %copy-done.2, f32[32,16384]{1,0:T(8,128)S(1)} %copy-done, f32[32,16384]{1,0:T(8,128)S(1)} %copy-done.1), custom_call_target="tpu_custom_call" | custom-call | flops 805306368 | bytes 6291456 | tf_op jit(solution)/shard_map/local_bonds/pallas_call | solution.py:440
  14.8 1.7 %ready_3.1 = (f32[32,10240]{1,0:T(8,128)S(1)}, f32[32,6144]{1,0:T(8,128)S(1)}) custom-call(s32[1]{0:T(128)} %bitcast.device_ref, s32[18]{0:T(128)S(1)} %copy-done.2, f32[32,16384]{1,0:T(8,128)} %collective-permute-done.1.swap_ref), custom_call_target="tpu_custom_call" | custom-call | flops 524288 | bytes 4194304 | tf_op jit(solution)/shard_map/ready_3/pallas_call | solution.py:459
  16.6 2.0 %ready.1 = (f32[32,10240]{1,0:T(8,128)S(1)}, f32[32,6144]{1,0:T(8,128)S(1)}) custom-call(s32[1]{0:T(128)} %bitcast.device_ref, s32[18]{0:T(128)S(1)} %copy-done.2, f32[32,16384]{1,0:T(8,128)S(1)} %copy-done, f32[32,16384]{1,0:T(8,128)} %collective-permute-done.1.swap_ref), custom_call_target="tpu_custom_call" | custom-call | flops 3145728 | bytes 6291456 | tf_op jit(solution)/shard_map/ready/pallas_call | solution.py:449
  18.5 3.2 %collective-permute-done.arrived_ref.first_ref = f32[32,10240]{1,0:T(8,128)S(1)} collective-permute-done((f32[32,10240]{1,0:T(8,128)}, f32[32,10240]{1,0:T(8,128)S(1)}, u32[]{:S(2)}, u32[]{:S(2)}) %collective-permute-start) | collective-permute-done | bytes 1310752 | tf_op jit(solution)/shard_map/ppermute | solution.py:420
  22.4 2.1 %collective-permute-start.4 = (f32[32,10240]{1,0:T(8,128)S(1)}, f32[32,10240]{1,0:T(8,128)S(1)}, u32[]{:S(2)}, u32[]{:S(2)}) collective-permute-start(f32[32,10240]{1,0:T(8,128)S(1)} %sent_on_0.1), channel_id=1, source_target_pairs={{0,1},{1,4},{2,5},{3,7},{4,0},{5,2},{6,3},{7,6},{8,9},{9,12},{10,1... | collective-permute-start | bytes 3932168 | tf_op jit(solution)/shard_map/ppermute | solution.py:420
  24.4 1.5 %sent_3_0.1 = f32[32,10240]{1,0:T(8,128)S(1)} custom-call(s32[18]{0:T(128)S(1)} %copy-done.2, f32[32,10240]{1,0:T(8,128)S(1)} %get-tuple-element.36.ready_ref, f32[32,10240]{1,0:T(8,128)} %collective-permute-done.5.refs_0_.arrived_ref), custom_call_target="tpu_custom_call" | custom-call | tf_op jit(solution)/shard_map/sent_3_0/pallas_call | solution.py:496
  25.9 3.5 %collective-permute-start.6 = (f32[32,10240]{1,0:T(8,128)S(1)}, f32[32,10240]{1,0:T(8,128)S(1)}, u32[]{:S(2)}, u32[]{:S(2)}) collective-permute-start(f32[32,10240]{1,0:T(8,128)S(1)} %sent_3_0.1), channel_id=1, source_target_pairs={{0,8},{1,9},{2,10},{3,11},{4,16},{5,17},{6,18},{7,19},{24,12},{25,... | collective-permute-start | bytes 3932168 | tf_op jit(solution)/shard_map/ppermute | solution.py:420
  30.2 1.2 %sent_on_20.1 = f32[32,6144]{1,0:T(8,128)S(1)} custom-call(s32[1]{0:T(128)} %bitcast.device_ref, s32[18]{0:T(128)S(1)} %copy-done.2, f32[32,6144]{1,0:T(8,128)S(1)} %get-tuple-element.29.ready_ref, f32[32,6144]{1,0:T(8,128)} %collective-permute-done.2.arrived_ref.first_ref), custom_call_target="tpu_custom_call" | custom-call | tf_op jit(solution)/shard_map/sent_on_20/pallas_call | solution.py:480
  31.4 2.1 %collective-permute-start.3 = (f32[32,6144]{1,0:T(8,128)S(1)}, f32[32,6144]{1,0:T(8,128)S(1)}, u32[]{:S(2)}, u32[]{:S(2)}) collective-permute-start(f32[32,6144]{1,0:T(8,128)S(1)} %sent_on_20.1), channel_id=1, source_target_pairs={{0,1},{1,4},{2,5},{3,7},{4,0},{5,2},{6,3},{7,6},{8,9},{9,12},{10,1... | collective-permute-start | bytes 2359304 | tf_op jit(solution)/shard_map/ppermute | solution.py:420
  33.5 1.2 %sent_3_20.1 = f32[32,6144]{1,0:T(8,128)S(1)} custom-call(s32[18]{0:T(128)S(1)} %copy-done.2, f32[32,6144]{1,0:T(8,128)S(1)} %get-tuple-element.42.ready_ref, f32[32,6144]{1,0:T(8,128)} %collective-permute-done.7.refs_0_.arrived_ref), custom_call_target="tpu_custom_call" | custom-call | tf_op jit(solution)/shard_map/sent_3_20/pallas_call | solution.py:496
  34.8 3.4 %collective-permute-start.8 = (f32[32,6144]{1,0:T(8,128)S(1)}, f32[32,6144]{1,0:T(8,128)S(1)}, u32[]{:S(2)}, u32[]{:S(2)}) collective-permute-start(f32[32,6144]{1,0:T(8,128)S(1)} %sent_3_20.1), channel_id=1, source_target_pairs={{0,8},{1,9},{2,10},{3,11},{4,16},{5,17},{6,18},{7,19},{24,12},{25,... | collective-permute-start | bytes 2359304 | tf_op jit(solution)/shard_map/ppermute | solution.py:420
  38.2 1.5 %gather_first_20.1.one_ref = f32[32,6144]{1,0:T(8,128)S(1)} custom-call(s32[1]{0:T(128)} %bitcast.device_ref, s32[18]{0:T(128)S(1)} %copy-done.2, f32[32,16384]{1,0:T(8,128)S(1)} %local_bonds.1.local_ref, f32[32,6144]{1,0:T(8,128)} %collective-permute-done.2.arrived_ref.first_ref, f32[32,6144]{1,0:T(8,128)} %collective-permute-done.7.refs_0_.arrived_ref), custom_call_target="tpu_custom_call" | custom-call | tf_op jit(solution)/shard_map/gather_first_20/pallas_call | solution.py:512
  39.8 1.6 %gather_first_0.1.one_ref = f32[32,10240]{1,0:T(8,128)S(1)} custom-call(s32[1]{0:T(128)} %bitcast.device_ref, s32[18]{0:T(128)S(1)} %copy-done.2, f32[32,16384]{1,0:T(8,128)S(1)} %local_bonds.1.local_ref, f32[32,10240]{1,0:T(8,128)S(1)} %collective-permute-done.arrived_ref.first_ref, f32[32,10240]{1,0:T(8,128)} %collective-permute-done.5.refs_0_.arrived_ref), custom_call_target="tpu_custom_call" | custom-call | tf_op jit(solution)/shard_map/gather_first_0/pallas_call | solution.py:512
  41.4 1.9 %collective-permute-done.4.two_ref = f32[32,10240]{1,0:T(8,128)S(1)} collective-permute-done((f32[32,10240]{1,0:T(8,128)S(1)}, f32[32,10240]{1,0:T(8,128)S(1)}, u32[]{:S(2)}, u32[]{:S(2)}) %collective-permute-start.4) | collective-permute-done | bytes 1310752 | tf_op jit(solution)/shard_map/ppermute | solution.py:420
  45.1 6.5 %collective-permute-done.3.two_ref = f32[32,6144]{1,0:T(8,128)S(1)} collective-permute-done((f32[32,6144]{1,0:T(8,128)S(1)}, f32[32,6144]{1,0:T(8,128)S(1)}, u32[]{:S(2)}, u32[]{:S(2)}) %collective-permute-start.3) | collective-permute-done | bytes 786464 | tf_op jit(solution)/shard_map/ppermute | solution.py:420
  51.7 1.1 %collective-permute-done.8.refs_0_ = f32[32,6144]{1,0:T(8,128)S(1)} collective-permute-done((f32[32,6144]{1,0:T(8,128)S(1)}, f32[32,6144]{1,0:T(8,128)S(1)}, u32[]{:S(2)}, u32[]{:S(2)}) %collective-permute-start.8) | collective-permute-done | bytes 786464 | tf_op jit(solution)/shard_map/ppermute | solution.py:420
  53.6 1.2 %collective-permute-done.9 = f32[8,128]{1,0:T(8,128)S(1)} collective-permute-done((f32[8,128]{1,0:T(8,128)S(1)}, f32[8,128]{1,0:T(8,128)S(1)}, u32[]{:S(2)}, u32[]{:S(2)}) %collective-permute-start.9) | collective-permute-done | bytes 4128 | tf_op jit(solution)/shard_map/ppermute | solution.py:420
  54.8 2.3 %collective-permute-start.10 = (f32[8,128]{1,0:T(8,128)S(1)}, f32[8,128]{1,0:T(8,128)S(1)}, u32[]{:S(2)}, u32[]{:S(2)}) collective-permute-start(f32[8,128]{1,0:T(8,128)S(1)} %add.22), channel_id=1, source_target_pairs={{0,12},{1,13},{2,14},{3,15},{4,8},{5,9},{6,10},{7,11},{8,4},{9,5},... | collective-permute-start | bytes 12296 | tf_op jit(solution)/shard_map/ppermute | solution.py:420
  57.3 1.2 %collective-permute-start.12 = (f32[8,128]{1,0:T(8,128)S(1)}, f32[8,128]{1,0:T(8,128)S(1)}, u32[]{:S(2)}, u32[]{:S(2)}) collective-permute-start(f32[8,128]{1,0:T(8,128)S(1)} %add.22), channel_id=1, source_target_pairs={{0,28},{1,29},{2,30},{3,31},{4,24},{5,25},{6,26},{7,27},{8,20},{9,... | collective-permute-start | bytes 12296 | tf_op jit(solution)/shard_map/ppermute | solution.py:420
  58.4 1.6 %collective-permute-done.11 = f32[8,128]{1,0:T(8,128)S(1)} collective-permute-done((f32[8,128]{1,0:T(8,128)S(1)}, f32[8,128]{1,0:T(8,128)S(1)}, u32[]{:S(2)}, u32[]{:S(2)}) %collective-permute-start.11) | collective-permute-done | bytes 4128 | tf_op jit(solution)/shard_map/ppermute | solution.py:420
  60.1 1.1 %collective-permute-done.12 = f32[8,128]{1,0:T(8,128)S(1)} collective-permute-done((f32[8,128]{1,0:T(8,128)S(1)}, f32[8,128]{1,0:T(8,128)S(1)}, u32[]{:S(2)}, u32[]{:S(2)}) %collective-permute-start.12) | collective-permute-done | bytes 4128 | tf_op jit(solution)/shard_map/ppermute | solution.py:420
  61.2 1.5 %collective-permute-start.13 = (f32[8,128]{1,0:T(8,128)S(1)}, f32[8,128]{1,0:T(8,128)S(1)}, u32[]{:S(2)}, u32[]{:S(2)}) collective-permute-start(f32[8,128]{1,0:T(8,128)S(1)} %add_add_fusion), channel_id=1, source_target_pairs={{0,5},{1,4},{2,7},{3,6},{4,1},{5,0},{6,3},{7,2},{8,13},{9,12},{10,... | collective-permute-start | bytes 12296 | tf_op jit(solution)/shard_map/ppermute | solution.py:420
  62.7 1.5 %collective-permute-done.13 = f32[8,128]{1,0:T(8,128)S(1)} collective-permute-done((f32[8,128]{1,0:T(8,128)S(1)}, f32[8,128]{1,0:T(8,128)S(1)}, u32[]{:S(2)}, u32[]{:S(2)}) %collective-permute-start.13) | collective-permute-done | bytes 4128 | tf_op jit(solution)/shard_map/ppermute | solution.py:420
  64.2 2.5 %collective-permute-start.14 = (f32[8,128]{1,0:T(8,128)S(1)}, f32[8,128]{1,0:T(8,128)S(1)}, u32[]{:S(2)}, u32[]{:S(2)}) collective-permute-start(f32[8,128]{1,0:T(8,128)S(1)} %add.26), channel_id=1, source_target_pairs={{0,6},{1,7},{2,4},{3,5},{4,2},{5,3},{6,0},{7,1},{8,14},{9,15},{10,... | collective-permute-start | bytes 12296 | tf_op jit(solution)/shard_map/ppermute | solution.py:420
  66.8 1.4 %collective-permute-done.14 = f32[8,128]{1,0:T(8,128)S(1)} collective-permute-done((f32[8,128]{1,0:T(8,128)S(1)}, f32[8,128]{1,0:T(8,128)S(1)}, u32[]{:S(2)}, u32[]{:S(2)}) %collective-permute-start.14) | collective-permute-done | bytes 4128 | tf_op jit(solution)/shard_map/ppermute | solution.py:420
  68.2 3.0 %factor_apply.1 = (f32[32,16384]{1,0:T(8,128)}, f32[32,32]{1,0:T(8,128)}) custom-call(f32[8,128]{1,0:T(8,128)S(1)} %add.27.gram_ref, f32[32,10240]{1,0:T(8,128)S(1)} %get-tuple-element.44.refs_0_, f32[32,6144]{1,0:T(8,128)S(1)} %get-tuple-element.45.refs_1_), custom_call_target="tpu_custom_call" | custom-call | flops 201326592 | bytes 4194304 | tf_op jit(solution)/shard_map/factor_apply/pallas_call | solution.py:569
  (27 shorter events, 5.1 us)
Async XLA Ops:
  0.6 14.2 %collective-permute-start.1 = (f32[32,16384]{1,0:T(8,128)}, f32[32,16384]{1,0:T(8,128)}, u32[]{:S(2)}, u32[]{:S(2)}) collective-permute-start(f32[32,16384]{1,0:T(8,128)} %own_ref), channel_id=1, source_target_pairs={{0,4},{1,5},{2,6},{3,7},{4,0},{5,1},{6,2},{7,3},{8,12},{9,13},{10,... | collective-permute-start | bytes 6291464 | tf_op jit(solution)/shard_map/ppermute | solution.py:420
  3.2 7.4 %copy-start = (f32[32,16384]{1,0:T(8,128)S(1)}, f32[32,16384]{1,0:T(8,128)}, u32[]{:S(2)}) copy-start(f32[32,16384]{1,0:T(8,128)} %own_ref) | copy-start | bytes 6291460
  3.3 7.4 %copy-start.2 = (s32[18]{0:T(128)S(1)}, s32[18]{0:T(128)}, u32[]{:S(2)}) copy-start(s32[18]{0:T(128)} %bond_ref.17) | copy-start | bytes 220
  3.3 7.4 %copy-start.3 = (s32[19]{0:T(128)S(1)}, s32[19]{0:T(128)}, u32[]{:S(2)}) copy-start(s32[19]{0:T(128)} %field_ref.1) | copy-start | bytes 232
  3.3 18.4 %collective-permute-start = (f32[32,10240]{1,0:T(8,128)}, f32[32,10240]{1,0:T(8,128)S(1)}, u32[]{:S(2)}, u32[]{:S(2)}) collective-permute-start(f32[32,10240]{1,0:T(8,128)} %cut_0.1), channel_id=1, source_target_pairs={{0,4},{1,0},{2,1},{3,2},{4,5},{5,6},{6,7},{7,3},{8,12},{9,8},{10,9... | collective-permute-start | bytes 3932168 | tf_op jit(solution)/shard_map/ppermute | solution.py:420
  3.4 21.1 %collective-permute-start.5 = (f32[32,10240]{1,0:T(8,128)}, f32[32,10240]{1,0:T(8,128)}, u32[]{:S(2)}, u32[]{:S(2)}) collective-permute-start(f32[32,10240]{1,0:T(8,128)} %cut_0.1), channel_id=1, source_target_pairs={{8,4},{9,5},{10,6},{11,7},{12,28},{13,29},{14,30},{15,31},{16,0},{... | collective-permute-start | bytes 3932168 | tf_op jit(solution)/shard_map/ppermute | solution.py:420
  6.7 23.5 %collective-permute-start.2 = (f32[32,6144]{1,0:T(8,128)}, f32[32,6144]{1,0:T(8,128)}, u32[]{:S(2)}, u32[]{:S(2)}) collective-permute-start(f32[32,6144]{1,0:T(8,128)} %cut_10240.1), channel_id=1, source_target_pairs={{0,4},{1,0},{2,1},{3,2},{4,5},{5,6},{6,7},{7,3},{8,12},{9,8},{10,9... | collective-permute-start | bytes 2359304 | tf_op jit(solution)/shard_map/ppermute | solution.py:420
  9.4 24.1 %collective-permute-start.7 = (f32[32,6144]{1,0:T(8,128)}, f32[32,6144]{1,0:T(8,128)}, u32[]{:S(2)}, u32[]{:S(2)}) collective-permute-start(f32[32,6144]{1,0:T(8,128)} %cut_10240.1), channel_id=1, source_target_pairs={{8,4},{9,5},{10,6},{11,7},{12,28},{13,29},{14,30},{15,31},{16,0},{... | collective-permute-start | bytes 2359304 | tf_op jit(solution)/shard_map/ppermute | solution.py:420
  10.7 1.6 %copy-start.1 = (f32[32,16384]{1,0:T(8,128)S(1)}, f32[32,16384]{1,0:T(8,128)}, u32[]{:S(2)}) copy-start(f32[32,16384]{1,0:T(8,128)} %prev_ref.1) | copy-start | bytes 6291460
  22.4 20.9 %collective-permute-start.4 = (f32[32,10240]{1,0:T(8,128)S(1)}, f32[32,10240]{1,0:T(8,128)S(1)}, u32[]{:S(2)}, u32[]{:S(2)}) collective-permute-start(f32[32,10240]{1,0:T(8,128)S(1)} %sent_on_0.1), channel_id=1, source_target_pairs={{0,1},{1,4},{2,5},{3,7},{4,0},{5,2},{6,3},{7,6},{8,9},{9,12},{10,1... | collective-permute-start | bytes 3932168 | tf_op jit(solution)/shard_map/ppermute | solution.py:420
  25.9 18.5 %collective-permute-start.6 = (f32[32,10240]{1,0:T(8,128)S(1)}, f32[32,10240]{1,0:T(8,128)S(1)}, u32[]{:S(2)}, u32[]{:S(2)}) collective-permute-start(f32[32,10240]{1,0:T(8,128)S(1)} %sent_3_0.1), channel_id=1, source_target_pairs={{0,8},{1,9},{2,10},{3,11},{4,16},{5,17},{6,18},{7,19},{24,12},{25,... | collective-permute-start | bytes 3932168 | tf_op jit(solution)/shard_map/ppermute | solution.py:420
  31.4 20.2 %collective-permute-start.3 = (f32[32,6144]{1,0:T(8,128)S(1)}, f32[32,6144]{1,0:T(8,128)S(1)}, u32[]{:S(2)}, u32[]{:S(2)}) collective-permute-start(f32[32,6144]{1,0:T(8,128)S(1)} %sent_on_20.1), channel_id=1, source_target_pairs={{0,1},{1,4},{2,5},{3,7},{4,0},{5,2},{6,3},{7,6},{8,9},{9,12},{10,1... | collective-permute-start | bytes 2359304 | tf_op jit(solution)/shard_map/ppermute | solution.py:420
  34.8 18.1 %collective-permute-start.8 = (f32[32,6144]{1,0:T(8,128)S(1)}, f32[32,6144]{1,0:T(8,128)S(1)}, u32[]{:S(2)}, u32[]{:S(2)}) collective-permute-start(f32[32,6144]{1,0:T(8,128)S(1)} %sent_3_20.1), channel_id=1, source_target_pairs={{0,8},{1,9},{2,10},{3,11},{4,16},{5,17},{6,18},{7,19},{24,12},{25,... | collective-permute-start | bytes 2359304 | tf_op jit(solution)/shard_map/ppermute | solution.py:420
  53.6 1.2 %collective-permute-start.9 = (f32[8,128]{1,0:T(8,128)S(1)}, f32[8,128]{1,0:T(8,128)S(1)}, u32[]{:S(2)}, u32[]{:S(2)}) collective-permute-start(f32[8,128]{1,0:T(8,128)S(1)} %get-tuple-element.43), channel_id=1, source_target_pairs={{0,4},{1,5},{2,6},{3,7},{4,0},{5,1},{6,2},{7,3},{8,12},{9,13},{10,... | collective-permute-start | bytes 12296 | tf_op jit(solution)/shard_map/ppermute | solution.py:420
  54.8 3.7 %collective-permute-start.10 = (f32[8,128]{1,0:T(8,128)S(1)}, f32[8,128]{1,0:T(8,128)S(1)}, u32[]{:S(2)}, u32[]{:S(2)}) collective-permute-start(f32[8,128]{1,0:T(8,128)S(1)} %add.22), channel_id=1, source_target_pairs={{0,12},{1,13},{2,14},{3,15},{4,8},{5,9},{6,10},{7,11},{8,4},{9,5},... | collective-permute-start | bytes 12296 | tf_op jit(solution)/shard_map/ppermute | solution.py:420
  57.0 3.0 %collective-permute-start.11 = (f32[8,128]{1,0:T(8,128)S(1)}, f32[8,128]{1,0:T(8,128)S(1)}, u32[]{:S(2)}, u32[]{:S(2)}) collective-permute-start(f32[8,128]{1,0:T(8,128)S(1)} %add.22), channel_id=1, source_target_pairs={{0,20},{1,21},{2,22},{3,23},{4,16},{5,17},{6,18},{7,19},{8,28},{9,... | collective-permute-start | bytes 12296 | tf_op jit(solution)/shard_map/ppermute | solution.py:420
  57.3 3.9 %collective-permute-start.12 = (f32[8,128]{1,0:T(8,128)S(1)}, f32[8,128]{1,0:T(8,128)S(1)}, u32[]{:S(2)}, u32[]{:S(2)}) collective-permute-start(f32[8,128]{1,0:T(8,128)S(1)} %add.22), channel_id=1, source_target_pairs={{0,28},{1,29},{2,30},{3,31},{4,24},{5,25},{6,26},{7,27},{8,20},{9,... | collective-permute-start | bytes 12296 | tf_op jit(solution)/shard_map/ppermute | solution.py:420
  61.2 3.0 %collective-permute-start.13 = (f32[8,128]{1,0:T(8,128)S(1)}, f32[8,128]{1,0:T(8,128)S(1)}, u32[]{:S(2)}, u32[]{:S(2)}) collective-permute-start(f32[8,128]{1,0:T(8,128)S(1)} %add_add_fusion), channel_id=1, source_target_pairs={{0,5},{1,4},{2,7},{3,6},{4,1},{5,0},{6,3},{7,2},{8,13},{9,12},{10,... | collective-permute-start | bytes 12296 | tf_op jit(solution)/shard_map/ppermute | solution.py:420
  64.2 3.9 %collective-permute-start.14 = (f32[8,128]{1,0:T(8,128)S(1)}, f32[8,128]{1,0:T(8,128)S(1)}, u32[]{:S(2)}, u32[]{:S(2)}) collective-permute-start(f32[8,128]{1,0:T(8,128)S(1)} %add.26), channel_id=1, source_target_pairs={{0,6},{1,7},{2,4},{3,5},{4,2},{5,3},{6,0},{7,1},{8,14},{9,15},{10,... | collective-permute-start | bytes 12296 | tf_op jit(solution)/shard_map/ppermute | solution.py:420
